TPU v7x, 32 devices: a whole 2x2x4 slice. The times are simulated.
32 devices in a mesh: dp: 4 (over y, core), seq: 8 (over z, x).
Axes of the slice: x: 2, y: 2, z: 4, core: 2. Of those that a mesh axis runs over, the one named last changes fastest.
Arguments:
- tokens: bfloat16 [4, 1024, 2048], P('dp', 'seq'), may hold values from -6 to 6
- cotangent: bfloat16 [4, 1024, 2048], P('dp', 'seq'), may hold values from -6 to 6
- inner_weight: float32 [2048, 6144], P(('dp', 'seq')), may hold values from -0.125 to 0.125
- outer_weight: float32 [2048, 2048], P(('dp', 'seq')), may hold values from -0.75 to 0.75
- expand_weight: float32 [2048, 16384], P(('dp', 'seq')), may hold values from -0.125 to 0.125
- shrink_weight: float32 [8192, 2048], P(('dp', 'seq')), may hold values from -0.0625 to 0.0625
- norm_gains: float32 [2, 2048], P(None, ('dp', 'seq')), may hold values from 0.3 to 2.5
- first_inner: float32 [2048, 6144], P(('dp', 'seq')), may hold values from -0.00021362305 to 0.00021362305
- first_outer: float32 [2048, 2048], P(('dp', 'seq')), may hold values from -0.00021362305 to 0.00021362305
- first_expand: float32 [2048, 16384], P(('dp', 'seq')), may hold values from -0.00021362305 to 0.00021362305
- first_shrink: float32 [8192, 2048], P(('dp', 'seq')), may hold values from -0.00021362305 to 0.00021362305
- first_gains: float32 [2, 2048], P(None, ('dp', 'seq')), may hold values from -0.0017089844 to 0.0017089844
- second_inner: float32 [2048, 6144], P(('dp', 'seq')), may hold values from 8e-10 to 3.2e-09
- second_outer: float32 [2048, 2048], P(('dp', 'seq')), may hold values from 8e-10 to 3.2e-09
- second_expand: float32 [2048, 16384], P(('dp', 'seq')), may hold values from 8e-10 to 3.2e-09
- second_shrink: float32 [8192, 2048], P(('dp', 'seq')), may hold values from 8e-10 to 3.2e-09
- second_gains: float32 [2, 2048], P(None, ('dp', 'seq')), may hold values from 5e-08 to 2e-07
- document_index: int32 [4, 1024], P('dp', 'seq'), may hold values from 0 to 3, as said below
- group_order: int32 [16], replicated, may hold values from 0 to 15, as said below
Outputs:
- layer_output: float32 [4, 1024, 2048], P('dp', 'seq')
- input_gradient: float32 [4, 1024, 2048], P('dp', 'seq')
- global_norm: float32 [], replicated
- moment_inner: float32 [2048, 6144], P(('dp', 'seq'))
- moment_outer: float32 [2048, 2048], P(('dp', 'seq'))
- moment_expand: float32 [2048, 16384], P(('dp', 'seq'))
- moment_shrink: float32 [8192, 2048], P(('dp', 'seq'))
- moment_gains: float32 [2, 2048], P(None, ('dp', 'seq'))
- square_inner: float32 [2048, 6144], P(('dp', 'seq'))
- square_outer: float32 [2048, 2048], P(('dp', 'seq'))
- square_expand: float32 [2048, 16384], P(('dp', 'seq'))
- square_shrink: float32 [8192, 2048], P(('dp', 'seq'))
- square_gains: float32 [2, 2048], P(None, ('dp', 'seq'))
- master_inner: float32 [2048, 6144], P(('dp', 'seq'))
- master_outer: float32 [2048, 2048], P(('dp', 'seq'))
- master_expand: float32 [2048, 16384], P(('dp', 'seq'))
- master_shrink: float32 [8192, 2048], P(('dp', 'seq'))
- master_gains: float32 [2, 2048], P(None, ('dp', 'seq'))
Inputs may be any that keep to these rules, and one draw needn't show every extreme that they name: `document_index`: In one sequence document 1 begins within the first 64 positions and ends within the last 64. `group_order`: each group number appears once.
All inputs are finite; a program needn't handle non-finite values.
Results may differ from a plain program's by a relative error of at most 0.015.
The roundings to bfloat16 on the way count: a program that leaves them out, or rounds other values in their place, can miss the bound.
Values may be sent and summed in bfloat16 or wider, within the bound.
No kernel may reach another device: no remote copies, remote signals or barrier semaphores. Data moves between devices by JAX's collectives and lax.ppermute only.
A program may use at most 576 MiB of HBM per device.

v0:
```python
import math

import jax
import jax.numpy as jnp
from jax import lax
from jax.sharding import PartitionSpec as P

HEADS = 16
STEP = 10


EPSILON = 1e-05
THETA = 10000.0
BETA_ONE = 0.9
BETA_TWO = 0.95
RATE = 0.05
GAIN_RATE = 0.5
DECAY = 0.1
ADAM_EPSILON = 1e-08
CLIP = 1.0


def angles(positions, width):
    frequency = THETA ** (-(jnp.arange(width // 2, dtype=jnp.float32) * 2.0) / width)
    turned = positions.astype(jnp.float32)[:, None] * frequency[None, :]
    return (jnp.cos(turned)[:, None, :], jnp.sin(turned)[:, None, :])


def rotate(values, cosine, sine):
    half = values.shape[-1] // 2
    first, second = (values[..., :half], values[..., half:])
    return jnp.concatenate(
        [first * cosine - second * sine, second * cosine + first * sine], axis=-1
    )


def unrotate(upstream, cosine, sine):
    half = upstream.shape[-1] // 2
    first, second = (upstream[..., :half], upstream[..., half:])
    return jnp.concatenate(
        [first * cosine + second * sine, second * cosine - first * sine], axis=-1
    )


def norm_back(upstream, normed, inverse):
    return inverse * (upstream - normed * jnp.mean(upstream * normed, axis=-1, keepdims=True))


def contract_rows(left, right):
    return lax.dot_general(
        left, right, (((0,), (0,)), ((), ())), preferred_element_type=jnp.float32
    )


def contract_last(left, right):
    return lax.dot_general(
        left, right, (((1,), (1,)), ((), ())), preferred_element_type=jnp.float32
    )


def project_in(normed, weight, gain):
    rows = normed.shape[0]

    def add_piece(carry, pieces, start):
        piece_left = (normed * pieces[1].astype(jnp.float32)).astype(jnp.bfloat16)
        partial_sum = jnp.dot(piece_left, pieces[0], preferred_element_type=jnp.float32)
        return (partial_sum, pieces[1])

    initial = (
        jnp.zeros((rows, weight.shape[1]), jnp.float32),
        jnp.zeros((normed.shape[1],), jnp.bfloat16),
    )
    product, full_gain = add_piece(
        initial,
        (
            lax.all_gather(weight.astype(jnp.bfloat16), ("dp", "seq"), axis=0, tiled=True),
            lax.all_gather(gain.astype(jnp.bfloat16), ("dp", "seq"), axis=0, tiled=True),
        ),
        jnp.int32(0),
    )
    left = (normed * full_gain.astype(jnp.float32)).astype(jnp.bfloat16)
    return (product, left, None, full_gain.astype(jnp.float32))


def project_mid(left, weight):

    def add_piece(partial_sum, piece, start):
        return jnp.dot(left, piece, preferred_element_type=jnp.float32)

    initial = jnp.zeros((left.shape[0], weight.shape[1]), jnp.float32)
    product = add_piece(
        initial,
        lax.all_gather(weight.astype(jnp.bfloat16), ("dp", "seq"), axis=0, tiled=True),
        jnp.int32(0),
    )
    return (product, None)


def weights_back(upstream, weight):
    return contract_last(
        upstream, lax.all_gather(weight.astype(jnp.bfloat16), ("dp", "seq"), axis=0, tiled=True)
    )


def reduce_in(left, upstream):
    owned = left.shape[1] // lax.axis_size(("dp", "seq"))

    def term(start, count):
        return contract_rows(left, upstream)

    return lax.psum_scatter(
        term(jnp.int32(0), lax.axis_size(("dp", "seq")) * owned),
        ("dp", "seq"),
        scatter_dimension=0,
        tiled=True,
    )


def reduce_mid(left, upstream):
    owned = left.shape[1] // lax.axis_size(("dp", "seq"))

    def term(start, count):
        return contract_rows(left, upstream)

    return lax.psum_scatter(
        term(jnp.int32(0), lax.axis_size(("dp", "seq")) * owned),
        ("dp", "seq"),
        scatter_dimension=0,
        tiled=True,
    )


def adamw(weight, grad, first, second, factor, decay, rate):
    grad = grad * factor
    first = BETA_ONE * first + (1.0 - BETA_ONE) * grad
    second = BETA_TWO * second + (1.0 - BETA_TWO) * grad * grad
    update = (
        first / (1.0 - BETA_ONE**STEP) / (jnp.sqrt(second / (1.0 - BETA_TWO**STEP)) + ADAM_EPSILON)
    )
    return (first, second, weight - rate * (update + decay * weight))


def body(
    tokens,
    cotangent,
    inner_weight,
    outer_weight,
    expand_weight,
    shrink_weight,
    norm_gains,
    first_inner,
    first_outer,
    first_expand,
    first_shrink,
    first_gains,
    second_inner,
    second_outer,
    second_expand,
    second_shrink,
    second_gains,
    document_index,
    group_order,
):
    inputs = tokens[0].astype(jnp.float32)
    rows, width = inputs.shape
    head_size = width // HEADS
    length = rows * lax.axis_size("seq")
    scale = head_size ** (-0.5)
    offset = -math.log(length)
    group = rows // 2
    within = jnp.arange(group, dtype=jnp.int32)
    paired = lax.dynamic_slice_in_dim(group_order, 2 * lax.axis_index("seq"), 2)
    own_place = (paired[:, None] * group + within[None, :]).reshape(-1)
    all_places = (group_order[:, None] * group + within[None, :]).reshape(-1)
    own_document = document_index[0].astype(jnp.bfloat16)
    cosine, sine = angles(own_place, head_size)
    inverse_first = lax.rsqrt(jnp.mean(inputs * inputs, axis=-1, keepdims=True) + EPSILON)
    normed_first = inputs * inverse_first
    projected, attend_input, kept_inner, gain_one = project_in(
        normed_first, inner_weight, norm_gains[0]
    )
    queries = projected[:, :width].reshape(rows, HEADS, head_size)
    query_rot = rotate(queries, cosine, sine).astype(jnp.bfloat16)
    key_rot = rotate(projected[:, width : 2 * width].reshape(rows, HEADS, head_size), cosine, sine)
    key_rot = key_rot.reshape(rows, width).astype(jnp.bfloat16)
    value_low = projected[:, 2 * width :].astype(jnp.bfloat16)

    def sigmoid_weights(key_piece, document_piece):
        count = key_piece.shape[0]
        scores = (
            jnp.einsum(
                "qhd,khd->hqk",
                query_rot,
                key_piece.reshape(count, HEADS, head_size),
                preferred_element_type=jnp.float32,
            )
            * scale
            + offset
        )
        visible = (own_document[:, None] == document_piece[None, :]) & (
            all_places[None, :] <= own_place[:, None]
        )
        return jax.nn.sigmoid(scores) * visible.astype(jnp.float32)[None]

    key_piece = lax.all_gather(key_rot, "seq", axis=0, tiled=True)
    value_piece = lax.all_gather(value_low, "seq", axis=0, tiled=True)
    document_piece = lax.all_gather(own_document, "seq", axis=0, tiled=True)
    count = key_piece.shape[0]
    weights = sigmoid_weights(key_piece, document_piece).astype(jnp.bfloat16)
    attended = jnp.einsum(
        "hqk,khd->qhd",
        weights,
        value_piece.reshape(count, HEADS, head_size),
        preferred_element_type=jnp.float32,
    )
    attended = attended.reshape(rows, width).astype(jnp.bfloat16)
    branch, kept_outer = project_mid(attended, outer_weight)
    residual = inputs + branch
    inverse_second = lax.rsqrt(jnp.mean(residual * residual, axis=-1, keepdims=True) + EPSILON)
    normed_second = residual * inverse_second
    gate_up, mlp_input, kept_expand, gain_two = project_in(
        normed_second, expand_weight, norm_gains[1]
    )
    hidden = gate_up.shape[1] // 2
    gate = gate_up[:, :hidden]
    upward = gate_up[:, hidden:]
    squash = jax.nn.sigmoid(gate)
    activation = (gate * squash * upward).astype(jnp.bfloat16)
    feed, kept_shrink = project_mid(activation, shrink_weight)
    output = residual + feed
    upstream = cotangent[0]
    down_grad = weights_back(upstream, shrink_weight)
    grad_shrink = reduce_mid(activation, upstream)
    d_gate = down_grad * upward * squash * (1.0 + gate * (1.0 - squash))
    d_upward = down_grad * gate * squash
    d_gate_up = jnp.concatenate([d_gate, d_upward], axis=1).astype(jnp.bfloat16)
    d_mlp_input = weights_back(d_gate_up, expand_weight)
    grad_expand = reduce_in(mlp_input, d_gate_up)
    partial_gain_two = jnp.sum(d_mlp_input * normed_second, axis=0)
    d_residual = upstream.astype(jnp.float32) + norm_back(
        d_mlp_input * gain_two, normed_second, inverse_second
    )
    d_residual_low = d_residual.astype(jnp.bfloat16)
    d_attended = weights_back(d_residual_low, outer_weight)
    grad_outer = reduce_mid(attended, d_residual_low)
    d_attended_flat = d_attended.astype(jnp.bfloat16)
    d_attended_low = d_attended_flat.reshape(rows, HEADS, head_size)
    key_piece = lax.all_gather(key_rot, "seq", axis=0, tiled=True)
    value_piece = lax.all_gather(value_low, "seq", axis=0, tiled=True)
    document_piece = lax.all_gather(own_document, "seq", axis=0, tiled=True)
    count = key_piece.shape[0]
    score_count = key_piece.shape[0]
    weights = sigmoid_weights(key_piece, document_piece)
    d_weights = jnp.einsum(
        "qhd,khd->hqk",
        d_attended_low,
        value_piece.reshape(score_count, HEADS, head_size),
        preferred_element_type=jnp.float32,
    )
    d_scores = (d_weights * weights * (1.0 - weights)).astype(jnp.bfloat16)
    weights, d_scores, key_heads = (
        weights,
        d_scores,
        key_piece.reshape(score_count, HEADS, head_size),
    )
    d_query = (
        jnp.einsum("hqk,khd->qhd", d_scores, key_heads, preferred_element_type=jnp.float32) * scale
    )
    key_term = (
        jnp.einsum("hqk,qhd->khd", d_scores, query_rot, preferred_element_type=jnp.float32) * scale
    )
    value_term = jnp.einsum(
        "hqk,qhd->khd",
        weights.astype(jnp.bfloat16),
        d_attended_low,
        preferred_element_type=jnp.float32,
    )
    d_keys = key_term.reshape(count, width)
    d_values = value_term.reshape(count, width)
    backward_sums = (d_query, d_keys, d_values)
    d_query = backward_sums[0]
    key_grad, value_grad = (
        lax.psum_scatter(
            backward_sums[1].astype(jnp.bfloat16), "seq", scatter_dimension=0, tiled=True
        ).astype(jnp.float32),
        lax.psum_scatter(
            backward_sums[2].astype(jnp.bfloat16), "seq", scatter_dimension=0, tiled=True
        ).astype(jnp.float32),
    )
    d_projected = jnp.concatenate(
        [
            unrotate(d_query, cosine, sine).reshape(rows, width),
            unrotate(key_grad.reshape(rows, HEADS, head_size), cosine, sine).reshape(rows, width),
            value_grad,
        ],
        axis=1,
    ).astype(jnp.bfloat16)
    d_attend_input = weights_back(d_projected, inner_weight)
    grad_inner = reduce_in(attend_input, d_projected)
    partial_gain_one = jnp.sum(d_attend_input * normed_first, axis=0)
    input_gradient = d_residual + norm_back(d_attend_input * gain_one, normed_first, inverse_first)
    local_squares = (
        jnp.sum(grad_inner * grad_inner)
        + jnp.sum(grad_outer * grad_outer)
        + jnp.sum(grad_expand * grad_expand)
    )
    local_squares = local_squares + jnp.sum(grad_shrink * grad_shrink)
    matrix_squares, gains_whole = lax.psum(
        (local_squares, jnp.stack([partial_gain_one, partial_gain_two])), ("dp", "seq")
    )
    owned_gains = norm_gains.shape[1]
    grad_gains = lax.dynamic_slice_in_dim(
        gains_whole, lax.axis_index(("dp", "seq")) * owned_gains, owned_gains, 1
    )
    global_norm = jnp.sqrt(matrix_squares + jnp.sum(gains_whole * gains_whole))
    factor = CLIP / jnp.maximum(global_norm, CLIP)
    gradients = (grad_inner, grad_outer, grad_expand, grad_shrink, grad_gains)
    masters = (inner_weight, outer_weight, expand_weight, shrink_weight, norm_gains)
    firsts = (first_inner, first_outer, first_expand, first_shrink, first_gains)
    seconds = (second_inner, second_outer, second_expand, second_shrink, second_gains)
    decays = (DECAY, DECAY, DECAY, DECAY, 0.0)
    rates = (RATE, RATE, RATE, RATE, GAIN_RATE)
    results = [
        adamw(
            masters[index],
            gradients[index],
            firsts[index],
            seconds[index],
            factor,
            decays[index],
            rates[index],
        )
        for index in range(5)
    ]
    return (
        output[None],
        input_gradient[None],
        global_norm,
        results[0][0],
        results[1][0],
        results[2][0],
        results[3][0],
        results[4][0],
        results[0][1],
        results[1][1],
        results[2][1],
        results[3][1],
        results[4][1],
        results[0][2],
        results[1][2],
        results[2][2],
        results[3][2],
        results[4][2],
    )


def solution(mesh):
    placed = (
        P("dp", "seq", None),
        P("dp", "seq", None),
        P(("dp", "seq"), None),
        P(("dp", "seq"), None),
        P(("dp", "seq"), None),
        P(("dp", "seq"), None),
        P(None, ("dp", "seq")),
        P(("dp", "seq"), None),
        P(("dp", "seq"), None),
        P(("dp", "seq"), None),
        P(("dp", "seq"), None),
        P(None, ("dp", "seq")),
        P(("dp", "seq"), None),
        P(("dp", "seq"), None),
        P(("dp", "seq"), None),
        P(("dp", "seq"), None),
        P(None, ("dp", "seq")),
        P("dp", "seq"),
        P(),
    )
    return jax.shard_map(
        body,
        mesh=mesh,
        in_specs=placed,
        out_specs=(
            P("dp", "seq", None),
            P("dp", "seq", None),
            P(),
            P(("dp", "seq"), None),
            P(("dp", "seq"), None),
            P(("dp", "seq"), None),
            P(("dp", "seq"), None),
            P(None, ("dp", "seq")),
            P(("dp", "seq"), None),
            P(("dp", "seq"), None),
            P(("dp", "seq"), None),
            P(("dp", "seq"), None),
            P(None, ("dp", "seq")),
            P(("dp", "seq"), None),
            P(("dp", "seq"), None),
            P(("dp", "seq"), None),
            P(("dp", "seq"), None),
            P(None, ("dp", "seq")),
        ),
        check_vma=False,
    )
```

profile of v0, /device:TPU:0, one launch (start us, length us, event | category | flops | bytes accessed | tf_op | source)
XLA Modules:
  0.0 6306.1 jit_solution(4879971367290432117)
XLA Ops:
  7.2 2.4 convert_element_type.134
  11.8 43.3 all-reduce.4
  56.7 113.9 %all-gather.10.cloned.1.call-done = bf16[2048,6144]{1,0:T(8,128)(2,1)} async-done(((bf16[64,6144]{1,0:T(8,128)(2,1)}), bf16[2048,6144]{1,0:T(8,128)(2,1)}) %all-gather.10.cloned.1.call-update) | async-done | bytes 25165840 | tf_op jit(solution)/shard_map/all_gather | solution.py:76
  170.5 10.1 fusion.45
  189.5 3.9 convert_element_type.148
  194.9 18.7 all-gather.1
  213.8 46.1 all-gather.14.cloned.1.call-done
  259.9 8.5 divide_multiply_fusion
  268.4 65.8 %all-gather.12.cloned.1.call-done = bf16[1024,2048]{1,0:T(8,128)(2,1)} async-done(((bf16[128,2048]{1,0:T(8,128)(2,1)}), bf16[1024,2048]{1,0:T(8,128)(2,1)}) %all-gather.12.cloned.1.call-update) | async-done | bytes 4194320 | tf_op jit(solution)/shard_map/all_gather | solution.py:206
  334.2 6.4 fusion.21
  340.6 72.7 %all-gather.16.cloned.1.call-done = bf16[2048,2048]{1,0:T(8,128)(2,1)} async-done(((bf16[64,2048]{1,0:T(8,128)(2,1)}), bf16[2048,2048]{1,0:T(8,128)(2,1)}) %all-gather.16.cloned.1.call-update) | async-done | bytes 8388624 | tf_op jit(solution)/shard_map/all_gather | solution.py:93
  413.3 4.7 multiply_reduce_fusion.5
  418.1 353.6 %all-gather.18.cloned.1.call-done = bf16[2048,16384]{1,0:T(8,128)(2,1)} async-done(((bf16[64,16384]{1,0:T(8,128)(2,1)}), bf16[2048,16384]{1,0:T(8,128)(2,1)}) %all-gather.18.cloned.1.call-update) | async-done | bytes 67108880 | tf_op jit(solution)/shard_map/all_gather | solution.py:76
  771.7 27.5 fusion.54
  799.2 168.9 %all-gather.20.cloned.1.call-done = bf16[8192,2048]{1,0:T(8,128)(2,1)} async-done(((bf16[256,2048]{1,0:T(8,128)(2,1)}), bf16[8192,2048]{1,0:T(8,128)(2,1)}) %all-gather.20.cloned.1.call-update) | async-done | bytes 33554448 | tf_op jit(solution)/shard_map/all_gather | solution.py:93
  968.1 21.0 multiply_convert_fusion.3
  989.0 31.0 multiply_reduce_fusion.3
  1021.7 7.4 convolution_convert_fusion.1
  1031.2 6.6 multiply_convert_fusion.1
  1037.8 3.4 multiply_convert_fusion
  1041.2 6.5 copy.83
  1047.8 6.8 convolution_convert_fusion
  1054.6 6.4 copy.85
  1061.2 8.1 fusion.41
  1069.5 4.9 fusion.20
  1074.4 59.6 reduce-scatter.20.cloned.1.call-done
  1136.4 2.4 copy.92
  1138.8 2.4 copy.91
  1141.1 3.2 add_convert_fusion.1
  1146.9 79.6 %reduce-scatter.22.cloned.1.call-done = bf16[128,2048]{1,0:T(8,128)(2,1)} async-done(((bf16[1024,2048]{1,0:T(8,128)(2,1)}), bf16[128,2048]{1,0:T(8,128)(2,1)}) %reduce-scatter.22.cloned.1.call-update) | async-done | bytes 524304
  1227.8 21.3 fusion.34
  1249.1 25.9 fusion.37
  1275.4 46.4 fusion.7
  1321.8 16.9 fusion.11
  1338.7 20.8 fusion.32
  1359.6 227.1 %reduce-scatter.16.cloned.1.call-done = f32[64,2048]{1,0:T(8,128)} async-done(((f32[2048,2048]{1,0:T(8,128)}), f32[64,2048]{1,0:T(8,128)}) %reduce-scatter.16.cloned.1.call-update) | async-done | bytes 524304 | tf_op jit(solution)/shard_map/reduce_scatter | solution.py:125
  1588.4 435.4 %reduce-scatter.14.cloned.1.call-done = f32[64,6144]{1,0:T(8,128)} async-done(((f32[2048,6144]{1,0:T(8,128)}), f32[64,6144]{1,0:T(8,128)}) %reduce-scatter.14.cloned.1.call-update) | async-done | bytes 1572880 | tf_op jit(solution)/shard_map/reduce_scatter | solution.py:111
  2023.8 2.4 multiply_reduce_fusion.2
  2027.5 1400.2 %reduce-scatter.18.cloned.1.call-done = f32[256,2048]{1,0:T(8,128)} async-done(((f32[8192,2048]{1,0:T(8,128)}), f32[256,2048]{1,0:T(8,128)}) %reduce-scatter.18.cloned.1.call-update) | async-done | bytes 2097168 | tf_op jit(solution)/shard_map/reduce_scatter | solution.py:125
  3427.7 2.7 multiply_reduce_fusion.1
  3430.5 2795.1 %reduce-scatter.24.cloned.1.call-done = f32[64,16384]{1,0:T(8,128)} async-done(((f32[2048,16384]{1,0:T(8,128)}), f32[64,16384]{1,0:T(8,128)}) %reduce-scatter.24.cloned.1.call-update) | async-done | bytes 4194320
  6225.6 3.9 multiply_reduce_fusion
  6230.8 2.6 fusion.31
  6233.4 39.9 all-reduce.3
  6276.0 2.7 multiply_subtract_fusion.3
  6278.7 5.0 multiply_subtract_fusion.2
  6283.8 6.3 multiply_subtract_fusion.1
  6292.0 5.7 multiply_subtract_fusion
  (130 shorter events, 29.7 us)
Async XLA Ops:
  7.2 163.3 %copy-start.5 = (bf16[1,128,2048]{2,1,0:T(8,128)(2,1)S(1)}, bf16[1,128,2048]{2,1,0:T(8,128)(2,1)}, u32[]{:S(2)}) copy-start(bf16[1,128,2048]{2,1,0:T(8,128)(2,1)} %param.19) | copy-start | bytes 1572868
  7.2 163.3 %all-gather.10.cloned.1.call-start = ((), (), s32[]{:S(2)}) async-start(), calls=%async_computation.6 | async-start | bytes 25952256 | tf_op jit(solution)/shard_map/all_gather | solution.py:76
  9.7 250.2 %all-gather.14.cloned.1.call-start = ((), (), s32[]{:S(2)}) async-start(), calls=%async_computation.8 | async-start | bytes 4718592 | tf_op jit(solution)/shard_map/all_gather | solution.py:205
  180.6 1.7 copy-start.6
  183.0 5.7 copy-start.16
  185.2 74.7 %copy-start.13 = (bf16[128,16,64]{2,0,1:T(8,128)(2,1)}, bf16[128,16,64]{2,0,1:T(8,128)(2,1)S(1)}, u32[]{:S(2)}) copy-start(bf16[128,16,64]{2,0,1:T(8,128)(2,1)S(1)} %get-tuple-element.48) | copy-start | bytes 786436
  186.5 147.7 %all-gather.12.cloned.1.call-start = ((), (), s32[]{:S(2)}) async-start(), calls=%async_computation.7 | async-start | bytes 4718592 | tf_op jit(solution)/shard_map/all_gather | solution.py:206
  188.7 224.7 %all-gather.16.cloned.1.call-start = ((), (), s32[]{:S(2)}) async-start(), calls=%async_computation.9 | async-start | bytes 8650752 | tf_op jit(solution)/shard_map/all_gather | solution.py:93
  189.5 4.0 copy-start.7
  189.5 582.2 %all-gather.18.cloned.1.call-start = ((), (), s32[]{:S(2)}) async-start(), calls=%async_computation.10 | async-start | bytes 69206016 | tf_op jit(solution)/shard_map/all_gather | solution.py:76
  193.4 1.3 copy-start.27
  193.4 1.4 copy-start.28
  193.4 774.6 %all-gather.20.cloned.1.call-start = ((), (), s32[]{:S(2)}) async-start(), calls=%async_computation.11 | async-start | bytes 34603008 | tf_op jit(solution)/shard_map/all_gather | solution.py:93
  194.6 939.4 %reduce-scatter.20.cloned.1.call-start = ((), (), s32[]{:S(2)}) async-start(), calls=%async_computation.15 | async-start | bytes 4718592
  771.6 196.4 %copy-start.12 = (bf16[1,128,2048]{2,1,0:T(8,128)(2,1)S(1)}, bf16[1,128,2048]{2,1,0:T(8,128)(2,1)}, u32[]{:S(2)}) copy-start(bf16[1,128,2048]{2,1,0:T(8,128)(2,1)} %param.20) | copy-start | bytes 1572868
  1021.7 39.5 copy-start.1
  1031.2 6.6 copy-start.14
  1031.2 6.7 copy-start.15
  1037.8 3.4 copy-start
  1047.8 178.7 %reduce-scatter.22.cloned.1.call-start = ((), (), s32[]{:S(2)}) async-start(), calls=%async_computation.16 | async-start | bytes 4718592
  1061.1 525.6 %reduce-scatter.16.cloned.1.call-start = ((), (), s32[]{:S(2)}) async-start(), calls=%async_computation.13 | async-start | bytes 17301504 | tf_op jit(solution)/shard_map/reduce_scatter | solution.py:125
  1069.3 954.6 %reduce-scatter.14.cloned.1.call-start = ((), (), s32[]{:S(2)}) async-start(), calls=%async_computation.12 | async-start | bytes 51904512 | tf_op jit(solution)/shard_map/reduce_scatter | solution.py:111
  1249.1 2178.6 %reduce-scatter.18.cloned.1.call-start = ((), (), s32[]{:S(2)}) async-start(), calls=%async_computation.14 | async-start | bytes 69206016 | tf_op jit(solution)/shard_map/reduce_scatter | solution.py:125
  1275.1 4950.5 %reduce-scatter.24.cloned.1.call-start = ((), (), s32[]{:S(2)}) async-start(), calls=%async_computation.17 | async-start | bytes 138412032
  1338.7 20.8 copy-start.23
  1359.5 4871.3 %copy-start.2 = (f32[128,2048]{1,0:T(8,128)S(1)}, f32[128,2048]{1,0:T(8,128)}, u32[]{:S(2)}) copy-start(f32[128,2048]{1,0:T(8,128)} %copy-done.1) | copy-start | bytes 3145732
  3430.5 2844.8 %copy-start.24 = (f32[2,64]{1,0:T(2,128)S(1)}, f32[2,64]{1,0:T(2,128)}, u32[]{:S(2)}) copy-start(f32[2,64]{1,0:T(2,128)} %param.25) | copy-start | bytes 1540
  3430.5 2844.8 %copy-start.25 = (f32[2,64]{1,0:T(2,128)S(1)}, f32[2,64]{1,0:T(2,128)}, u32[]{:S(2)}) copy-start(f32[2,64]{1,0:T(2,128)} %param.35) | copy-start | bytes 1540
  3430.5 2844.8 %copy-start.26 = (f32[2,64]{1,0:T(2,128)S(1)}, f32[2,64]{1,0:T(2,128)}, u32[]{:S(2)}) copy-start(f32[2,64]{1,0:T(2,128)} %param.30) | copy-start | bytes 1540
  3430.5 2845.5 %copy-start.17 = (f32[64,2048]{1,0:T(8,128)S(1)}, f32[64,2048]{1,0:T(8,128)}, u32[]{:S(2)}) copy-start(f32[64,2048]{1,0:T(8,128)} %param.22) | copy-start | bytes 1572868
  3430.5 2845.5 %copy-start.18 = (f32[64,2048]{1,0:T(8,128)S(1)}, f32[64,2048]{1,0:T(8,128)}, u32[]{:S(2)}) copy-start(f32[64,2048]{1,0:T(8,128)} %reduce-scatter.16.cloned.1.call-done) | copy-start | bytes 1572868
  3430.5 2845.5 %copy-start.22 = (f32[64,2048]{1,0:T(8,128)S(1)}, f32[64,2048]{1,0:T(8,128)}, u32[]{:S(2)}) copy-start(f32[64,2048]{1,0:T(8,128)} %param.32) | copy-start | bytes 1572868
  6275.3 3.4 copy-start.20
  6275.3 3.4 copy-start.21
  6278.7 5.1 copy-start.8
  6278.7 5.1 copy-start.9
  6278.7 5.0 copy-start.19
  6278.7 11.4 copy-start.11
  6283.8 6.4 copy-start.3
  6283.8 6.4 copy-start.4
  6283.8 8.2 copy-start.10
Sparse Core Ops, SparseCore 0:
  11.6 158.9 all-gather.9
  186.6 73.2 all-gather.13
  262.6 71.5 all-gather.11
  337.6 75.6 all-gather.15
  416.7 354.8 all-gather.17
  775.1 192.9 all-gather.19
  1047.9 86.0 reduce-scatter.19
  1138.7 87.7 reduce-scatter.21
  1228.8 357.8 reduce-scatter.15
  1592.9 430.8 reduce-scatter.13
  2026.2 1401.4 reduce-scatter.17
  3429.9 2795.6 reduce-scatter.23
where the time goes:
time: 6310 us
  waiting for transfers between devices  5820 us (92%)
  matrix products  278 us (4%)
  blocking collectives  102 us (2%)
    unnamed x15, waiting for transfers between devices  2930 us
    reduce_scatter x2, waiting for transfers between devices, reduce_mid(): lax.psum_scatter(term(jnp.int32(0), lax.axis_size(('dp', 'seq')) * owned)...  1630 us
    all_gather x2, waiting for transfers between devices, project_in(): lax.all_gather(weight.astype(jnp.bfloat16), ('dp', 'seq'), axis=0, tiled=...  467 us
    reduce_scatter x1, waiting for transfers between devices, reduce_in(): lax.psum_scatter(term(jnp.int32(0), lax.axis_size(('dp', 'seq')) * owned)...  435 us
    all_gather x2, waiting for transfers between devices, project_mid(): lax.all_gather(weight.astype(jnp.bfloat16), ('dp', 'seq'), axis=0, tiled=...  242 us
  transfers between devices with their start and end apart: 12, of which 12 were waited for; matrix products, arithmetic and copies ran while one was open for 4% of the time, Pallas kernels for 0%

commit v1 on v0

--- a/solution.py
+++ b/solution.py
@@ -18,6 +18,7 @@
 DECAY = 0.1
 ADAM_EPSILON = 1e-08
 CLIP = 1.0
+BOTH = ("dp", "seq")
 
 
 def angles(positions, width):
@@ -55,6 +56,351 @@
 def contract_last(left, right):
     return lax.dot_general(
         left, right, (((1,), (1,)), ((), ())), preferred_element_type=jnp.float32
+    )
+
+
+def multiply(left, right):
+    return jnp.dot(left, right, preferred_element_type=jnp.float32)
+
+
+def adamw(weight, grad, first, second, factor, decay, rate):
+    grad = grad * factor
+    first = BETA_ONE * first + (1.0 - BETA_ONE) * grad
+    second = BETA_TWO * second + (1.0 - BETA_TWO) * grad * grad
+    update = (
+        first / (1.0 - BETA_ONE**STEP) / (jnp.sqrt(second / (1.0 - BETA_TWO**STEP)) + ADAM_EPSILON)
+    )
+    return (first, second, weight - rate * (update + decay * weight))
+
+
+def move(value, where):
+    pairs = []
+    for dp in range(lax.axis_size("dp")):
+        for seq in range(lax.axis_size("seq")):
+            target = where(dp, seq // 2, seq % 2)
+            if target is not None:
+                pairs.append(
+                    (
+                        dp * lax.axis_size("seq") + seq,
+                        target[0] * lax.axis_size("seq") + target[1] * 2 + target[2],
+                    )
+                )
+    return lax.ppermute(value, BOTH, pairs)
+
+
+def depth_of():
+    return lax.axis_size("seq") // 2
+
+
+def across(value):
+    return move(value, lambda dp, z, x: (dp, z, 1 - x))
+
+
+def turn(value, k):
+    depth = depth_of()
+    return move(value, lambda dp, z, x: (dp, (z + k) % depth, x))
+
+
+def line(value, hop, direction):
+    depth = depth_of()
+
+    def where(dp, z, x):
+        if direction > 0:
+            return (dp, z + 1, x) if z >= hop - 1 and z + 1 < depth else None
+        return (dp, z - 1, x) if z <= depth - hop and z >= 1 else None
+
+    return move(value, where)
+
+
+def across_from(value, hop, direction):
+    depth = depth_of()
+
+    def where(dp, z, x):
+        valid = z >= hop if direction > 0 else z + hop < depth
+        return (dp, z, 1 - x) if valid else None
+
+    return move(value, where)
+
+
+def gather_rows(block):
+    depth = depth_of()
+    z = lax.axis_index("seq") // 2
+    up, down = [block], [block]
+    for hop in range(1, depth):
+        up.append(line(up[-1], hop, 1))
+        down.append(line(down[-1], hop, -1))
+    pieces = [jnp.concatenate([block, across(block)], axis=0)]
+    up_across = [None] + [across_from(up[k], k, 1) for k in range(1, depth)]
+    down_across = [None] + [across_from(down[k], k, -1) for k in range(1, depth)]
+    for k in range(1, depth):
+        pieces.append(
+            jnp.where(
+                z >= k,
+                jnp.concatenate([up[k], up_across[k]], axis=0),
+                jnp.concatenate([down[depth - k], down_across[depth - k]], axis=0),
+            )
+        )
+    return pieces
+
+
+def gather_small(block):
+    depth = depth_of()
+    column = jnp.stack([block] + [turn(block, k) for k in range(1, depth)])
+    other = across(column)
+    return jnp.stack([column, other], axis=1)
+
+
+def scatter_rows(partial):
+    depth = depth_of()
+    order = sorted(range(1, depth), key=lambda k: -min(k, depth - k)) + [0]
+    sums = {}
+    for k in order:
+        term = partial(k)
+        rows = term.shape[0] // 2
+        received = across(term[rows:])
+        total = term[:rows].astype(jnp.float32) + received.astype(jnp.float32)
+        sums[k] = turn(total.astype(jnp.bfloat16), -k).astype(jnp.float32) if k else total
+    total = sums[0]
+    for k in range(1, depth):
+        total = total + sums[k]
+    return total
+
+
+def sum_everywhere(value):
+    for stride in range(2):
+        value = value + move(value, lambda dp, z, x: (dp ^ (1 << stride), z, x))
+    for stride in range((depth_of() - 1).bit_length()):
+        value = value + move(value, lambda dp, z, x: (dp, z ^ (1 << stride), x))
+    return value + across(value)
+
+
+def swap(value):
+    return move(value, lambda dp, z, x: (x * 2 + dp % 2, z, dp // 2))
+
+
+def exchange(chunks):
+    return lax.all_to_all(chunks, "seq", 0, 0, tiled=True)
+
+
+def share(rows):
+    return lax.all_gather(rows, "dp", axis=0, tiled=True)
+
+
+def reduce_over(rows):
+    return lax.psum_scatter(rows, "dp", scatter_dimension=0, tiled=True)
+
+
+def body(
+    tokens,
+    cotangent,
+    inner_weight,
+    outer_weight,
+    expand_weight,
+    shrink_weight,
+    norm_gains,
+    first_inner,
+    first_outer,
+    first_expand,
+    first_shrink,
+    first_gains,
+    second_inner,
+    second_outer,
+    second_expand,
+    second_shrink,
+    second_gains,
+    document_index,
+    group_order,
+):
+    bf16, f32 = jnp.bfloat16, jnp.float32
+    rows, width = tokens.shape[1:]
+    n_dp, n_seq = lax.axis_size("dp"), lax.axis_size("seq")
+    depth = depth_of()
+    head = width // HEADS
+    own_heads = HEADS // n_seq
+    owned = inner_weight.shape[0]
+    length = rows * n_seq
+    scale = head ** (-0.5)
+    offset = -math.log(length)
+    group = rows // 2
+    hidden = expand_weight.shape[1] // 2
+    slab = shrink_weight.shape[0]
+    device = lax.axis_index(BOTH)
+    z, x = lax.axis_index("seq") // 2, lax.axis_index("seq") % 2
+
+    inputs_low = tokens[0]
+    upstream = cotangent[0]
+
+    inner_chunks = inner_weight.astype(bf16).reshape(owned, 3, 2, own_heads, depth, head)
+    inner_chunks = inner_chunks.transpose(4, 2, 0, 1, 3, 5).reshape(
+        n_seq, owned, 3 * own_heads * head
+    )
+    inner = share(exchange(inner_chunks).reshape(n_seq * owned, -1))
+    outer = share(swap(outer_weight.astype(bf16)))
+    outer = outer.reshape(2, own_heads, owned, width).transpose(1, 0, 2, 3).reshape(-1, width)
+    expand_chunks = expand_weight.astype(bf16).reshape(owned, 2, n_dp, n_seq, slab)
+    expand_chunks = expand_chunks.transpose(3, 0, 1, 2, 4).reshape(n_seq, owned, 2 * n_dp * slab)
+    expand = share(exchange(expand_chunks).reshape(n_seq * owned, -1))
+    shrink = share(shrink_weight.astype(bf16))
+
+    gains = lax.dynamic_update_slice(
+        jnp.zeros((2, width), f32),
+        norm_gains.astype(bf16).astype(f32),
+        (jnp.int32(0), device * norm_gains.shape[1]),
+    )
+    gains = sum_everywhere(gains)
+    gain_one, gain_two = gains[0], gains[1]
+
+    sources = [((z - k) % depth) * 2 + (x ^ j) for k in range(depth) for j in range(2)]
+    groups = jnp.concatenate([lax.dynamic_slice_in_dim(group_order, 2 * s, 2) for s in sources])
+    within = jnp.arange(group, dtype=jnp.int32)
+    places = (groups[:, None] * group + within[None, :]).reshape(-1)
+    documents = gather_small(document_index[0]).reshape(-1)
+    cosine, sine = angles(places, head)
+
+    def first_norm(piece):
+        values = piece.astype(f32)
+        inverse = lax.rsqrt(jnp.mean(values * values, axis=-1, keepdims=True) + EPSILON)
+        return values * inverse, inverse
+
+    token_pieces = gather_rows(inputs_low)
+    attend_pieces = [(first_norm(piece)[0] * gain_one).astype(bf16) for piece in token_pieces]
+    projected = jnp.concatenate([multiply(piece, inner) for piece in attend_pieces], axis=0)
+    projected = projected.reshape(length, 3, own_heads, head)
+    query_rot = rotate(projected[:, 0], cosine, sine).astype(bf16)
+    key_rot = rotate(projected[:, 1], cosine, sine).astype(bf16)
+    value_low = projected[:, 2].astype(bf16)
+
+    visible = (documents[:, None] == documents[None, :]) & (places[None, :] <= places[:, None])
+    visible = visible.astype(f32)[None]
+
+    def heads_dot(spec, left, right):
+        return jnp.einsum(spec, left, right, preferred_element_type=f32)
+
+    scores = heads_dot("qhd,khd->hqk", query_rot, key_rot) * scale + offset
+    weights = jax.nn.sigmoid(scores) * visible
+    weights_low = weights.astype(bf16)
+    attended = heads_dot("hqk,khd->qhd", weights_low, value_low)
+    attended = attended.reshape(length, own_heads * head).astype(bf16)
+
+    def rows_of(array, k):
+        return array[2 * rows * k : 2 * rows * (k + 1)]
+
+    branch = scatter_rows(lambda k: multiply(rows_of(attended, k), outer).astype(bf16))
+    inputs = inputs_low.astype(f32)
+    residual = inputs + branch
+    inverse_second = lax.rsqrt(jnp.mean(residual * residual, axis=-1, keepdims=True) + EPSILON)
+    normed_second = residual * inverse_second
+
+    upstream_pieces = gather_rows(upstream)
+    mlp_pieces = gather_rows((normed_second * gain_two).astype(bf16))
+    share_hidden = hidden // n_seq
+
+    activations, gate_up_grads = [None] * depth, [None] * depth
+
+    def feed_back(k):
+        gate_up = multiply(mlp_pieces[k], expand)
+        gate, upward = gate_up[:, :share_hidden], gate_up[:, share_hidden:]
+        squash = jax.nn.sigmoid(gate)
+        activations[k] = (gate * squash * upward).astype(bf16)
+        down_grad = contract_last(upstream_pieces[k], shrink)
+        d_gate = down_grad * upward * squash * (1.0 + gate * (1.0 - squash))
+        d_upward = down_grad * gate * squash
+        gate_up_grads[k] = jnp.concatenate([d_gate, d_upward], axis=1).astype(bf16)
+        return contract_last(gate_up_grads[k], expand).astype(bf16)
+
+    d_mlp_input = scatter_rows(feed_back)
+    feed = scatter_rows(lambda k: multiply(activations[k], shrink).astype(bf16))
+    output = residual + feed
+    upstream_all = jnp.concatenate(upstream_pieces, axis=0)
+    grad_shrink = reduce_over(
+        contract_rows(jnp.concatenate(activations, axis=0), upstream_all).astype(bf16)
+    )
+    grad_expand = contract_rows(
+        jnp.concatenate(mlp_pieces, axis=0), jnp.concatenate(gate_up_grads, axis=0)
+    )
+    grad_expand = reduce_over(grad_expand.astype(bf16))
+
+    partial_gain_two = jnp.sum(d_mlp_input * normed_second, axis=0)
+    d_residual = upstream.astype(f32) + norm_back(
+        d_mlp_input * gain_two, normed_second, inverse_second
+    )
+
+    residual_pieces = gather_rows(d_residual.astype(bf16))
+    d_attended = jnp.concatenate(
+        [contract_last(piece, outer) for piece in residual_pieces], axis=0
+    ).astype(bf16)
+    grad_outer = contract_rows(attended, jnp.concatenate(residual_pieces, axis=0)).astype(bf16)
+    grad_outer = grad_outer.reshape(own_heads, 2, owned, width).transpose(1, 0, 2, 3)
+    grad_outer = reduce_over(grad_outer.reshape(-1, width))
+    d_attended = d_attended.reshape(length, own_heads, head)
+    d_weights = heads_dot("qhd,khd->hqk", d_attended, value_low)
+    d_scores = (d_weights * weights * (1.0 - weights)).astype(bf16)
+    d_query = heads_dot("hqk,khd->qhd", d_scores, key_rot) * scale
+    d_key = heads_dot("hqk,qhd->khd", d_scores, query_rot) * scale
+    d_value = heads_dot("hqk,qhd->khd", weights_low, d_attended)
+    d_projected = jnp.stack(
+        [unrotate(d_query, cosine, sine), unrotate(d_key, cosine, sine), d_value], axis=1
+    )
+    d_projected = d_projected.reshape(length, -1).astype(bf16)
+    d_attend_input = scatter_rows(
+        lambda k: contract_last(rows_of(d_projected, k), inner).astype(bf16)
+    )
+    grad_inner = contract_rows(jnp.concatenate(attend_pieces, axis=0), d_projected)
+    grad_inner = reduce_over(grad_inner.astype(bf16))
+
+    normed_first, inverse_first = first_norm(inputs_low)
+    partial_gain_one = jnp.sum(d_attend_input * normed_first, axis=0)
+    input_gradient = d_residual + norm_back(d_attend_input * gain_one, normed_first, inverse_first)
+
+    local_squares = sum(
+        jnp.sum(jnp.square(grad.astype(f32)))
+        for grad in (grad_inner, grad_outer, grad_expand, grad_shrink)
+    )
+    sums = sum_everywhere(
+        jnp.concatenate(
+            [partial_gain_one, partial_gain_two, jnp.full((128,), local_squares)]
+        ).reshape(-1, 128)
+    ).reshape(-1)
+    gains_whole = sums[: 2 * width].reshape(2, width)
+    grad_gains = lax.dynamic_slice_in_dim(
+        gains_whole, device * norm_gains.shape[1], norm_gains.shape[1], 1
+    )
+    global_norm = jnp.sqrt(sums[2 * width] + jnp.sum(gains_whole * gains_whole))
+    factor = CLIP / jnp.maximum(global_norm, CLIP)
+
+    grad_inner = exchange(grad_inner.reshape(n_seq, owned, -1))
+    grad_inner = grad_inner.reshape(depth, 2, owned, 3, own_heads, head)
+    grad_inner = grad_inner.transpose(2, 3, 1, 4, 0, 5).reshape(inner_weight.shape)
+    grad_outer = swap(grad_outer)
+    grad_expand = exchange(grad_expand.reshape(n_seq, owned, -1))
+    grad_expand = grad_expand.reshape(n_seq, owned, 2, n_dp, slab)
+    grad_expand = grad_expand.transpose(1, 2, 3, 0, 4).reshape(expand_weight.shape)
+
+    gradients = (grad_inner, grad_outer, grad_expand, grad_shrink, grad_gains)
+    masters = (inner_weight, outer_weight, expand_weight, shrink_weight, norm_gains)
+    firsts = (first_inner, first_outer, first_expand, first_shrink, first_gains)
+    seconds = (second_inner, second_outer, second_expand, second_shrink, second_gains)
+    decays = (DECAY, DECAY, DECAY, DECAY, 0.0)
+    rates = (RATE, RATE, RATE, RATE, GAIN_RATE)
+    results = [
+        adamw(
+            masters[index],
+            gradients[index].astype(f32),
+            firsts[index],
+            seconds[index],
+            factor,
+            decays[index],
+            rates[index],
+        )
+        for index in range(5)
+    ]
+    return (
+        output[None],
+        input_gradient[None],
+        global_norm,
+        *(result[0] for result in results),
+        *(result[1] for result in results),
+        *(result[2] for result in results),
     )
 
 
@@ -130,17 +476,7 @@
     )
 
 
-def adamw(weight, grad, first, second, factor, decay, rate):
-    grad = grad * factor
-    first = BETA_ONE * first + (1.0 - BETA_ONE) * grad
-    second = BETA_TWO * second + (1.0 - BETA_TWO) * grad * grad
-    update = (
-        first / (1.0 - BETA_ONE**STEP) / (jnp.sqrt(second / (1.0 - BETA_TWO**STEP)) + ADAM_EPSILON)
-    )
-    return (first, second, weight - rate * (update + decay * weight))
-
-
-def body(
+def gathered_body(
     tokens,
     cotangent,
     inner_weight,
@@ -355,6 +691,7 @@
 
 
 def solution(mesh):
+    whole_heads = HEADS % mesh.shape["seq"] == 0 and mesh.shape["dp"] == 4
     placed = (
         P("dp", "seq", None),
         P("dp", "seq", None),
@@ -377,7 +714,7 @@
         P(),
     )
     return jax.shard_map(
-        body,
+        body if whole_heads else gathered_body,
         mesh=mesh,
         in_specs=placed,
         out_specs=(

time: 6310 us -> 942 us (0.15)
  waiting for transfers between devices: 5820 us -> 294 us
  starting transfers between devices: 0.88 us -> 236 us
  matrix products: 278 us -> 125 us
    unnamed x15 -> x8, waiting for transfers between devices: 2930 us -> 0.13 us
    reduce_scatter x3 -> x4, waiting for transfers between devices: 2060 us -> 0.03 us  [reduce_over(): return lax.psum_scatter(rows, 'dp', scatter_dimension=0, tiled=True)]
    all_gather x6 -> x4, waiting for transfers between devices: 821 us -> 0.04 us  [share(): return lax.all_gather(rows, 'dp', axis=0, tiled=True)]
    ppermute x0 -> x96, waiting for transfers between devices: none -> 272 us  [move(): return lax.ppermute(value, BOTH, pairs)]
    ppermute x0 -> x96, starting transfers between devices: none -> 225 us  [move(): return lax.ppermute(value, BOTH, pairs)]
    all_to_all x0 -> x2, blocking collectives: none -> 88.5 us  [exchange(): return lax.all_to_all(chunks, 'seq', 0, 0, tiled=True)]
  transfers between devices with their start and end apart: 12 -> 106, of which waited for: 12 -> 36; matrix products, arithmetic and copies ran while one was open for 4% -> 27% of each run, Pallas kernels for 0% -> 0%
where the time goes in v1:
time: 942 us; the launch traced here: 932 us
  waiting for transfers between devices  294 us (31%)
  starting transfers between devices  236 us (25%)
  matrix products  125 us (13%)
  other arithmetic  92.9 us (10%)
  blocking collectives  88.5 us (9%)
  local copies, waits for them, and re-layouts  73.2 us (8%)
  between operations  22.4 us (2%)
    ppermute x96, waiting for transfers between devices, move(): return lax.ppermute(value, BOTH, pairs)  272 us
    ppermute x96, starting transfers between devices, move(): return lax.ppermute(value, BOTH, pairs)  225 us
    all_to_all x2, blocking collectives, exchange(): return lax.all_to_all(chunks, 'seq', 0, 0, tiled=True)  88.5 us
    dot_general x4, matrix products, contract_rows(): lax.dot_general(left, right, (((0,), (0,)), ((), ())), preferred_element_...  43.2 us
    dot_general x16, matrix products, contract_last(): lax.dot_general(left, right, (((1,), (1,)), ((), ())), preferred_element_...  35.6 us
    dot_general x16, matrix products, multiply(): return jnp.dot(left, right, preferred_element_type=jnp.float32)  31.7 us
    unnamed x254, local copies, waits for them, and re-layouts  22.4 us
    all_to_all x2, waiting for transfers between devices, exchange(): return lax.all_to_all(chunks, 'seq', 0, 0, tiled=True)  21.9 us
  transfers between devices with their start and end apart: 106, of which 36 were waited for; matrix products, arithmetic and copies ran while one was open for 27% of the time, Pallas kernels for 0%

profile of v1, /device:TPU:0, one launch (start us, length us, event | category | flops | bytes accessed | tf_op | source)
XLA Modules:
  0.0 931.7 jit_solution(6162934746189172827)
XLA Ops:
  12.8 36.6 %all_to_all.20 = bf16[8,64,768]{2,1,0:T(8,128)(2,1)} all-to-all(bf16[8,64,768]{2,1,0:T(8,128)(2,1)S(1)} %reshape.396), channel_id=1, replica_groups=mesh['dp'=4,'seq'=8] {'seq'}, dimensions={0} | all-to-all | bytes 1572864 | tf_op jit(solution)/shard_map/all_to_all | solution.py:182
  56.0 51.9 %all_to_all.21 = bf16[8,64,2048]{2,1,0:T(8,128)(2,1)} all-to-all(bf16[8,64,2048]{2,1,0:T(8,128)(2,1)} %reshape.402), channel_id=1, replica_groups=mesh['dp'=4,'seq'=8] {'seq'}, dimensions={0} | all-to-all | bytes 4194304 | tf_op jit(solution)/shard_map/all_to_all | solution.py:182
  112.3 5.4 collective-permute-start.6
  119.7 5.9 collective-permute-done.6
  132.4 5.4 collective-permute-start.3
  143.7 6.9 collective-permute-done.4
  164.7 7.1 collective-permute-done.14
  205.4 5.2 reshape.398
  235.4 9.1 collective-permute-done.28
  244.7 20.9 %collective-permute-done.26 = bf16[128,2048]{1,0:T(8,128)(2,1)S(1)} collective-permute-done((bf16[128,2048]{1,0:T(8,128)(2,1)S(1)}, bf16[128,2048]{1,0:T(8,128)(2,1)S(1)}, u32[]{:S(2)}, u32[]{:S(2)}) %collective-permute-start.26) | collective-permute-done | bytes 524320 | tf_op jit(solution)/shard_map/ppermute | solution.py:88
  265.8 4.7 collective-permute-start.27
  274.7 12.3 %collective-permute-done.27 = bf16[128,2048]{1,0:T(8,128)(2,1)S(1)} collective-permute-done((bf16[128,2048]{1,0:T(8,128)(2,1)S(1)}, bf16[128,2048]{1,0:T(8,128)(2,1)S(1)}, u32[]{:S(2)}, u32[]{:S(2)}) %collective-permute-start.27) | collective-permute-done | bytes 524320 | tf_op jit(solution)/shard_map/ppermute | solution.py:88
  288.6 9.2 collective-permute-start.32
  299.7 7.1 collective-permute-done.32
  318.7 18.4 %collective-permute-done.34 = bf16[128,2048]{1,0:T(8,128)(2,1)} collective-permute-done((bf16[128,2048]{1,0:T(8,128)(2,1)S(1)}, bf16[128,2048]{1,0:T(8,128)(2,1)}, u32[]{:S(2)}, u32[]{:S(2)}) %collective-permute-start.34) | collective-permute-done | bytes 524320 | tf_op jit(solution)/shard_map/ppermute | solution.py:88
  352.2 7.7 fusion.127
  359.9 6.8 collective-permute-done.67
  375.7 6.0 multiply_convert_fusion.2
  391.8 20.8 %collective-permute-start.53 = (bf16[128,2048]{1,0:T(8,128)(2,1)S(1)}, bf16[128,2048]{1,0:T(8,128)(2,1)S(1)}, u32[]{:S(2)}, u32[]{:S(2)}) collective-permute-start(bf16[128,2048]{1,0:T(8,128)(2,1)S(1)} %copy-done.63), channel_id=1, source_target_pairs={{2,3},{3,2},{4,5},{5,4},{6,7},{7,6},{10,11},{11,10},{12,13},{13,12... | collective-permute-start | bytes 1572872 | tf_op jit(solution)/shard_map/ppermute | solution.py:88
  427.7 12.8 %collective-permute-done.37 = bf16[128,2048]{1,0:T(8,128)(2,1)S(1)} collective-permute-done((bf16[128,2048]{1,0:T(8,128)(2,1)S(1)}, bf16[128,2048]{1,0:T(8,128)(2,1)S(1)}, u32[]{:S(2)}, u32[]{:S(2)}) %collective-permute-start.37) | collective-permute-done | bytes 524320 | tf_op jit(solution)/shard_map/ppermute | solution.py:88
  466.3 7.9 collective-permute-done.63
  478.4 7.0 collective-permute-done.58
  485.6 5.0 collective-permute-start.59
  490.6 5.5 collective-permute-done.51
  500.4 9.2 collective-permute-done.59
  512.7 5.1 collective-permute-start.71
  517.8 10.1 %collective-permute-done.73 = bf16[128,2048]{1,0:T(8,128)(2,1)S(1)} collective-permute-done((bf16[128,2048]{1,0:T(8,128)(2,1)S(1)}, bf16[128,2048]{1,0:T(8,128)(2,1)S(1)}, u32[]{:S(2)}, u32[]{:S(2)}) %collective-permute-start.73) | collective-permute-done | bytes 524320 | tf_op jit(solution)/shard_map/ppermute | solution.py:88
  531.4 11.7 %collective-permute-done.74 = bf16[128,2048]{1,0:T(8,128)(2,1)S(1)} collective-permute-done((bf16[128,2048]{1,0:T(8,128)(2,1)S(1)}, bf16[128,2048]{1,0:T(8,128)(2,1)S(1)}, u32[]{:S(2)}, u32[]{:S(2)}) %collective-permute-start.74) | collective-permute-done | bytes 524320 | tf_op jit(solution)/shard_map/ppermute | solution.py:88
  549.9 7.5 collective-permute-done.75
  565.0 9.1 collective-permute-done.76
  575.0 7.0 collective-permute-done.82
  601.8 8.2 fusion.24
  620.6 9.1 convolution_convert_fusion.1
  640.4 24.7 %convolution_convert_fusion = bf16[2048,2048]{1,0:T(8,128)(2,1)} fusion(bf16[1024,2048]{1,0:T(8,128)(2,1)} %constant_dynamic-update-slice_fusion.5, bf16[256,1024]{1,0:T(8,128)(2,1)S(1)} %copy-done.109, bf16[256,1024]{1,0:T(8,128)(2,1)S(1)} %copy-done.107, bf16[256,1024]{1,0:T(8,128)(2,1)S(1)} %copy-done.113, bf16[256,1024]{1,0:T(8,128)(2,1)S(1)} %copy-done.111, ...), kind=kOutput, calls=%fused_computation.2 | convolution fusion | flops 8627683328 | bytes 16777216 | tf_op jit(solution)/shard_map/dot_general | solution.py:51
  694.7 13.9 %collective-permute-done.84 = bf16[128,2048]{1,0:T(8,128)(2,1)S(1)} collective-permute-done((bf16[128,2048]{1,0:T(8,128)(2,1)S(1)}, bf16[128,2048]{1,0:T(8,128)(2,1)S(1)}, u32[]{:S(2)}, u32[]{:S(2)}) %collective-permute-start.84) | collective-permute-done | bytes 524320 | tf_op jit(solution)/shard_map/ppermute | solution.py:88
  710.3 9.5 %collective-permute-done.86 = bf16[128,2048]{1,0:T(8,128)(2,1)S(1)} collective-permute-done((bf16[128,2048]{1,0:T(8,128)(2,1)S(1)}, bf16[128,2048]{1,0:T(8,128)(2,1)S(1)}, u32[]{:S(2)}, u32[]{:S(2)}) %collective-permute-start.86) | collective-permute-done | bytes 524320 | tf_op jit(solution)/shard_map/ppermute | solution.py:88
  723.4 7.6 collective-permute-done.88
  743.2 29.9 %collective-permute-start.49 = (bf16[128,2048]{1,0:T(8,128)(2,1)}, bf16[128,2048]{1,0:T(8,128)(2,1)}, u32[]{:S(2)}, u32[]{:S(2)}) collective-permute-start(bf16[128,2048]{1,0:T(8,128)(2,1)} %add_convert_fusion.8), channel_id=1, source_target_pairs={{0,2},{1,3},{2,4},{3,5},{4,6},{5,7},{6,0},{7,1},{8,10},{9,11},{10,... | collective-permute-start | bytes 1572872 | tf_op jit(solution)/shard_map/ppermute | solution.py:88
  773.1 13.5 %collective-permute-done.87 = bf16[128,2048]{1,0:T(8,128)(2,1)S(1)} collective-permute-done((bf16[128,2048]{1,0:T(8,128)(2,1)S(1)}, bf16[128,2048]{1,0:T(8,128)(2,1)S(1)}, u32[]{:S(2)}, u32[]{:S(2)}) %collective-permute-start.87) | collective-permute-done | bytes 524320 | tf_op jit(solution)/shard_map/ppermute | solution.py:88
  802.4 6.3 all-to-all-start.2
  814.7 14.1 %collective-permute-done.92 = f32[33,128]{1,0:T(8,128)S(1)} collective-permute-done((f32[33,128]{1,0:T(8,128)S(1)}, f32[33,128]{1,0:T(8,128)S(1)}, u32[]{:S(2)}, u32[]{:S(2)}) %collective-permute-start.92) | collective-permute-done | bytes 16928 | tf_op jit(solution)/shard_map/ppermute | solution.py:88
  828.8 6.0 collective-permute-start.93
  834.8 4.5 collective-permute-done.93
  869.5 6.3 multiply_subtract_fusion.1
  878.8 21.9 %all-to-all-done.3 = bf16[8,64,2048]{2,1,0:T(8,128)(2,1)S(1)} async-done(((bf16[8,64,2048]{2,1,0:T(8,128)(2,1)}), bf16[8,64,2048]{2,1,0:T(8,128)(2,1)S(1)}, u32[]{:S(2)}, u32[]{:S(2)}) %all-to-all-start.3) | async-done | bytes 2097184 | tf_op jit(solution)/shard_map/all_to_all | solution.py:182
  903.3 6.2 mul.808
  909.5 4.8 copy.72
  917.8 5.6 multiply_subtract_fusion
  (604 shorter events, 372.1 us)
Async XLA Ops:
  7.2 170.7 %all-gather.7.cloned.1.call-start = ((), (), s32[]{:S(2)}) async-start(), calls=%async_computation.9 | async-start | bytes 1310720 | tf_op jit(solution)/shard_map/all_gather | solution.py:186
  9.7 186.8 %all-gather.5.cloned.1.call-start = ((), (), s32[]{:S(2)}) async-start(), calls=%async_computation.8 | async-start | bytes 3932160 | tf_op jit(solution)/shard_map/all_gather | solution.py:186
  49.4 302.8 %all-gather.9.cloned.1.call-start = ((), (), s32[]{:S(2)}) async-start(), calls=%async_computation.10 | async-start | bytes 10485760 | tf_op jit(solution)/shard_map/all_gather | solution.py:186
  107.9 267.7 %all-gather.11.cloned.1.call-start = ((), (), s32[]{:S(2)}) async-start(), calls=%async_computation.11 | async-start | bytes 5242880 | tf_op jit(solution)/shard_map/all_gather | solution.py:186
  111.0 26.8 %collective-permute-start.8 = (bf16[128,2048]{1,0:T(8,128)(2,1)S(1)}, bf16[128,2048]{1,0:T(8,128)(2,1)}, u32[]{:S(2)}, u32[]{:S(2)}) collective-permute-start(bf16[128,2048]{1,0:T(8,128)(2,1)S(1)} %bitcast.179), channel_id=1, source_target_pairs={{2,0},{3,1},{4,2},{5,3},{6,4},{7,5},{10,8},{11,9},{12,10},{13,11},... | collective-permute-start | bytes 1572872 | tf_op jit(solution)/shard_map/ppermute | solution.py:88
  119.2 669.0 %reduce-scatter.7.cloned.1.call-start = ((), (), s32[]{:S(2)}) async-start(), calls=%async_computation.13 | async-start | bytes 1310720 | tf_op jit(solution)/shard_map/reduce_scatter | solution.py:190
  125.6 25.4 %collective-permute-start.12 = (bf16[128,2048]{1,0:T(8,128)(2,1)}, bf16[128,2048]{1,0:T(8,128)(2,1)S(1)}, u32[]{:S(2)}, u32[]{:S(2)}) collective-permute-start(bf16[128,2048]{1,0:T(8,128)(2,1)} %collective-permute-done.6), channel_id=1, source_target_pairs={{2,4},{3,5},{4,6},{5,7},{10,12},{11,13},{12,14},{13,15},{18,20},{1... | collective-permute-start | bytes 1572872 | tf_op jit(solution)/shard_map/ppermute | solution.py:88
  126.5 34.1 %collective-permute-start = (bf16[128,2048]{1,0:T(8,128)(2,1)S(1)}, bf16[128,2048]{1,0:T(8,128)(2,1)S(1)}, u32[]{:S(2)}, u32[]{:S(2)}) collective-permute-start(bf16[128,2048]{1,0:T(8,128)(2,1)S(1)} %bitcast.181), channel_id=1, source_target_pairs={{0,1},{1,0},{2,3},{3,2},{4,5},{5,4},{6,7},{7,6},{8,9},{9,8},{10,11... | collective-permute-start | bytes 1572872 | tf_op jit(solution)/shard_map/ppermute | solution.py:88
  231.8 42.8 %collective-permute-start.23 = (bf16[128,2048]{1,0:T(8,128)(2,1)S(1)}, bf16[128,2048]{1,0:T(8,128)(2,1)S(1)}, u32[]{:S(2)}, u32[]{:S(2)}) collective-permute-start(bf16[128,2048]{1,0:T(8,128)(2,1)S(1)} %slice.296), channel_id=1, source_target_pairs={{0,1},{1,0},{2,3},{3,2},{4,5},{5,4},{6,7},{7,6},{8,9},{9,8},{10,11... | collective-permute-start | bytes 1572872 | tf_op jit(solution)/shard_map/ppermute | solution.py:88
  232.8 32.8 %collective-permute-start.26 = (bf16[128,2048]{1,0:T(8,128)(2,1)S(1)}, bf16[128,2048]{1,0:T(8,128)(2,1)S(1)}, u32[]{:S(2)}, u32[]{:S(2)}) collective-permute-start(bf16[128,2048]{1,0:T(8,128)(2,1)S(1)} %slice.302), channel_id=1, source_target_pairs={{0,1},{1,0},{2,3},{3,2},{4,5},{5,4},{6,7},{7,6},{8,9},{9,8},{10,11... | collective-permute-start | bytes 1572872 | tf_op jit(solution)/shard_map/ppermute | solution.py:88
  235.0 36.2 %collective-permute-start.24 = (bf16[128,2048]{1,0:T(8,128)(2,1)S(1)}, bf16[128,2048]{1,0:T(8,128)(2,1)S(1)}, u32[]{:S(2)}, u32[]{:S(2)}) collective-permute-start(bf16[128,2048]{1,0:T(8,128)(2,1)S(1)} %slice.299), channel_id=1, source_target_pairs={{0,1},{1,0},{2,3},{3,2},{4,5},{5,4},{6,7},{7,6},{8,9},{9,8},{10,11... | collective-permute-start | bytes 1572872 | tf_op jit(solution)/shard_map/ppermute | solution.py:88
  244.7 30.0 %collective-permute-start.29 = (bf16[128,2048]{1,0:T(8,128)(2,1)S(1)}, bf16[128,2048]{1,0:T(8,128)(2,1)S(1)}, u32[]{:S(2)}, u32[]{:S(2)}) collective-permute-start(bf16[128,2048]{1,0:T(8,128)(2,1)S(1)} %add_convert_fusion.11), channel_id=1, source_target_pairs={{0,2},{1,3},{2,4},{3,5},{4,6},{5,7},{6,0},{7,1},{8,10},{9,11},{10,... | collective-permute-start | bytes 1572872 | tf_op jit(solution)/shard_map/ppermute | solution.py:88
  315.2 24.0 %collective-permute-start.45 = (bf16[128,2048]{1,0:T(8,128)(2,1)}, bf16[128,2048]{1,0:T(8,128)(2,1)S(1)}, u32[]{:S(2)}, u32[]{:S(2)}) collective-permute-start(bf16[128,2048]{1,0:T(8,128)(2,1)} %collective-permute-done.40), channel_id=1, source_target_pairs={{4,6},{5,7},{12,14},{13,15},{20,22},{21,23},{28,30},{29,31}} | collective-permute-start | bytes 1572872 | tf_op jit(solution)/shard_map/ppermute | solution.py:88
  315.9 28.0 %collective-permute-start.54 = (bf16[128,2048]{1,0:T(8,128)(2,1)S(1)}, bf16[128,2048]{1,0:T(8,128)(2,1)}, u32[]{:S(2)}, u32[]{:S(2)}) collective-permute-start(bf16[128,2048]{1,0:T(8,128)(2,1)S(1)} %bitcast.195), channel_id=1, source_target_pairs={{2,0},{3,1},{4,2},{5,3},{6,4},{7,5},{10,8},{11,9},{12,10},{13,11},... | collective-permute-start | bytes 1572872 | tf_op jit(solution)/shard_map/ppermute | solution.py:88
  317.2 28.7 %collective-permute-start.65 = (bf16[128,2048]{1,0:T(8,128)(2,1)}, bf16[128,2048]{1,0:T(8,128)(2,1)}, u32[]{:S(2)}, u32[]{:S(2)}) collective-permute-start(bf16[128,2048]{1,0:T(8,128)(2,1)} %collective-permute-done.60), channel_id=1, source_target_pairs={{4,6},{5,7},{12,14},{13,15},{20,22},{21,23},{28,30},{29,31}} | collective-permute-start | bytes 1572872 | tf_op jit(solution)/shard_map/ppermute | solution.py:88
  339.9 115.1 %collective-permute-start.50 = (bf16[128,2048]{1,0:T(8,128)(2,1)S(1)}, bf16[128,2048]{1,0:T(8,128)(2,1)}, u32[]{:S(2)}, u32[]{:S(2)}) collective-permute-start(bf16[128,2048]{1,0:T(8,128)(2,1)S(1)} %bitcast.196), channel_id=1, source_target_pairs={{0,1},{1,0},{2,3},{3,2},{4,5},{5,4},{6,7},{7,6},{8,9},{9,8},{10,11... | collective-permute-start | bytes 1572872 | tf_op jit(solution)/shard_map/ppermute | solution.py:88
  366.7 25.0 %collective-permute-start.61 = (bf16[128,2048]{1,0:T(8,128)(2,1)}, bf16[128,2048]{1,0:T(8,128)(2,1)}, u32[]{:S(2)}, u32[]{:S(2)}) collective-permute-start(bf16[128,2048]{1,0:T(8,128)(2,1)} %collective-permute-done.60), channel_id=1, source_target_pairs={{4,5},{5,4},{6,7},{7,6},{12,13},{13,12},{14,15},{15,14},{20,21},{2... | collective-permute-start | bytes 1572872 | tf_op jit(solution)/shard_map/ppermute | solution.py:88
  368.1 48.3 %collective-permute-start.62 = (bf16[128,2048]{1,0:T(8,128)(2,1)}, bf16[128,2048]{1,0:T(8,128)(2,1)}, u32[]{:S(2)}, u32[]{:S(2)}) collective-permute-start(bf16[128,2048]{1,0:T(8,128)(2,1)} %collective-permute-done.55), channel_id=1, source_target_pairs={{0,1},{1,0},{2,3},{3,2},{8,9},{9,8},{10,11},{11,10},{16,17},{17,16... | collective-permute-start | bytes 1572872 | tf_op jit(solution)/shard_map/ppermute | solution.py:88
  385.1 27.5 %collective-permute-start.56 = (bf16[128,2048]{1,0:T(8,128)(2,1)}, bf16[128,2048]{1,0:T(8,128)(2,1)S(1)}, u32[]{:S(2)}, u32[]{:S(2)}) collective-permute-start(bf16[128,2048]{1,0:T(8,128)(2,1)} %collective-permute-done.55), channel_id=1, source_target_pairs={{2,0},{3,1},{10,8},{11,9},{18,16},{19,17},{26,24},{27,25}} | collective-permute-start | bytes 1572872 | tf_op jit(solution)/shard_map/ppermute | solution.py:88
  386.6 30.6 %collective-permute-start.36 = (bf16[128,2048]{1,0:T(8,128)(2,1)}, bf16[128,2048]{1,0:T(8,128)(2,1)S(1)}, u32[]{:S(2)}, u32[]{:S(2)}) collective-permute-start(bf16[128,2048]{1,0:T(8,128)(2,1)} %collective-permute-done.35), channel_id=1, source_target_pairs={{2,0},{3,1},{10,8},{11,9},{18,16},{19,17},{26,24},{27,25}} | collective-permute-start | bytes 1572872 | tf_op jit(solution)/shard_map/ppermute | solution.py:88
  391.8 53.0 %collective-permute-start.53 = (bf16[128,2048]{1,0:T(8,128)(2,1)S(1)}, bf16[128,2048]{1,0:T(8,128)(2,1)S(1)}, u32[]{:S(2)}, u32[]{:S(2)}) collective-permute-start(bf16[128,2048]{1,0:T(8,128)(2,1)S(1)} %copy-done.63), channel_id=1, source_target_pairs={{2,3},{3,2},{4,5},{5,4},{6,7},{7,6},{10,11},{11,10},{12,13},{13,12... | collective-permute-start | bytes 1572872 | tf_op jit(solution)/shard_map/ppermute | solution.py:88
  412.6 32.4 %collective-permute-start.57 = (bf16[128,2048]{1,0:T(8,128)(2,1)S(1)}, bf16[128,2048]{1,0:T(8,128)(2,1)S(1)}, u32[]{:S(2)}, u32[]{:S(2)}) collective-permute-start(bf16[128,2048]{1,0:T(8,128)(2,1)S(1)} %collective-permute-done.56), channel_id=1, source_target_pairs={{0,1},{1,0},{8,9},{9,8},{16,17},{17,16},{24,25},{25,24}} | collective-permute-start | bytes 1572872 | tf_op jit(solution)/shard_map/ppermute | solution.py:88
  417.2 23.3 %collective-permute-start.37 = (bf16[128,2048]{1,0:T(8,128)(2,1)S(1)}, bf16[128,2048]{1,0:T(8,128)(2,1)S(1)}, u32[]{:S(2)}, u32[]{:S(2)}) collective-permute-start(bf16[128,2048]{1,0:T(8,128)(2,1)S(1)} %collective-permute-done.36), channel_id=1, source_target_pairs={{0,1},{1,0},{8,9},{9,8},{16,17},{17,16},{24,25},{25,24}} | collective-permute-start | bytes 1572872 | tf_op jit(solution)/shard_map/ppermute | solution.py:88
  425.8 26.9 %collective-permute-start.30 = (bf16[128,2048]{1,0:T(8,128)(2,1)S(1)}, bf16[128,2048]{1,0:T(8,128)(2,1)S(1)}, u32[]{:S(2)}, u32[]{:S(2)}) collective-permute-start(bf16[128,2048]{1,0:T(8,128)(2,1)S(1)} %copy-done.50), channel_id=1, source_target_pairs={{0,1},{1,0},{2,3},{3,2},{4,5},{5,4},{6,7},{7,6},{8,9},{9,8},{10,11... | collective-permute-start | bytes 1572872 | tf_op jit(solution)/shard_map/ppermute | solution.py:88
  444.8 29.4 %collective-permute-start.63 = (bf16[128,2048]{1,0:T(8,128)(2,1)S(1)}, bf16[128,2048]{1,0:T(8,128)(2,1)S(1)}, u32[]{:S(2)}, u32[]{:S(2)}) collective-permute-start(bf16[128,2048]{1,0:T(8,128)(2,1)S(1)} %slice.328), channel_id=1, source_target_pairs={{0,1},{1,0},{2,3},{3,2},{4,5},{5,4},{6,7},{7,6},{8,9},{9,8},{10,11... | collective-permute-start | bytes 1572872 | tf_op jit(solution)/shard_map/ppermute | solution.py:88
  450.8 34.7 %collective-permute-start.58 = (bf16[128,2048]{1,0:T(8,128)(2,1)S(1)}, bf16[128,2048]{1,0:T(8,128)(2,1)S(1)}, u32[]{:S(2)}, u32[]{:S(2)}) collective-permute-start(bf16[128,2048]{1,0:T(8,128)(2,1)S(1)} %slice.326), channel_id=1, source_target_pairs={{0,1},{1,0},{2,3},{3,2},{4,5},{5,4},{6,7},{7,6},{8,9},{9,8},{10,11... | collective-permute-start | bytes 1572872 | tf_op jit(solution)/shard_map/ppermute | solution.py:88
  462.3 33.8 %collective-permute-start.51 = (bf16[128,2048]{1,0:T(8,128)(2,1)S(1)}, bf16[128,2048]{1,0:T(8,128)(2,1)S(1)}, u32[]{:S(2)}, u32[]{:S(2)}) collective-permute-start(bf16[128,2048]{1,0:T(8,128)(2,1)S(1)} %slice.324), channel_id=1, source_target_pairs={{0,1},{1,0},{2,3},{3,2},{4,5},{5,4},{6,7},{7,6},{8,9},{9,8},{10,11... | collective-permute-start | bytes 1572872 | tf_op jit(solution)/shard_map/ppermute | solution.py:88
  463.4 32.7 %collective-permute-start.69 = (bf16[128,2048]{1,0:T(8,128)(2,1)S(1)}, bf16[128,2048]{1,0:T(8,128)(2,1)S(1)}, u32[]{:S(2)}, u32[]{:S(2)}) collective-permute-start(bf16[128,2048]{1,0:T(8,128)(2,1)S(1)} %add_convert_fusion.5), channel_id=1, source_target_pairs={{0,2},{1,3},{2,4},{3,5},{4,6},{5,7},{6,0},{7,1},{8,10},{9,11},{10,... | collective-permute-start | bytes 1572872 | tf_op jit(solution)/shard_map/ppermute | solution.py:88
  474.4 26.1 %collective-permute-start.64 = (bf16[128,2048]{1,0:T(8,128)(2,1)S(1)}, bf16[128,2048]{1,0:T(8,128)(2,1)S(1)}, u32[]{:S(2)}, u32[]{:S(2)}) collective-permute-start(bf16[128,2048]{1,0:T(8,128)(2,1)S(1)} %add_convert_fusion.6), channel_id=1, source_target_pairs={{0,4},{1,5},{2,6},{3,7},{4,0},{5,1},{6,2},{7,3},{8,12},{9,13},{10,... | collective-permute-start | bytes 1572872 | tf_op jit(solution)/shard_map/ppermute | solution.py:88
  485.6 24.0 %collective-permute-start.59 = (bf16[128,2048]{1,0:T(8,128)(2,1)S(1)}, bf16[128,2048]{1,0:T(8,128)(2,1)S(1)}, u32[]{:S(2)}, u32[]{:S(2)}) collective-permute-start(bf16[128,2048]{1,0:T(8,128)(2,1)S(1)} %add_convert_fusion.7), channel_id=1, source_target_pairs={{0,6},{1,7},{2,0},{3,1},{4,2},{5,3},{6,4},{7,5},{8,14},{9,15},{10,... | collective-permute-start | bytes 1572872 | tf_op jit(solution)/shard_map/ppermute | solution.py:88
  584.8 205.0 %reduce-scatter.5.cloned.1.call-start = ((), (), s32[]{:S(2)}) async-start(), calls=%async_computation.12 | async-start | bytes 3932160 | tf_op jit(solution)/shard_map/reduce_scatter | solution.py:190
  609.9 183.3 %reduce-scatter.11.cloned.1.call-start = ((), (), s32[]{:S(2)}) async-start(), calls=%async_computation.15 | async-start | bytes 5242880 | tf_op jit(solution)/shard_map/reduce_scatter | solution.py:190
  629.7 165.9 %reduce-scatter.9.cloned.1.call-start = ((), (), s32[]{:S(2)}) async-start(), calls=%async_computation.14 | async-start | bytes 10485760 | tf_op jit(solution)/shard_map/reduce_scatter | solution.py:190
  671.0 63.7 %collective-permute-start.48 = (bf16[128,2048]{1,0:T(8,128)(2,1)}, bf16[128,2048]{1,0:T(8,128)(2,1)}, u32[]{:S(2)}, u32[]{:S(2)}) collective-permute-start(bf16[128,2048]{1,0:T(8,128)(2,1)} %slice.322), channel_id=1, source_target_pairs={{0,1},{1,0},{2,3},{3,2},{4,5},{5,4},{6,7},{7,6},{8,9},{9,8},{10,11... | collective-permute-start | bytes 1572872 | tf_op jit(solution)/shard_map/ppermute | solution.py:88
  675.0 64.2 %collective-permute-start.43 = (bf16[128,2048]{1,0:T(8,128)(2,1)}, bf16[128,2048]{1,0:T(8,128)(2,1)}, u32[]{:S(2)}, u32[]{:S(2)}) collective-permute-start(bf16[128,2048]{1,0:T(8,128)(2,1)} %slice.318), channel_id=1, source_target_pairs={{0,1},{1,0},{2,3},{3,2},{4,5},{5,4},{6,7},{7,6},{8,9},{9,8},{10,11... | collective-permute-start | bytes 1572872 | tf_op jit(solution)/shard_map/ppermute | solution.py:88
  690.3 29.4 %collective-permute-start.86 = (bf16[128,2048]{1,0:T(8,128)(2,1)S(1)}, bf16[128,2048]{1,0:T(8,128)(2,1)S(1)}, u32[]{:S(2)}, u32[]{:S(2)}) collective-permute-start(bf16[128,2048]{1,0:T(8,128)(2,1)S(1)} %slice.343), channel_id=1, source_target_pairs={{0,1},{1,0},{2,3},{3,2},{4,5},{5,4},{6,7},{7,6},{8,9},{9,8},{10,11... | collective-permute-start | bytes 1572872 | tf_op jit(solution)/shard_map/ppermute | solution.py:88
  693.0 38.0 %collective-permute-start.88 = (bf16[128,2048]{1,0:T(8,128)(2,1)S(1)}, bf16[128,2048]{1,0:T(8,128)(2,1)S(1)}, u32[]{:S(2)}, u32[]{:S(2)}) collective-permute-start(bf16[128,2048]{1,0:T(8,128)(2,1)S(1)} %slice.346), channel_id=1, source_target_pairs={{0,1},{1,0},{2,3},{3,2},{4,5},{5,4},{6,7},{7,6},{8,9},{9,8},{10,11... | collective-permute-start | bytes 1572872 | tf_op jit(solution)/shard_map/ppermute | solution.py:88
  708.5 34.5 %collective-permute-start.83 = (bf16[128,2048]{1,0:T(8,128)(2,1)S(1)}, bf16[128,2048]{1,0:T(8,128)(2,1)S(1)}, u32[]{:S(2)}, u32[]{:S(2)}) collective-permute-start(bf16[128,2048]{1,0:T(8,128)(2,1)S(1)} %slice.337), channel_id=1, source_target_pairs={{0,1},{1,0},{2,3},{3,2},{4,5},{5,4},{6,7},{7,6},{8,9},{9,8},{10,11... | collective-permute-start | bytes 1572872 | tf_op jit(solution)/shard_map/ppermute | solution.py:88
  719.8 23.5 %collective-permute-start.85 = (bf16[128,2048]{1,0:T(8,128)(2,1)S(1)}, bf16[128,2048]{1,0:T(8,128)(2,1)S(1)}, u32[]{:S(2)}, u32[]{:S(2)}) collective-permute-start(bf16[128,2048]{1,0:T(8,128)(2,1)S(1)} %add_convert_fusion.2), channel_id=1, source_target_pairs={{0,6},{1,7},{2,0},{3,1},{4,2},{5,3},{6,4},{7,5},{8,14},{9,15},{10,... | collective-permute-start | bytes 1572872 | tf_op jit(solution)/shard_map/ppermute | solution.py:88
  731.0 55.6 %collective-permute-start.87 = (bf16[128,2048]{1,0:T(8,128)(2,1)S(1)}, bf16[128,2048]{1,0:T(8,128)(2,1)S(1)}, u32[]{:S(2)}, u32[]{:S(2)}) collective-permute-start(bf16[128,2048]{1,0:T(8,128)(2,1)S(1)} %add_convert_fusion.1), channel_id=1, source_target_pairs={{0,4},{1,5},{2,6},{3,7},{4,0},{5,1},{6,2},{7,3},{8,12},{9,13},{10,... | collective-permute-start | bytes 1572872 | tf_op jit(solution)/shard_map/ppermute | solution.py:88
  734.7 52.0 %collective-permute-start.89 = (bf16[128,2048]{1,0:T(8,128)(2,1)S(1)}, bf16[128,2048]{1,0:T(8,128)(2,1)S(1)}, u32[]{:S(2)}, u32[]{:S(2)}) collective-permute-start(bf16[128,2048]{1,0:T(8,128)(2,1)S(1)} %add_convert_fusion), channel_id=1, source_target_pairs={{0,2},{1,3},{2,4},{3,5},{4,6},{5,7},{6,0},{7,1},{8,10},{9,11},{10,... | collective-permute-start | bytes 1572872 | tf_op jit(solution)/shard_map/ppermute | solution.py:88
  739.2 61.2 %collective-permute-start.38 = (bf16[128,2048]{1,0:T(8,128)(2,1)}, bf16[128,2048]{1,0:T(8,128)(2,1)S(1)}, u32[]{:S(2)}, u32[]{:S(2)}) collective-permute-start(bf16[128,2048]{1,0:T(8,128)(2,1)} %slice.314), channel_id=1, source_target_pairs={{0,1},{1,0},{2,3},{3,2},{4,5},{5,4},{6,7},{7,6},{8,9},{9,8},{10,11... | collective-permute-start | bytes 1572872 | tf_op jit(solution)/shard_map/ppermute | solution.py:88
  743.0 97.8 %collective-permute-start.31 = (bf16[128,2048]{1,0:T(8,128)(2,1)}, bf16[128,2048]{1,0:T(8,128)(2,1)}, u32[]{:S(2)}, u32[]{:S(2)}) collective-permute-start(bf16[128,2048]{1,0:T(8,128)(2,1)} %slice.310), channel_id=1, source_target_pairs={{0,1},{1,0},{2,3},{3,2},{4,5},{5,4},{6,7},{7,6},{8,9},{9,8},{10,11... | collective-permute-start | bytes 1572872 | tf_op jit(solution)/shard_map/ppermute | solution.py:88
  743.2 97.6 %collective-permute-start.49 = (bf16[128,2048]{1,0:T(8,128)(2,1)}, bf16[128,2048]{1,0:T(8,128)(2,1)}, u32[]{:S(2)}, u32[]{:S(2)}) collective-permute-start(bf16[128,2048]{1,0:T(8,128)(2,1)} %add_convert_fusion.8), channel_id=1, source_target_pairs={{0,2},{1,3},{2,4},{3,5},{4,6},{5,7},{6,0},{7,1},{8,10},{9,11},{10,... | collective-permute-start | bytes 1572872 | tf_op jit(solution)/shard_map/ppermute | solution.py:88
  786.6 54.2 %collective-permute-start.44 = (bf16[128,2048]{1,0:T(8,128)(2,1)}, bf16[128,2048]{1,0:T(8,128)(2,1)}, u32[]{:S(2)}, u32[]{:S(2)}) collective-permute-start(bf16[128,2048]{1,0:T(8,128)(2,1)} %add_convert_fusion.9), channel_id=1, source_target_pairs={{0,4},{1,5},{2,6},{3,7},{4,0},{5,1},{6,2},{7,3},{8,12},{9,13},{10,... | collective-permute-start | bytes 1572872 | tf_op jit(solution)/shard_map/ppermute | solution.py:88
  802.4 38.5 %collective-permute-start.39 = (bf16[128,2048]{1,0:T(8,128)(2,1)}, bf16[128,2048]{1,0:T(8,128)(2,1)}, u32[]{:S(2)}, u32[]{:S(2)}) collective-permute-start(bf16[128,2048]{1,0:T(8,128)(2,1)} %add_convert_fusion.10), channel_id=1, source_target_pairs={{0,6},{1,7},{2,0},{3,1},{4,2},{5,3},{6,4},{7,5},{8,14},{9,15},{10,... | collective-permute-start | bytes 1572872 | tf_op jit(solution)/shard_map/ppermute | solution.py:88
  802.4 47.1 %all-to-all-start.2 = ((bf16[8,64,768]{2,1,0:T(8,128)(2,1)}), bf16[8,64,768]{2,1,0:T(8,128)(2,1)S(1)}, u32[]{:S(2)}, u32[]{:S(2)}) async-start(bf16[8,64,768]{2,1,0:T(8,128)(2,1)} %bitcast.192), calls=%async_computation.6 | async-start | bytes 1572864 | tf_op jit(solution)/shard_map/all_to_all | solution.py:182
  849.5 51.2 %all-to-all-start.3 = ((bf16[8,64,2048]{2,1,0:T(8,128)(2,1)}), bf16[8,64,2048]{2,1,0:T(8,128)(2,1)S(1)}, u32[]{:S(2)}, u32[]{:S(2)}) async-start(bf16[8,64,2048]{2,1,0:T(8,128)(2,1)} %bitcast.186), calls=%async_computation.7 | async-start | bytes 4194304 | tf_op jit(solution)/shard_map/all_to_all | solution.py:182
  (182 other events, 2040.7 us)
Sparse Core Ops, SparseCore 0:
  10.2 28.3 all-gather.6
  49.6 26.6 all-gather.4
  108.0 56.6 all-gather.8
  166.7 34.5 all-gather.10
  584.9 26.4 reduce-scatter.6
  614.0 37.9 reduce-scatter.4
  655.1 44.4 reduce-scatter.10
  702.4 71.6 reduce-scatter.8

commit v2 on v0

--- a/solution.py
+++ b/solution.py
@@ -3,6 +3,8 @@
 import jax
 import jax.numpy as jnp
 from jax import lax
+from jax.experimental import pallas as pl
+from jax.experimental.pallas import tpu as pltpu
 from jax.sharding import PartitionSpec as P
 
 HEADS = 16
@@ -18,6 +20,7 @@
 DECAY = 0.1
 ADAM_EPSILON = 1e-08
 CLIP = 1.0
+BOTH = ("dp", "seq")
 
 
 def angles(positions, width):
@@ -55,6 +58,491 @@
 def contract_last(left, right):
     return lax.dot_general(
         left, right, (((1,), (1,)), ((), ())), preferred_element_type=jnp.float32
+    )
+
+
+def multiply(left, right):
+    return jnp.dot(left, right, preferred_element_type=jnp.float32)
+
+
+def adamw(weight, grad, first, second, factor, decay, rate):
+    grad = grad * factor
+    first = BETA_ONE * first + (1.0 - BETA_ONE) * grad
+    second = BETA_TWO * second + (1.0 - BETA_TWO) * grad * grad
+    update = (
+        first / (1.0 - BETA_ONE**STEP) / (jnp.sqrt(second / (1.0 - BETA_TWO**STEP)) + ADAM_EPSILON)
+    )
+    return (first, second, weight - rate * (update + decay * weight))
+
+
+def move(value, where):
+    pairs = []
+    for dp in range(lax.axis_size("dp")):
+        for seq in range(lax.axis_size("seq")):
+            target = where(dp, seq // 2, seq % 2)
+            if target is not None:
+                pairs.append(
+                    (
+                        dp * lax.axis_size("seq") + seq,
+                        target[0] * lax.axis_size("seq") + target[1] * 2 + target[2],
+                    )
+                )
+    return lax.ppermute(value, BOTH, pairs)
+
+
+FAR_FIRST = [2, 3, 1, 0]
+DEPTH = 4
+
+
+def across(value):
+    return move(value, lambda dp, z, x: (dp, z, 1 - x))
+
+
+def turn(value, k):
+    return move(value, lambda dp, z, x: (dp, z ^ k, x))
+
+
+def line(value, hop, direction):
+    def where(dp, z, x):
+        if direction > 0:
+            return (dp, z + 1, x) if z >= hop - 1 and z + 1 < DEPTH else None
+        return (dp, z - 1, x) if z <= DEPTH - hop and z >= 1 else None
+
+    return move(value, where)
+
+
+def gather_rows(block, holds=()):
+    z = lax.axis_index("seq") // 2
+    up, down = [block], [block]
+    for hop in range(1, DEPTH):
+        held = holds[hop - 2 : hop - 1] if hop >= 2 else ()
+        up.append(line(after(up[-1], *held), hop, 1))
+        down.append(line(after(down[-1], *held), hop, -1))
+    column = [
+        block,
+        jnp.where(z % 2 == 0, down[1], up[1]),
+        jnp.where(z < 2, down[2], up[2]),
+        jnp.where(z < 2, jnp.where(z == 0, down[3], down[1]), jnp.where(z == 3, up[3], up[1])),
+    ]
+    return [jnp.concatenate([piece, across(piece)], axis=0) for piece in column]
+
+
+def nothing(*others):
+    firsts = [lax.slice(other, (0,) * other.ndim, (1,) * other.ndim) for other in others]
+    return sum(first.reshape(()).astype(jnp.float32) for first in firsts) * 0.0
+
+
+def after(value, *others):
+    return value + nothing(*others).astype(value.dtype) if others else value
+
+
+def pairs_of():
+    return [(k, j) for k in range(DEPTH) for j in range(2)]
+
+
+def sources_of():
+    z, x = lax.axis_index("seq") // 2, lax.axis_index("seq") % 2
+    return [(z ^ k) * 2 + (x ^ j) for k, j in pairs_of()]
+
+
+def exchange(blocks):
+    return lax.all_to_all(blocks, "seq", 0, 0, tiled=True)
+
+
+def exchange_small(blocks):
+    return [
+        move(block, lambda dp, z, x: (dp, z ^ k, x ^ j)) if (k, j) != (0, 0) else block
+        for (k, j), block in zip(pairs_of(), blocks, strict=True)
+    ]
+
+
+def by_place(columns, n_seq):
+    rows, groups, _, size = columns.shape
+    return columns.transpose(2, 0, 1, 3).reshape(n_seq, rows, -1)
+
+
+def copy_block(order, source, target):
+    target[...] = source[...]
+
+
+def pick(blocks, order):
+    count, rows, columns = blocks.shape
+    block = (1, rows, columns)
+    return pl.pallas_call(
+        copy_block,
+        grid_spec=pltpu.PrefetchScalarGridSpec(
+            num_scalar_prefetch=1,
+            grid=(count,),
+            in_specs=[pl.BlockSpec(block, lambda i, order: (order[i], 0, 0))],
+            out_specs=pl.BlockSpec(block, lambda i, order: (i, 0, 0)),
+        ),
+        out_shape=jax.ShapeDtypeStruct(blocks.shape, blocks.dtype),
+        compiler_params=pltpu.CompilerParams(vmem_limit_bytes=32 * 1024 * 1024),
+        cost_estimate=pl.CostEstimate(flops=0, bytes_accessed=4 * blocks.size, transcendentals=0),
+    )(order.astype(jnp.int32), blocks)
+
+
+def in_place(received):
+    return pick(jnp.stack(received), jnp.stack(sources_of()))
+
+
+def side_by_side(received):
+    count, (rows, columns) = len(received), received[0].shape
+    return pl.pallas_call(
+        copy_block,
+        grid_spec=pltpu.PrefetchScalarGridSpec(
+            num_scalar_prefetch=1,
+            grid=(count,),
+            in_specs=[pl.BlockSpec((None, rows, columns), lambda i, order: (order[i], 0, 0))],
+            out_specs=pl.BlockSpec((rows, columns), lambda i, order: (0, i)),
+        ),
+        out_shape=jax.ShapeDtypeStruct((rows, count * columns), received[0].dtype),
+        compiler_params=pltpu.CompilerParams(vmem_limit_bytes=32 * 1024 * 1024),
+        cost_estimate=pl.CostEstimate(
+            flops=0, bytes_accessed=4 * count * rows * columns, transcendentals=0
+        ),
+    )(jnp.stack(sources_of()).astype(jnp.int32), jnp.stack(received))
+
+
+def scatter_rows(partial, order):
+    sums, came = {}, []
+    for n, k in enumerate(order):
+        term = partial(k, came[n - 2 : n - 1] if n >= 2 else [])
+        rows = term.shape[0] // 2
+        came.append(across(term[rows:]))
+        total = term[:rows].astype(jnp.float32) + came[-1].astype(jnp.float32)
+        sums[k] = turn(total.astype(jnp.bfloat16), k).astype(jnp.float32) if k else total
+    return sum(sums[k] for k in range(DEPTH)), came
+
+
+def sum_everywhere(value):
+    def of_four(where):
+        others = [move(value, lambda dp, z, x: where(dp, z, x, mask)) for mask in (1, 2, 3)]
+        return (value + others[0]) + (others[1] + others[2])
+
+    value = of_four(lambda dp, z, x, mask: (dp ^ mask, z, x))
+    value = of_four(lambda dp, z, x, mask: (dp, z ^ mask, x))
+    return value + across(value)
+
+
+def other_core(value):
+    return move(value, lambda dp, z, x: (dp ^ 1, z, x))
+
+
+def other_y(value):
+    return move(value, lambda dp, z, x: (dp ^ 2, z, x))
+
+
+def share(rows):
+    return lax.all_gather(rows, "dp", axis=0, tiled=True)
+
+
+def share_by_hand(rows):
+    dp = lax.axis_index("dp")
+    pair = jnp.stack([rows, other_y(rows)])
+    other = other_core(pair)
+    masks = [at ^ dp for at in range(4)]
+    order = jnp.stack([(mask % 2) * 2 + mask // 2 for mask in masks])
+    whole = pick(jnp.concatenate([pair, other]), order)
+    return whole.reshape(-1, *rows.shape[1:]), pair[1]
+
+
+def share_small(value):
+    dp = lax.axis_index("dp")
+    whole = jnp.zeros((4, *value.shape), value.dtype)
+    for mask in range(4):
+        piece = move(value, lambda dp, z, x: (dp ^ mask, z, x)) if mask else value
+        whole = lax.dynamic_update_index_in_dim(whole, piece, dp ^ mask, 0)
+    return whole
+
+
+def reduce_over(rows):
+    return lax.psum_scatter(rows, "dp", scatter_dimension=0, tiled=True)
+
+
+def take(array, index, axis):
+    return lax.dynamic_index_in_dim(array, index, axis, keepdims=False)
+
+
+def add_low(left, right, *holds):
+    total = left.astype(jnp.float32) + right.astype(jnp.float32)
+    return after(total, *holds).astype(jnp.bfloat16)
+
+
+def reduce_by_hand(rows, *holds):
+    dp = lax.axis_index("dp")
+    y, core = dp // 2, dp % 2
+    parts = rows.reshape(2, 2, -1, *rows.shape[1:])
+    parts = add_low(take(parts, core, 1), other_core(take(parts, 1 - core, 1)))
+    return add_low(take(parts, y, 0), other_y(take(parts, 1 - y, 0)), *holds)
+
+
+def reduce_along_seq(rows, holds, last_holds):
+    z, x = lax.axis_index("seq") // 2, lax.axis_index("seq") % 2
+    parts = rows.reshape(DEPTH, 2, -1, *rows.shape[1:])
+    parts = add_low(take(parts, x, 1), across(take(parts, 1 - x, 1)), *holds)
+    total = after(take(parts, z, 0).astype(jnp.float32), *last_holds)
+    for k in range(1, DEPTH):
+        total = total + turn(take(parts, z ^ k, 0), k).astype(jnp.float32)
+    return total
+
+
+def body(
+    tokens,
+    cotangent,
+    inner_weight,
+    outer_weight,
+    expand_weight,
+    shrink_weight,
+    norm_gains,
+    first_inner,
+    first_outer,
+    first_expand,
+    first_shrink,
+    first_gains,
+    second_inner,
+    second_outer,
+    second_expand,
+    second_shrink,
+    second_gains,
+    document_index,
+    group_order,
+):
+    bf16, f32 = jnp.bfloat16, jnp.float32
+    rows, width = tokens.shape[1:]
+    n_dp, n_seq = lax.axis_size("dp"), lax.axis_size("seq")
+    head = width // HEADS
+    own_heads = HEADS // n_seq
+    own_width = own_heads * head
+    owned = inner_weight.shape[0]
+    length = rows * n_seq
+    scale = head ** (-0.5)
+    offset = -math.log(length)
+    group = rows // 2
+    hidden = expand_weight.shape[1] // 2
+    share_hidden = hidden // n_seq
+    slab = shrink_weight.shape[0]
+    device = lax.axis_index(BOTH)
+    sources = sources_of()
+
+    inputs_low = tokens[0]
+    upstream = cotangent[0]
+
+    with jax.named_scope("inner"):
+        gain_parts = share_small(norm_gains.astype(bf16).reshape(-1))
+        small = jnp.concatenate([gain_parts.reshape(-1), document_index[0].astype(bf16)])
+        small = jnp.pad(small[None], ((0, 15), (0, 3 * own_width - small.size)))
+        inner_low = by_place(inner_weight.astype(bf16).reshape(owned, 3, n_seq, own_width), n_seq)
+        small = jnp.broadcast_to(small, (n_seq, *small.shape))
+        inner_blocks = exchange(jnp.concatenate([inner_low, small], axis=1))
+        inner, inner_first = share_by_hand(inner_blocks[:, :owned].reshape(n_seq * owned, -1))
+        small = inner_blocks[:, owned]
+        gains = small[:, : gain_parts.size].reshape(n_seq, n_dp, 2, -1).astype(f32)
+        gains = gains.transpose(2, 1, 0, 3).reshape(2, width)
+        documents = small[:, gain_parts.size : gain_parts.size + rows]
+        documents = jnp.concatenate([take(documents, s, 0) for s in sources]).astype(f32)
+    with jax.named_scope("shrink"):
+        shrink = share(shrink_weight.astype(bf16))
+    gain_one, gain_two = gains[0], gains[1]
+
+    groups = jnp.concatenate([lax.dynamic_slice_in_dim(group_order, 2 * s, 2) for s in sources])
+    within = jnp.arange(group, dtype=jnp.int32)
+    places = (groups[:, None] * group + within[None, :]).reshape(-1)
+    cosine, sine = (part[:, 0] for part in angles(places, head))
+    cosine, sine = jnp.concatenate([cosine] * 2, axis=1), jnp.concatenate([-sine, sine], axis=1)
+
+    def turned(values, sign):
+        half = head // 2
+        swapped = jnp.concatenate([values[:, half:], values[:, :half]], axis=1)
+        return values * cosine + swapped * (sine * sign)
+
+    def head_of(array, part, h):
+        start = (part * own_heads + h) * head
+        return array[:, start : start + head]
+
+    def first_norm(piece):
+        values = piece.astype(f32)
+        inverse = lax.rsqrt(jnp.mean(values * values, axis=-1, keepdims=True) + EPSILON)
+        return values * inverse, inverse
+
+    with jax.named_scope("tokens"):
+        block = jnp.concatenate([inputs_low, outer_weight.astype(bf16)], axis=0)
+        pieces = gather_rows(block, [inner_blocks, inner_first])
+        pieces = [piece.reshape(2, rows + owned, width) for piece in pieces]
+        token_pieces = [piece[:, :rows].reshape(2 * rows, width) for piece in pieces]
+    with jax.named_scope("outer"):
+        outer = [piece[j, rows:] for piece in pieces for j in range(2)]
+        outer[0] = after(outer[0], shrink)
+        outer = share(in_place(outer).reshape(n_seq * owned, width))
+    with jax.named_scope("expand"):
+        expand_low = after(expand_weight, *token_pieces[1:]).astype(bf16)
+        expand_low = expand_low.reshape(owned, 2 * n_dp, n_seq, slab)
+        expand_blocks = exchange(by_place(expand_low, n_seq))
+    with jax.named_scope("attend"):
+        attend_pieces = [(first_norm(piece)[0] * gain_one).astype(bf16) for piece in token_pieces]
+        projected = jnp.concatenate([multiply(piece, inner) for piece in attend_pieces], axis=0)
+        visible = (documents[:, None] == documents[None, :]) & (places[None, :] <= places[:, None])
+        visible = visible.astype(f32)
+        query_rot, key_rot, value_low, weights, attended = [], [], [], [], []
+        for h in range(own_heads):
+            query_rot.append(turned(head_of(projected, 0, h), 1.0).astype(bf16))
+            key_rot.append(turned(head_of(projected, 1, h), 1.0).astype(bf16))
+            value_low.append(head_of(projected, 2, h).astype(bf16))
+            scores = contract_last(query_rot[h], key_rot[h]) * scale + offset
+            weights.append(jax.nn.sigmoid(scores) * visible)
+            attended.append(multiply(weights[h].astype(bf16), value_low[h]).astype(bf16))
+        attended = jnp.concatenate(attended, axis=1).reshape(n_seq, rows, own_width)
+
+    with jax.named_scope("rows"):
+        attended_rows = side_by_side(exchange_small(list(attended)))
+    with jax.named_scope("expand"):
+        expand_blocks = after(expand_blocks, attended_rows, outer)
+        expand = share(expand_blocks.reshape(n_seq * owned, -1))
+    inputs = inputs_low.astype(f32)
+    residual = inputs + multiply(attended_rows, outer)
+    inverse_second = lax.rsqrt(jnp.mean(residual * residual, axis=-1, keepdims=True) + EPSILON)
+    normed_second = residual * inverse_second
+
+    with jax.named_scope("mlp_input"):
+        mlp_pieces = gather_rows((normed_second * gain_two).astype(bf16))
+    with jax.named_scope("gate_up"):
+        gate_ups = [multiply(piece, expand) for piece in mlp_pieces]
+    with jax.named_scope("cotangent"):
+        upstream_pieces = gather_rows(after(upstream, *mlp_pieces[1:]))
+    activations, gate_up_grads = [None] * DEPTH, [None] * DEPTH
+
+    def feed_back(k, earlier):
+        gate, upward = gate_ups[k][:, :share_hidden], gate_ups[k][:, share_hidden:]
+        gate = after(gate, *earlier)
+        squash = jax.nn.sigmoid(gate)
+        activations[k] = (gate * squash * upward).astype(bf16)
+        down_grad = contract_last(upstream_pieces[k], shrink)
+        d_gate = down_grad * upward * squash * (1.0 + gate * (1.0 - squash))
+        d_upward = down_grad * gate * squash
+        gate_up_grads[k] = jnp.concatenate([d_gate, d_upward], axis=1).astype(bf16)
+        return contract_last(gate_up_grads[k], expand).astype(bf16)
+
+    with jax.named_scope("d_mlp_input"):
+        d_mlp_input, came = scatter_rows(feed_back, [0, 2, 1, 3])
+    with jax.named_scope("grad_expand"):
+        grad_expand = contract_rows(
+            jnp.concatenate(mlp_pieces, axis=0), jnp.concatenate(gate_up_grads, axis=0)
+        )
+        grad_expand = after(grad_expand, *came[3:4]).astype(bf16)
+    with jax.named_scope("grad_shrink"):
+        grad_shrink = contract_rows(
+            jnp.concatenate(activations, axis=0), jnp.concatenate(upstream_pieces, axis=0)
+        )
+        grad_shrink = after(grad_shrink, *came[3:4]).astype(bf16)
+    d_mlp_input = after(d_mlp_input, grad_expand, grad_shrink)
+    with jax.named_scope("grad_expand"):
+        grad_expand = reduce_over(grad_expand)
+    with jax.named_scope("grad_shrink"):
+        grad_shrink = reduce_over(grad_shrink).astype(f32)
+    partial_gain_two = jnp.sum(d_mlp_input * normed_second, axis=0)
+    d_residual = upstream.astype(f32) + norm_back(
+        d_mlp_input * gain_two, normed_second, inverse_second
+    )
+
+    with jax.named_scope("heads"):
+        d_residual_low = d_residual.astype(bf16)
+        d_attended = contract_last(d_residual_low, outer).astype(bf16)
+        d_attended = by_place(d_attended.reshape(rows, 1, n_seq, own_width), n_seq)
+        d_attended = exchange_small([take(d_attended, s, 0) for s in sources])
+        d_attended = jnp.concatenate(d_attended)
+    with jax.named_scope("attend_back"):
+        d_query, d_key, d_value = [], [], []
+        for h in range(own_heads):
+            d_out = head_of(d_attended, 0, h)
+            d_weights = contract_last(d_out, value_low[h])
+            d_scores = (d_weights * weights[h] * (1.0 - weights[h])).astype(bf16)
+            d_query.append(turned(multiply(d_scores, key_rot[h]) * scale, -1.0))
+            d_key.append(turned(contract_rows(d_scores, query_rot[h]) * scale, -1.0))
+            d_value.append(contract_rows(weights[h].astype(bf16), d_out))
+        d_projected = jnp.concatenate(
+            [part.astype(bf16) for part in d_query + d_key + d_value], axis=1
+        )
+    with jax.named_scope("feed"):
+        feed = multiply(jnp.concatenate(activations, axis=0), shrink)
+        feed = after(feed, d_attended).astype(bf16).reshape(DEPTH, 2, rows, width)
+        feed = add_low(feed[:, 0], across(feed[:, 1]), d_projected)
+        output = residual + feed[0].astype(f32)
+        for k in range(1, DEPTH):
+            output = output + turn(feed[k], k).astype(f32)
+    gain_terms = [None] * DEPTH
+
+    def attend_back(k, earlier):
+        term = contract_last(d_projected[2 * rows * k : 2 * rows * (k + 1)], inner)
+        if k == FAR_FIRST[0]:
+            term = after(term, feed)
+        gain_terms[k] = jnp.sum(term * first_norm(token_pieces[k])[0], axis=0)
+        return term.astype(bf16)
+
+    with jax.named_scope("d_attend_input"):
+        d_attend_input, came_last = scatter_rows(attend_back, FAR_FIRST)
+    partial_gain_one = sum(gain_terms)
+    normed_first, inverse_first = first_norm(inputs_low)
+    input_gradient = d_residual + norm_back(d_attend_input * gain_one, normed_first, inverse_first)
+
+    with jax.named_scope("own_expand"):
+        own_expand = exchange(grad_expand.reshape(n_seq, owned, -1))
+    with jax.named_scope("grad_outer"):
+        grad_outer = contract_rows(attended_rows, d_residual_low).astype(bf16)
+        grad_outer = reduce_by_hand(grad_outer, came_last[-1])
+        grad_outer = reduce_along_seq(grad_outer, [d_attend_input], [own_expand])
+    grad_inner = contract_rows(jnp.concatenate(attend_pieces, axis=0), d_projected)
+    with jax.named_scope("grad_inner"):
+        grad_inner = reduce_by_hand(grad_inner.astype(bf16), came_last[-1])
+
+    local_squares = sum(
+        jnp.sum(jnp.square(grad.astype(f32)))
+        for grad in (grad_inner, grad_outer, grad_expand, grad_shrink)
+    )
+    with jax.named_scope("sums"):
+        sums = sum_everywhere(
+            jnp.concatenate(
+                [partial_gain_one, partial_gain_two, jnp.full((128,), local_squares)]
+            ).reshape(-1, 128)
+        ).reshape(-1)
+    gains_whole = sums[: 2 * width].reshape(2, width)
+    grad_gains = lax.dynamic_slice_in_dim(
+        gains_whole, device * norm_gains.shape[1], norm_gains.shape[1], 1
+    )
+    global_norm = jnp.sqrt(sums[2 * width] + jnp.sum(gains_whole * gains_whole))
+    factor = CLIP / jnp.maximum(global_norm, CLIP)
+
+    with jax.named_scope("own_inner"):
+        grad_inner = exchange(grad_inner.reshape(n_seq, owned, -1))
+    grad_inner = grad_inner.reshape(n_seq, owned, 3, own_width)
+    grad_inner = grad_inner.transpose(1, 2, 0, 3).reshape(inner_weight.shape)
+    grad_expand = own_expand.reshape(n_seq, owned, 2 * n_dp, slab)
+    grad_expand = grad_expand.transpose(1, 2, 0, 3).reshape(expand_weight.shape)
+
+    gradients = (grad_inner, grad_outer, grad_expand, grad_shrink, grad_gains)
+    masters = (inner_weight, outer_weight, expand_weight, shrink_weight, norm_gains)
+    firsts = (first_inner, first_outer, first_expand, first_shrink, first_gains)
+    seconds = (second_inner, second_outer, second_expand, second_shrink, second_gains)
+    decays = (DECAY, DECAY, DECAY, DECAY, 0.0)
+    rates = (RATE, RATE, RATE, RATE, GAIN_RATE)
+    results = [
+        adamw(
+            masters[index],
+            gradients[index].astype(f32),
+            firsts[index],
+            seconds[index],
+            factor,
+            decays[index],
+            rates[index],
+        )
+        for index in range(5)
+    ]
+    return (
+        output[None],
+        input_gradient[None],
+        global_norm,
+        *(result[0] for result in results),
+        *(result[1] for result in results),
+        *(result[2] for result in results),
     )
 
 
@@ -130,17 +618,7 @@
     )
 
 
-def adamw(weight, grad, first, second, factor, decay, rate):
-    grad = grad * factor
-    first = BETA_ONE * first + (1.0 - BETA_ONE) * grad
-    second = BETA_TWO * second + (1.0 - BETA_TWO) * grad * grad
-    update = (
-        first / (1.0 - BETA_ONE**STEP) / (jnp.sqrt(second / (1.0 - BETA_TWO**STEP)) + ADAM_EPSILON)
-    )
-    return (first, second, weight - rate * (update + decay * weight))
-
-
-def body(
+def gathered_body(
     tokens,
     cotangent,
     inner_weight,
@@ -355,6 +833,7 @@
 
 
 def solution(mesh):
+    whole_heads = mesh.shape["seq"] == 2 * DEPTH and mesh.shape["dp"] == 4
     placed = (
         P("dp", "seq", None),
         P("dp", "seq", None),
@@ -377,7 +856,7 @@
         P(),
     )
     return jax.shard_map(
-        body,
+        body if whole_heads else gathered_body,
         mesh=mesh,
         in_specs=placed,
         out_specs=(

time: 6310 us -> 843 us (0.13)
  waiting for transfers between devices: 5820 us -> 319 us
  matrix products: 278 us -> 109 us
  starting transfers between devices: 0.88 us -> 168 us
  blocking collectives: 102 us -> 0 us
    unnamed x15 -> x5, waiting for transfers between devices: 2930 us -> 0.08 us
    reduce_scatter x3 -> x2, waiting for transfers between devices: 2060 us -> 0.01 us  [reduce_over(): return lax.psum_scatter(rows, 'dp', scatter_dimension=0, tiled=True)]
    all_gather x6 -> x3, waiting for transfers between devices: 821 us -> 0.01 us  [share(): return lax.all_gather(rows, 'dp', axis=0, tiled=True)]
    ppermute x0 -> x82, waiting for transfers between devices: none -> 302 us  [move(): return lax.ppermute(value, BOTH, pairs)]
    ppermute x0 -> x82, starting transfers between devices: none -> 146 us  [move(): return lax.ppermute(value, BOTH, pairs)]
    dot_general x4 -> x8, matrix products: 102 us -> 32.4 us  [contract_rows(): lax.dot_general(left, right, (((0,), (0,)), ((), ())), preferred_element_...]
    dot_general x10 -> x14, matrix products: 95.9 us -> 32.2 us  [multiply(): return jnp.dot(left, right, preferred_element_type=jnp.float32)]
  transfers between devices with their start and end apart: 12 -> 91, of which waited for: 12 -> 38; matrix products, arithmetic and copies ran while one was open for 4% -> 27% of each run, Pallas kernels for 0% -> 0%
where the time goes in v2:
time: 843 us; the launch traced here: 833 us
  waiting for transfers between devices  319 us (38%)
  starting transfers between devices  168 us (20%)
  matrix products  109 us (13%)
  other arithmetic  107 us (13%)
  local copies, waits for them, and re-layouts  88.2 us (10%)
  between operations  36.2 us (4%)
    ppermute x82, waiting for transfers between devices, move(): return lax.ppermute(value, BOTH, pairs)  302 us
    ppermute x82, starting transfers between devices, move(): return lax.ppermute(value, BOTH, pairs)  146 us
    dot_general x17, matrix products, contract_last(): lax.dot_general(left, right, (((1,), (1,)), ((), ())), preferred_element_...  44.2 us
    unnamed x329, local copies, waits for them, and re-layouts  36.8 us
    dot_general x8, matrix products, contract_rows(): lax.dot_general(left, right, (((0,), (0,)), ((), ())), preferred_element_...  32.4 us
    dot_general x14, matrix products, multiply(): return jnp.dot(left, right, preferred_element_type=jnp.float32)  32.2 us
    all_to_all x4, starting transfers between devices, exchange(): return lax.all_to_all(blocks, 'seq', 0, 0, tiled=True)  21.7 us
    sub x5, other arithmetic, adamw(): return (first, second, weight - rate * (update + decay * weight))  18.5 us
  transfers between devices with their start and end apart: 91, of which 38 were waited for; matrix products, arithmetic and copies ran while one was open for 27% of the time, Pallas kernels for 0%

profile of v2, /device:TPU:0, one launch (start us, length us, event | category | flops | bytes accessed | tf_op | source)
XLA Modules:
  0.0 832.5 jit_solution(12157262398125127006)
XLA Ops:
  16.1 6.0 all-to-all-start
  24.4 4.0 collective-permute-start.7
  31.5 16.6 %all-to-all-done = bf16[8,80,768]{2,1,0:T(8,128)(2,1)} async-done(((bf16[8,80,768]{2,1,0:T(8,128)(2,1)}), bf16[8,80,768]{2,1,0:T(8,128)(2,1)}, u32[]{:S(2)}, u32[]{:S(2)}) %all-to-all-start) | async-done | bytes 983072 | tf_op jit(solution)/shard_map/inner/all_to_all | solution.py:149
  49.9 6.5 collective-permute-done.7
  67.4 14.1 %collective-permute-done.4 = bf16[512,768]{1,0:T(8,128)(2,1)S(1)} collective-permute-done((bf16[512,768]{1,0:T(8,128)(2,1)S(1)}, bf16[512,768]{1,0:T(8,128)(2,1)S(1)}, u32[]{:S(2)}, u32[]{:S(2)}) %collective-permute-start.4) | collective-permute-done | bytes 786464 | tf_op jit(solution)/shard_map/inner/ppermute | solution.py:90
  82.8 7.2 collective-permute-done.9
  99.1 15.1 %collective-permute-done.12 = bf16[192,2048]{1,0:T(8,128)(2,1)S(1)} collective-permute-done((bf16[192,2048]{1,0:T(8,128)(2,1)S(1)}, bf16[192,2048]{1,0:T(8,128)(2,1)S(1)}, u32[]{:S(2)}, u32[]{:S(2)}) %collective-permute-start.12) | collective-permute-done | bytes 786464 | tf_op jit(solution)/shard_map/tokens/ppermute | solution.py:90
  122.1 14.2 %collective-permute-done.8 = bf16[192,2048]{1,0:T(8,128)(2,1)} collective-permute-done((bf16[192,2048]{1,0:T(8,128)(2,1)}, bf16[192,2048]{1,0:T(8,128)(2,1)}, u32[]{:S(2)}, u32[]{:S(2)}) %collective-permute-start.8) | collective-permute-done | bytes 786464 | tf_op jit(solution)/shard_map/tokens/ppermute | solution.py:90
  139.0 11.6 %collective-permute-done.14 = bf16[192,2048]{1,0:T(8,128)(2,1)} collective-permute-done((bf16[192,2048]{1,0:T(8,128)(2,1)}, bf16[192,2048]{1,0:T(8,128)(2,1)}, u32[]{:S(2)}, u32[]{:S(2)}) %collective-permute-start.14) | collective-permute-done | bytes 786464 | tf_op jit(solution)/shard_map/tokens/ppermute | solution.py:90
  176.0 4.3 reshape.687
  180.3 7.5 all-to-all-start.1
  218.1 5.1 collective-permute-start.20
  229.0 15.4 %collective-permute-done.18 = bf16[128,256]{1,0:T(8,128)(2,1)S(1)} collective-permute-done((bf16[128,256]{1,0:T(8,128)(2,1)S(1)}, bf16[128,256]{1,0:T(8,128)(2,1)S(1)}, u32[]{:S(2)}, u32[]{:S(2)}) %collective-permute-start.18) | collective-permute-done | bytes 65568 | tf_op jit(solution)/shard_map/rows/ppermute | solution.py:90
  253.4 4.8 multiply_reduce_fusion.9
  260.6 4.6 collective-permute-start.24
  265.2 4.8 collective-permute-done.22
  278.6 7.6 collective-permute-done.25
  286.3 4.2 collective-permute-done.26
  296.2 5.2 collective-permute-done.32
  308.4 4.6 collective-permute-start.36
  324.2 10.8 %collective-permute-done.40 = bf16[128,2048]{1,0:T(8,128)(2,1)S(1)} collective-permute-done((bf16[128,2048]{1,0:T(8,128)(2,1)S(1)}, bf16[128,2048]{1,0:T(8,128)(2,1)S(1)}, u32[]{:S(2)}, u32[]{:S(2)}) %collective-permute-start.40) | collective-permute-done | bytes 524320 | tf_op jit(solution)/shard_map/cotangent/ppermute | solution.py:90
  339.0 9.4 %collective-permute-start.45 = (bf16[128,2048]{1,0:T(8,128)(2,1)S(1)}, bf16[128,2048]{1,0:T(8,128)(2,1)S(1)}, u32[]{:S(2)}, u32[]{:S(2)}) collective-permute-start(bf16[128,2048]{1,0:T(8,128)(2,1)S(1)} %collective-permute-done.37), channel_id=1, source_target_pairs={{4,6},{5,7},{12,14},{13,15},{20,22},{21,23},{28,30},{29,31}} | collective-permute-start | bytes 1572872 | tf_op jit(solution)/shard_map/cotangent/ppermute | solution.py:90
  356.6 6.2 fusion.61
  384.6 4.4 collective-permute-done.39
  397.8 5.2 multiply_convert_fusion.10
  408.4 16.6 %add_convert_fusion = bf16[2048,2048]{1,0:T(8,128)(2,1)} fusion(f32[]{:T(128)} %bitcast.64, bf16[1024,2048]{1,0:T(8,128)(2,1)S(1)} %copy-done.111, bf16[256,1024]{1,0:T(8,128)(2,1)} %copy-done.132, bf16[256,1024]{1,0:T(8,128)(2,1)} %copy-done.131, bf16[256,1024]{1,0:T(8,128)(2,1)} %copy-done.130, bf16[256,1024]{1,0:T(8,128)(2,1)S(1)} %get-tuple-element.73, ...), kind=kOutput, calls=%fused_computation | convolution fusion | flops 8631877632 | bytes 16777220 | tf_op jit(solution)/shard_map/grad_expand/dot_general | solution.py:53
  425.3 6.2 convolution_convert_fusion.2
  434.7 6.8 collective-permute-start.43
  442.8 4.0 collective-permute-start.42
  450.0 6.3 add_convert_fusion.2
  458.9 13.8 %collective-permute-done.43 = bf16[128,2048]{1,0:T(8,128)(2,1)} collective-permute-done((bf16[128,2048]{1,0:T(8,128)(2,1)}, bf16[128,2048]{1,0:T(8,128)(2,1)}, u32[]{:S(2)}, u32[]{:S(2)}) %collective-permute-start.43) | collective-permute-done | bytes 524320 | tf_op jit(solution)/shard_map/d_mlp_input/ppermute | solution.py:90
  483.8 9.1 %collective-permute-start.51 = (bf16[128,256]{1,0:T(8,128)(2,1)S(1)}, bf16[128,256]{1,0:T(8,128)(2,1)S(1)}, u32[]{:S(2)}, u32[]{:S(2)}) collective-permute-start(bf16[128,256]{1,0:T(8,128)(2,1)S(1)} %bitcast.377), channel_id=1, source_target_pairs={{0,2},{1,3},{2,0},{3,1},{4,6},{5,7},{6,4},{7,5},{8,10},{9,11},{10,... | collective-permute-start | bytes 196616 | tf_op jit(solution)/shard_map/heads/ppermute | solution.py:90
  494.0 3.9 collective-permute-start.53
  499.3 7.2 add_convert_fusion.1
  550.8 26.5 %collective-permute-done.60 = bf16[128,2048]{1,0:T(8,128)(2,1)} collective-permute-done((bf16[128,2048]{1,0:T(8,128)(2,1)}, bf16[128,2048]{1,0:T(8,128)(2,1)}, u32[]{:S(2)}, u32[]{:S(2)}) %collective-permute-start.60) | collective-permute-done | bytes 524320 | tf_op jit(solution)/shard_map/d_attend_input/ppermute | solution.py:90
  579.2 9.4 %collective-permute-done.61 = bf16[128,2048]{1,0:T(8,128)(2,1)} collective-permute-done((bf16[128,2048]{1,0:T(8,128)(2,1)}, bf16[128,2048]{1,0:T(8,128)(2,1)}, u32[]{:S(2)}, u32[]{:S(2)}) %collective-permute-start.61) | collective-permute-done | bytes 524320 | tf_op jit(solution)/shard_map/d_attend_input/ppermute | solution.py:90
  590.7 5.5 collective-permute-done.65
  600.4 5.5 fusion
  624.1 4.3 all-to-all-start.2
  628.4 24.7 %collective-permute-done.70 = bf16[512,2048]{1,0:T(8,128)(2,1)} collective-permute-done((bf16[512,2048]{1,0:T(8,128)(2,1)}, bf16[512,2048]{1,0:T(8,128)(2,1)}, u32[]{:S(2)}, u32[]{:S(2)}) %collective-permute-start.70) | collective-permute-done | bytes 2097184 | tf_op jit(solution)/shard_map/grad_outer/ppermute | solution.py:90
  663.6 48.1 %collective-permute-done.64 = bf16[128,2048]{1,0:T(8,128)(2,1)S(1)} collective-permute-done((bf16[128,2048]{1,0:T(8,128)(2,1)S(1)}, bf16[128,2048]{1,0:T(8,128)(2,1)S(1)}, u32[]{:S(2)}, u32[]{:S(2)}) %collective-permute-start.64) | collective-permute-done | bytes 524320 | tf_op jit(solution)/shard_map/d_attend_input/ppermute | solution.py:90
  724.7 5.4 collective-permute-done.72
  736.2 14.9 %collective-permute-done.73 = bf16[64,2048]{1,0:T(8,128)(2,1)} collective-permute-done((bf16[64,2048]{1,0:T(8,128)(2,1)S(1)}, bf16[64,2048]{1,0:T(8,128)(2,1)}, u32[]{:S(2)}, u32[]{:S(2)}) %collective-permute-start.73) | collective-permute-done | bytes 262176 | tf_op jit(solution)/shard_map/grad_outer/ppermute | solution.py:90
  760.5 9.6 %collective-permute-start.78 = (f32[33,128]{1,0:T(8,128)S(1)}, f32[33,128]{1,0:T(8,128)S(1)}, u32[]{:S(2)}, u32[]{:S(2)}) collective-permute-start(f32[33,128]{1,0:T(8,128)S(1)} %add_add_fusion.2), channel_id=1, source_target_pairs={{0,2},{1,3},{2,0},{3,1},{4,6},{5,7},{6,4},{7,5},{8,10},{9,11},{10,... | collective-permute-start | bytes 50696 | tf_op jit(solution)/shard_map/sums/ppermute | solution.py:90
  772.5 3.9 all-to-all-start.3
  793.2 4.4 copy.127
  803.7 9.5 %multiply_subtract_fusion = (f32[64,16384]{1,0:T(8,128)}, f32[64,16384]{1,0:T(8,128)}, f32[64,16384]{1,0:T(8,128)}) fusion(f32[64,16384]{1,0:T(8,128)S(1)} %copy-done.17, f32[64,16384]{1,0:T(8,128)} %bitcast.330, f32[64,16384]{1,0:T(8,128)} %param.33, f32[64,16384]{1,0:T(8,128)} %param.28), kind=kLoop, calls=%fused_computation.38 | loop fusion | flops 15728640 | bytes 29360128 | tf_op jit(solution)/shard_map/sub | solution.py:75
  820.6 3.9 multiply_subtract_fusion.1
  (693 shorter events, 347.7 us)
Async XLA Ops:
  16.1 31.9 %all-to-all-start = ((bf16[8,80,768]{2,1,0:T(8,128)(2,1)}), bf16[8,80,768]{2,1,0:T(8,128)(2,1)}, u32[]{:S(2)}, u32[]{:S(2)}) async-start(bf16[8,80,768]{2,1,0:T(8,128)(2,1)} %pad_maximum_fusion.8), calls=%async_computation | async-start | bytes 1966080 | tf_op jit(solution)/shard_map/inner/all_to_all | solution.py:149
  22.1 130.9 %all-gather.4.cloned.1.call-start = ((), (), s32[]{:S(2)}) async-start(), calls=%async_computation.6 | async-start | bytes 5242880 | tf_op jit(solution)/shard_map/shrink/all_gather | solution.py:237
  23.3 224.4 %all-gather.6.cloned.1.call-start = ((), (), s32[]{:S(2)}) async-start(), calls=%async_computation.7 | async-start | bytes 10485760 | tf_op jit(solution)/shard_map/outer/all_gather | solution.py:237
  24.4 31.9 %collective-permute-start.7 = (bf16[192,2048]{1,0:T(8,128)(2,1)}, bf16[192,2048]{1,0:T(8,128)(2,1)S(1)}, u32[]{:S(2)}, u32[]{:S(2)}) collective-permute-start(bf16[192,2048]{1,0:T(8,128)(2,1)} %pad_maximum_fusion.9), channel_id=1, source_target_pairs={{0,2},{1,3},{2,4},{3,5},{4,6},{5,7},{8,10},{9,11},{10,12},{11,13},... | collective-permute-start | bytes 2359304 | tf_op jit(solution)/shard_map/tokens/ppermute | solution.py:90
  28.4 30.5 %collective-permute-start.6 = (bf16[192,2048]{1,0:T(8,128)(2,1)}, bf16[192,2048]{1,0:T(8,128)(2,1)S(1)}, u32[]{:S(2)}, u32[]{:S(2)}) collective-permute-start(bf16[192,2048]{1,0:T(8,128)(2,1)} %pad_maximum_fusion.9), channel_id=1, source_target_pairs={{2,0},{3,1},{4,2},{5,3},{6,4},{7,5},{10,8},{11,9},{12,10},{13,11},... | collective-permute-start | bytes 2359304 | tf_op jit(solution)/shard_map/tokens/ppermute | solution.py:90
  29.7 64.7 %collective-permute-start.3 = (bf16[192,2048]{1,0:T(8,128)(2,1)}, bf16[192,2048]{1,0:T(8,128)(2,1)}, u32[]{:S(2)}, u32[]{:S(2)}) collective-permute-start(bf16[192,2048]{1,0:T(8,128)(2,1)} %pad_maximum_fusion.9), channel_id=1, source_target_pairs={{0,1},{1,0},{2,3},{3,2},{4,5},{5,4},{6,7},{7,6},{8,9},{9,8},{10,11... | collective-permute-start | bytes 2359304 | tf_op jit(solution)/shard_map/tokens/ppermute | solution.py:90
  57.4 25.4 %collective-permute-start.10 = (bf16[192,2048]{1,0:T(8,128)(2,1)}, bf16[192,2048]{1,0:T(8,128)(2,1)}, u32[]{:S(2)}, u32[]{:S(2)}) collective-permute-start(bf16[192,2048]{1,0:T(8,128)(2,1)} %broadcast_add_fusion.3), channel_id=1, source_target_pairs={{2,4},{3,5},{4,6},{5,7},{10,12},{11,13},{12,14},{13,15},{18,20},{1... | collective-permute-start | bytes 2359304 | tf_op jit(solution)/shard_map/tokens/ppermute | solution.py:90
  60.1 29.9 %collective-permute-start.9 = (bf16[192,2048]{1,0:T(8,128)(2,1)}, bf16[192,2048]{1,0:T(8,128)(2,1)}, u32[]{:S(2)}, u32[]{:S(2)}) collective-permute-start(bf16[192,2048]{1,0:T(8,128)(2,1)} %broadcast_add_fusion.4), channel_id=1, source_target_pairs={{2,0},{3,1},{4,2},{5,3},{10,8},{11,9},{12,10},{13,11},{18,16},{19,... | collective-permute-start | bytes 2359304 | tf_op jit(solution)/shard_map/tokens/ppermute | solution.py:90
  92.4 21.8 %collective-permute-start.12 = (bf16[192,2048]{1,0:T(8,128)(2,1)S(1)}, bf16[192,2048]{1,0:T(8,128)(2,1)S(1)}, u32[]{:S(2)}, u32[]{:S(2)}) collective-permute-start(bf16[192,2048]{1,0:T(8,128)(2,1)S(1)} %get-tuple-element.109), channel_id=1, source_target_pairs={{2,0},{3,1},{10,8},{11,9},{18,16},{19,17},{26,24},{27,25}} | collective-permute-start | bytes 2359304 | tf_op jit(solution)/shard_map/tokens/ppermute | solution.py:90
  97.8 21.6 %collective-permute-start.11 = (bf16[192,2048]{1,0:T(8,128)(2,1)}, bf16[192,2048]{1,0:T(8,128)(2,1)}, u32[]{:S(2)}, u32[]{:S(2)}) collective-permute-start(bf16[192,2048]{1,0:T(8,128)(2,1)} %get-tuple-element.107), channel_id=1, source_target_pairs={{0,1},{1,0},{2,3},{3,2},{4,5},{5,4},{6,7},{7,6},{8,9},{9,8},{10,11... | collective-permute-start | bytes 2359304 | tf_op jit(solution)/shard_map/tokens/ppermute | solution.py:90
  116.8 33.8 %collective-permute-start.14 = (bf16[192,2048]{1,0:T(8,128)(2,1)}, bf16[192,2048]{1,0:T(8,128)(2,1)}, u32[]{:S(2)}, u32[]{:S(2)}) collective-permute-start(bf16[192,2048]{1,0:T(8,128)(2,1)} %get-tuple-element.100), channel_id=1, source_target_pairs={{0,1},{1,0},{2,3},{3,2},{4,5},{5,4},{6,7},{7,6},{8,9},{9,8},{10,11... | collective-permute-start | bytes 2359304 | tf_op jit(solution)/shard_map/tokens/ppermute | solution.py:90
  164.9 22.8 %collective-permute-start.5 = (bf16[2,512,768]{2,1,0:T(8,128)(2,1)}, bf16[2,512,768]{2,1,0:T(8,128)(2,1)}, u32[]{:S(2)}, u32[]{:S(2)}) collective-permute-start(bf16[2,512,768]{2,1,0:T(8,128)(2,1)} %pad_maximum_fusion.4), channel_id=1, source_target_pairs={{0,8},{1,9},{2,10},{3,11},{4,12},{5,13},{6,14},{7,15},{8,0},{9,1},... | collective-permute-start | bytes 4718600 | tf_op jit(solution)/shard_map/inner/ppermute | solution.py:90
  180.3 69.9 %all-to-all-start.1 = ((bf16[8,64,2048]{2,1,0:T(8,128)(2,1)}), bf16[8,64,2048]{2,1,0:T(8,128)(2,1)}, u32[]{:S(2)}, u32[]{:S(2)}) async-start(bf16[8,64,2048]{2,1,0:T(8,128)(2,1)} %reshape.687), calls=%async_computation.1 | async-start | bytes 4194304 | tf_op jit(solution)/shard_map/expand/all_to_all | solution.py:149
  187.7 168.9 %all-gather.8.cloned.1.call-start = ((), (), s32[]{:S(2)}) async-start(), calls=%async_computation.8 | async-start | bytes 10485760 | tf_op jit(solution)/shard_map/expand/all_gather | solution.py:237
  213.8 30.7 %collective-permute-start.18 = (bf16[128,256]{1,0:T(8,128)(2,1)S(1)}, bf16[128,256]{1,0:T(8,128)(2,1)S(1)}, u32[]{:S(2)}, u32[]{:S(2)}) collective-permute-start(bf16[128,256]{1,0:T(8,128)(2,1)S(1)} %get-tuple-element.130), channel_id=1, source_target_pairs={{0,4},{1,5},{2,6},{3,7},{4,0},{5,1},{6,2},{7,3},{8,12},{9,13},{10,... | collective-permute-start | bytes 196616 | tf_op jit(solution)/shard_map/rows/ppermute | solution.py:90
  216.6 29.8 %collective-permute-start.19 = (bf16[128,256]{1,0:T(8,128)(2,1)S(1)}, bf16[128,256]{1,0:T(8,128)(2,1)S(1)}, u32[]{:S(2)}, u32[]{:S(2)}) collective-permute-start(bf16[128,256]{1,0:T(8,128)(2,1)S(1)} %get-tuple-element.131), channel_id=1, source_target_pairs={{0,5},{1,4},{2,7},{3,6},{4,1},{5,0},{6,3},{7,2},{8,13},{9,12},{10,... | collective-permute-start | bytes 196616 | tf_op jit(solution)/shard_map/rows/ppermute | solution.py:90
  218.1 28.3 %collective-permute-start.20 = (bf16[128,256]{1,0:T(8,128)(2,1)S(1)}, bf16[128,256]{1,0:T(8,128)(2,1)S(1)}, u32[]{:S(2)}, u32[]{:S(2)}) collective-permute-start(bf16[128,256]{1,0:T(8,128)(2,1)S(1)} %get-tuple-element.132), channel_id=1, source_target_pairs={{0,6},{1,7},{2,4},{3,5},{4,2},{5,3},{6,0},{7,1},{8,14},{9,15},{10,... | collective-permute-start | bytes 196616 | tf_op jit(solution)/shard_map/rows/ppermute | solution.py:90
  253.3 370.8 %reduce-scatter.3.cloned.1.call-start = ((), (), s32[]{:S(2)}) async-start(), calls=%async_computation.9 | async-start | bytes 10485760 | tf_op jit(solution)/shard_map/grad_expand/reduce_scatter | solution.py:260
  323.8 24.6 %collective-permute-start.33 = (bf16[128,2048]{1,0:T(8,128)(2,1)S(1)}, bf16[128,2048]{1,0:T(8,128)(2,1)S(1)}, u32[]{:S(2)}, u32[]{:S(2)}) collective-permute-start(bf16[128,2048]{1,0:T(8,128)(2,1)S(1)} %get-tuple-element.55), channel_id=1, source_target_pairs={{0,1},{1,0},{2,3},{3,2},{4,5},{5,4},{6,7},{7,6},{8,9},{9,8},{10,11... | collective-permute-start | bytes 1572872 | tf_op jit(solution)/shard_map/mlp_input/ppermute | solution.py:90
  354.9 36.1 %collective-permute-start.46 = (bf16[128,2048]{1,0:T(8,128)(2,1)}, bf16[128,2048]{1,0:T(8,128)(2,1)}, u32[]{:S(2)}, u32[]{:S(2)}) collective-permute-start(bf16[128,2048]{1,0:T(8,128)(2,1)} %get-tuple-element.47), channel_id=1, source_target_pairs={{0,1},{1,0},{2,3},{3,2},{4,5},{5,4},{6,7},{7,6},{8,9},{9,8},{10,11... | collective-permute-start | bytes 1572872 | tf_op jit(solution)/shard_map/cotangent/ppermute | solution.py:90
  425.0 297.3 %reduce-scatter.5.cloned.1.call-start = ((), (), s32[]{:S(2)}) async-start(), calls=%async_computation.10 | async-start | bytes 5242880 | tf_op jit(solution)/shard_map/grad_shrink/reduce_scatter | solution.py:260
  434.7 38.0 %collective-permute-start.43 = (bf16[128,2048]{1,0:T(8,128)(2,1)}, bf16[128,2048]{1,0:T(8,128)(2,1)}, u32[]{:S(2)}, u32[]{:S(2)}) collective-permute-start(bf16[128,2048]{1,0:T(8,128)(2,1)} %add_convert_fusion.8), channel_id=1, source_target_pairs={{0,4},{1,5},{2,6},{3,7},{4,0},{5,1},{6,2},{7,3},{8,12},{9,13},{10,... | collective-permute-start | bytes 1572872 | tf_op jit(solution)/shard_map/d_mlp_input/ppermute | solution.py:90
  442.8 30.7 %collective-permute-start.42 = (bf16[128,2048]{1,0:T(8,128)(2,1)S(1)}, bf16[128,2048]{1,0:T(8,128)(2,1)}, u32[]{:S(2)}, u32[]{:S(2)}) collective-permute-start(bf16[128,2048]{1,0:T(8,128)(2,1)S(1)} %add_convert_fusion.9), channel_id=1, source_target_pairs={{0,2},{1,3},{2,0},{3,1},{4,6},{5,7},{6,4},{7,5},{8,10},{9,11},{10,... | collective-permute-start | bytes 1572872 | tf_op jit(solution)/shard_map/d_mlp_input/ppermute | solution.py:90
  447.8 25.7 %collective-permute-start.48 = (bf16[128,2048]{1,0:T(8,128)(2,1)}, bf16[128,2048]{1,0:T(8,128)(2,1)}, u32[]{:S(2)}, u32[]{:S(2)}) collective-permute-start(bf16[128,2048]{1,0:T(8,128)(2,1)} %add_convert_fusion.7), channel_id=1, source_target_pairs={{0,6},{1,7},{2,4},{3,5},{4,2},{5,3},{6,0},{7,1},{8,14},{9,15},{10,... | collective-permute-start | bytes 1572872 | tf_op jit(solution)/shard_map/d_mlp_input/ppermute | solution.py:90
  483.5 28.2 %collective-permute-start.50 = (bf16[128,256]{1,0:T(8,128)(2,1)S(1)}, bf16[128,256]{1,0:T(8,128)(2,1)S(1)}, u32[]{:S(2)}, u32[]{:S(2)}) collective-permute-start(bf16[128,256]{1,0:T(8,128)(2,1)S(1)} %bitcast.378), channel_id=1, source_target_pairs={{0,1},{1,0},{2,3},{3,2},{4,5},{5,4},{6,7},{7,6},{8,9},{9,8},{10,11... | collective-permute-start | bytes 196616 | tf_op jit(solution)/shard_map/heads/ppermute | solution.py:90
  483.8 30.3 %collective-permute-start.51 = (bf16[128,256]{1,0:T(8,128)(2,1)S(1)}, bf16[128,256]{1,0:T(8,128)(2,1)S(1)}, u32[]{:S(2)}, u32[]{:S(2)}) collective-permute-start(bf16[128,256]{1,0:T(8,128)(2,1)S(1)} %bitcast.377), channel_id=1, source_target_pairs={{0,2},{1,3},{2,0},{3,1},{4,6},{5,7},{6,4},{7,5},{8,10},{9,11},{10,... | collective-permute-start | bytes 196616 | tf_op jit(solution)/shard_map/heads/ppermute | solution.py:90
  492.9 23.5 %collective-permute-start.52 = (bf16[128,256]{1,0:T(8,128)(2,1)S(1)}, bf16[128,256]{1,0:T(8,128)(2,1)S(1)}, u32[]{:S(2)}, u32[]{:S(2)}) collective-permute-start(bf16[128,256]{1,0:T(8,128)(2,1)S(1)} %bitcast.375), channel_id=1, source_target_pairs={{0,3},{1,2},{2,1},{3,0},{4,7},{5,6},{6,5},{7,4},{8,11},{9,10},{10,... | collective-permute-start | bytes 196616 | tf_op jit(solution)/shard_map/heads/ppermute | solution.py:90
  494.0 23.3 %collective-permute-start.53 = (bf16[128,256]{1,0:T(8,128)(2,1)S(1)}, bf16[128,256]{1,0:T(8,128)(2,1)S(1)}, u32[]{:S(2)}, u32[]{:S(2)}) collective-permute-start(bf16[128,256]{1,0:T(8,128)(2,1)S(1)} %bitcast.373), channel_id=1, source_target_pairs={{0,4},{1,5},{2,6},{3,7},{4,0},{5,1},{6,2},{7,3},{8,12},{9,13},{10,... | collective-permute-start | bytes 196616 | tf_op jit(solution)/shard_map/heads/ppermute | solution.py:90
  516.5 94.0 %collective-permute-start.49 = (bf16[4,128,2048]{2,1,0:T(8,128)(2,1)}, bf16[4,128,2048]{2,1,0:T(8,128)(2,1)}, u32[]{:S(2)}, u32[]{:S(2)}) collective-permute-start(bf16[4,128,2048]{2,1,0:T(8,128)(2,1)} %slice_bitcast_fusion), channel_id=1, source_target_pairs={{0,1},{1,0},{2,3},{3,2},{4,5},{5,4},{6,7},{7,6},{8,9},{9,8},{10,11... | collective-permute-start | bytes 6291464 | tf_op jit(solution)/shard_map/feed/ppermute | solution.py:90
  517.2 83.2 %collective-permute-start.69 = (bf16[2,512,2048]{2,1,0:T(8,128)(2,1)}, bf16[2,512,2048]{2,1,0:T(8,128)(2,1)}, u32[]{:S(2)}, u32[]{:S(2)}) collective-permute-start(bf16[2,512,2048]{2,1,0:T(8,128)(2,1)} %dynamic-slice_bitcast_fusion), channel_id=1, source_target_pairs={{0,8},{1,9},{2,10},{3,11},{4,12},{5,13},{6,14},{7,15},{8,0},{9,1},... | collective-permute-start | bytes 12582920 | tf_op jit(solution)/shard_map/grad_outer/ppermute | solution.py:90
  538.6 38.8 %collective-permute-start.60 = (bf16[128,2048]{1,0:T(8,128)(2,1)}, bf16[128,2048]{1,0:T(8,128)(2,1)}, u32[]{:S(2)}, u32[]{:S(2)}) collective-permute-start(bf16[128,2048]{1,0:T(8,128)(2,1)} %slice.500), channel_id=1, source_target_pairs={{0,1},{1,0},{2,3},{3,2},{4,5},{5,4},{6,7},{7,6},{8,9},{9,8},{10,11... | collective-permute-start | bytes 1572872 | tf_op jit(solution)/shard_map/d_attend_input/ppermute | solution.py:90
  543.0 45.6 %collective-permute-start.61 = (bf16[128,2048]{1,0:T(8,128)(2,1)}, bf16[128,2048]{1,0:T(8,128)(2,1)}, u32[]{:S(2)}, u32[]{:S(2)}) collective-permute-start(bf16[128,2048]{1,0:T(8,128)(2,1)} %slice.503), channel_id=1, source_target_pairs={{0,1},{1,0},{2,3},{3,2},{4,5},{5,4},{6,7},{7,6},{8,9},{9,8},{10,11... | collective-permute-start | bytes 1572872 | tf_op jit(solution)/shard_map/d_attend_input/ppermute | solution.py:90
  547.6 48.6 %collective-permute-start.65 = (bf16[128,2048]{1,0:T(8,128)(2,1)}, bf16[128,2048]{1,0:T(8,128)(2,1)}, u32[]{:S(2)}, u32[]{:S(2)}) collective-permute-start(bf16[128,2048]{1,0:T(8,128)(2,1)} %slice.510), channel_id=1, source_target_pairs={{0,1},{1,0},{2,3},{3,2},{4,5},{5,4},{6,7},{7,6},{8,9},{9,8},{10,11... | collective-permute-start | bytes 1572872 | tf_op jit(solution)/shard_map/d_attend_input/ppermute | solution.py:90
  590.7 70.7 %collective-permute-start.62 = (bf16[128,2048]{1,0:T(8,128)(2,1)}, bf16[128,2048]{1,0:T(8,128)(2,1)}, u32[]{:S(2)}, u32[]{:S(2)}) collective-permute-start(bf16[128,2048]{1,0:T(8,128)(2,1)} %add_convert_fusion.6), channel_id=1, source_target_pairs={{0,2},{1,3},{2,0},{3,1},{4,6},{5,7},{6,4},{7,5},{8,10},{9,11},{10,... | collective-permute-start | bytes 1572872 | tf_op jit(solution)/shard_map/d_attend_input/ppermute | solution.py:90
  598.5 63.6 %collective-permute-start.66 = (bf16[128,2048]{1,0:T(8,128)(2,1)}, bf16[128,2048]{1,0:T(8,128)(2,1)}, u32[]{:S(2)}, u32[]{:S(2)}) collective-permute-start(bf16[128,2048]{1,0:T(8,128)(2,1)} %add_convert_fusion.4), channel_id=1, source_target_pairs={{0,6},{1,7},{2,4},{3,5},{4,2},{5,3},{6,0},{7,1},{8,14},{9,15},{10,... | collective-permute-start | bytes 1572872 | tf_op jit(solution)/shard_map/d_attend_input/ppermute | solution.py:90
  609.0 44.1 %collective-permute-start.70 = (bf16[512,2048]{1,0:T(8,128)(2,1)}, bf16[512,2048]{1,0:T(8,128)(2,1)}, u32[]{:S(2)}, u32[]{:S(2)}) collective-permute-start(bf16[512,2048]{1,0:T(8,128)(2,1)} %dynamic-slice_bitcast_fusion.1), channel_id=1, source_target_pairs={{0,16},{1,17},{2,18},{3,19},{4,20},{5,21},{6,22},{7,23},{8,24},{9,... | collective-permute-start | bytes 6291464 | tf_op jit(solution)/shard_map/grad_outer/ppermute | solution.py:90
  620.2 38.4 %collective-permute-start.67 = (bf16[2,512,768]{2,1,0:T(8,128)(2,1)S(1)}, bf16[2,512,768]{2,1,0:T(8,128)(2,1)S(1)}, u32[]{:S(2)}, u32[]{:S(2)}) collective-permute-start(bf16[2,512,768]{2,1,0:T(8,128)(2,1)S(1)} %dynamic-slice_bitcast_fusion.2), channel_id=1, source_target_pairs={{0,8},{1,9},{2,10},{3,11},{4,12},{5,13},{6,14},{7,15},{8,0},{9,1},... | collective-permute-start | bytes 4718600 | tf_op jit(solution)/shard_map/grad_inner/ppermute | solution.py:90
  623.1 34.2 %collective-permute-start.63 = (bf16[128,2048]{1,0:T(8,128)(2,1)}, bf16[128,2048]{1,0:T(8,128)(2,1)}, u32[]{:S(2)}, u32[]{:S(2)}) collective-permute-start(bf16[128,2048]{1,0:T(8,128)(2,1)} %slice.507), channel_id=1, source_target_pairs={{0,1},{1,0},{2,3},{3,2},{4,5},{5,4},{6,7},{7,6},{8,9},{9,8},{10,11... | collective-permute-start | bytes 1572872 | tf_op jit(solution)/shard_map/d_attend_input/ppermute | solution.py:90
  624.1 110.3 %all-to-all-start.2 = ((bf16[8,64,2048]{2,1,0:T(8,128)(2,1)}), bf16[8,64,2048]{2,1,0:T(8,128)(2,1)}, u32[]{:S(2)}, u32[]{:S(2)}) async-start(bf16[8,64,2048]{2,1,0:T(8,128)(2,1)} %bitcast.341), calls=%async_computation.3 | async-start | bytes 4194304 | tf_op jit(solution)/shard_map/own_expand/all_to_all | solution.py:149
  656.4 58.5 %collective-permute-start.71 = (bf16[4,64,2048]{2,1,0:T(8,128)(2,1)S(1)}, bf16[4,64,2048]{2,1,0:T(8,128)(2,1)S(1)}, u32[]{:S(2)}, u32[]{:S(2)}) collective-permute-start(bf16[4,64,2048]{2,1,0:T(8,128)(2,1)S(1)} %dynamic-slice_bitcast_fusion.3), channel_id=1, source_target_pairs={{0,1},{1,0},{2,3},{3,2},{4,5},{5,4},{6,7},{7,6},{8,9},{9,8},{10,11... | collective-permute-start | bytes 3145736 | tf_op jit(solution)/shard_map/grad_outer/ppermute | solution.py:90
  658.5 53.2 %collective-permute-start.64 = (bf16[128,2048]{1,0:T(8,128)(2,1)S(1)}, bf16[128,2048]{1,0:T(8,128)(2,1)S(1)}, u32[]{:S(2)}, u32[]{:S(2)}) collective-permute-start(bf16[128,2048]{1,0:T(8,128)(2,1)S(1)} %add_convert_fusion.5), channel_id=1, source_target_pairs={{0,4},{1,5},{2,6},{3,7},{4,0},{5,1},{6,2},{7,3},{8,12},{9,13},{10,... | collective-permute-start | bytes 1572872 | tf_op jit(solution)/shard_map/d_attend_input/ppermute | solution.py:90
  658.6 98.4 %collective-permute-start.57 = (bf16[128,2048]{1,0:T(8,128)(2,1)}, bf16[128,2048]{1,0:T(8,128)(2,1)}, u32[]{:S(2)}, u32[]{:S(2)}) collective-permute-start(bf16[128,2048]{1,0:T(8,128)(2,1)} %get-tuple-element.91), channel_id=1, source_target_pairs={{0,2},{1,3},{2,0},{3,1},{4,6},{5,7},{6,4},{7,5},{8,10},{9,11},{10,... | collective-permute-start | bytes 1572872 | tf_op jit(solution)/shard_map/feed/ppermute | solution.py:90
  661.4 96.2 %collective-permute-start.58 = (bf16[128,2048]{1,0:T(8,128)(2,1)}, bf16[128,2048]{1,0:T(8,128)(2,1)}, u32[]{:S(2)}, u32[]{:S(2)}) collective-permute-start(bf16[128,2048]{1,0:T(8,128)(2,1)} %get-tuple-element.93), channel_id=1, source_target_pairs={{0,4},{1,5},{2,6},{3,7},{4,0},{5,1},{6,2},{7,3},{8,12},{9,13},{10,... | collective-permute-start | bytes 1572872 | tf_op jit(solution)/shard_map/feed/ppermute | solution.py:90
  662.2 53.9 %collective-permute-start.68 = (bf16[512,768]{1,0:T(8,128)(2,1)S(1)}, bf16[512,768]{1,0:T(8,128)(2,1)S(1)}, u32[]{:S(2)}, u32[]{:S(2)}) collective-permute-start(bf16[512,768]{1,0:T(8,128)(2,1)S(1)} %dynamic-slice_bitcast_fusion.4), channel_id=1, source_target_pairs={{0,16},{1,17},{2,18},{3,19},{4,20},{5,21},{6,22},{7,23},{8,24},{9,... | collective-permute-start | bytes 2359304 | tf_op jit(solution)/shard_map/grad_inner/ppermute | solution.py:90
  717.9 33.2 %collective-permute-start.73 = (bf16[64,2048]{1,0:T(8,128)(2,1)S(1)}, bf16[64,2048]{1,0:T(8,128)(2,1)}, u32[]{:S(2)}, u32[]{:S(2)}) collective-permute-start(bf16[64,2048]{1,0:T(8,128)(2,1)S(1)} %get-tuple-element.106), channel_id=1, source_target_pairs={{0,4},{1,5},{2,6},{3,7},{4,0},{5,1},{6,2},{7,3},{8,12},{9,13},{10,... | collective-permute-start | bytes 786440 | tf_op jit(solution)/shard_map/grad_outer/ppermute | solution.py:90
  719.3 31.9 %collective-permute-start.74 = (bf16[64,2048]{1,0:T(8,128)(2,1)S(1)}, bf16[64,2048]{1,0:T(8,128)(2,1)}, u32[]{:S(2)}, u32[]{:S(2)}) collective-permute-start(bf16[64,2048]{1,0:T(8,128)(2,1)S(1)} %get-tuple-element.105), channel_id=1, source_target_pairs={{0,6},{1,7},{2,4},{3,5},{4,2},{5,3},{6,0},{7,1},{8,14},{9,15},{10,... | collective-permute-start | bytes 786440 | tf_op jit(solution)/shard_map/grad_outer/ppermute | solution.py:90
  730.1 27.5 %collective-permute-start.59 = (bf16[128,2048]{1,0:T(8,128)(2,1)}, bf16[128,2048]{1,0:T(8,128)(2,1)}, u32[]{:S(2)}, u32[]{:S(2)}) collective-permute-start(bf16[128,2048]{1,0:T(8,128)(2,1)} %get-tuple-element.92), channel_id=1, source_target_pairs={{0,6},{1,7},{2,4},{3,5},{4,2},{5,3},{6,0},{7,1},{8,14},{9,15},{10,... | collective-permute-start | bytes 1572872 | tf_op jit(solution)/shard_map/feed/ppermute | solution.py:90
  772.5 25.2 %all-to-all-start.3 = ((bf16[8,64,768]{2,1,0:T(8,128)(2,1)}), bf16[8,64,768]{2,1,0:T(8,128)(2,1)S(1)}, u32[]{:S(2)}, u32[]{:S(2)}) async-start(bf16[8,64,768]{2,1,0:T(8,128)(2,1)} %bitcast.115), calls=%async_computation.5 | async-start | bytes 1572864 | tf_op jit(solution)/shard_map/own_inner/all_to_all | solution.py:149
  (186 other events, 1843.1 us)
Sparse Core Ops, SparseCore 0:
  25.1 35.9 all-gather.3
  163.8 60.9 all-gather.5
  253.4 57.9 all-gather.7
  425.1 76.8 reduce-scatter.2
  505.2 44.5 reduce-scatter.4

commit v3 on v2

--- a/solution.py
+++ b/solution.py
@@ -73,6 +73,49 @@
         first / (1.0 - BETA_ONE**STEP) / (jnp.sqrt(second / (1.0 - BETA_TWO**STEP)) + ADAM_EPSILON)
     )
     return (first, second, weight - rate * (update + decay * weight))
+
+
+def adamw_blocks(factor, weight, grad, first, second, weight_new, first_new, second_new):
+    count = grad.shape[0] if len(grad.shape) == 3 else 1
+    size = weight.shape[1] // count
+    for index in range(count):
+        columns = pl.ds(index * size, size)
+        low = grad[index] if len(grad.shape) == 3 else grad[...]
+        result = adamw(
+            weight[:, columns],
+            low.astype(jnp.float32),
+            first[:, columns],
+            second[:, columns],
+            factor[0],
+            DECAY,
+            RATE,
+        )
+        first_new[:, columns], second_new[:, columns], weight_new[:, columns] = result
+
+
+def adamw_matrix(weight, grad, first, second, factor, size=0):
+    rows, columns = weight.shape
+    if grad.ndim == 3:
+        places = grad.shape[0]
+        grad_spec = pl.BlockSpec((places, rows, size), lambda i: (0, 0, i))
+        grid = (grad.shape[2] // size,)
+        spec = pl.BlockSpec((rows, places * size), lambda i: (0, i))
+    else:
+        grid = (rows // 64,)
+        spec = grad_spec = pl.BlockSpec((64, columns), lambda i: (i, 0))
+    result = jax.ShapeDtypeStruct(weight.shape, jnp.float32)
+    weight_new, first_new, second_new = pl.pallas_call(
+        adamw_blocks,
+        grid=grid,
+        in_specs=[pl.BlockSpec(memory_space=pltpu.SMEM), spec, grad_spec, spec, spec],
+        out_specs=[spec, spec, spec],
+        out_shape=[result, result, result],
+        compiler_params=pltpu.CompilerParams(vmem_limit_bytes=56 * 1024 * 1024),
+        cost_estimate=pl.CostEstimate(
+            flops=20 * weight.size, bytes_accessed=26 * weight.size, transcendentals=weight.size
+        ),
+    )(factor.reshape(1), weight, grad, first, second)
+    return first_new, second_new, weight_new
 
 
 def move(value, where):
@@ -111,20 +154,24 @@
     return move(value, where)
 
 
-def gather_rows(block, holds=()):
+def gather_rows(block, first_holds=(), last_holds=(), crossing=None):
     z = lax.axis_index("seq") // 2
-    up, down = [block], [block]
-    for hop in range(1, DEPTH):
-        held = holds[hop - 2 : hop - 1] if hop >= 2 else ()
-        up.append(line(after(up[-1], *held), hop, 1))
-        down.append(line(after(down[-1], *held), hop, -1))
-    column = [
-        block,
-        jnp.where(z % 2 == 0, down[1], up[1]),
-        jnp.where(z < 2, down[2], up[2]),
-        jnp.where(z < 2, jnp.where(z == 0, down[3], down[1]), jnp.where(z == 3, up[3], up[1])),
-    ]
-    return [jnp.concatenate([piece, across(piece)], axis=0) for piece in column]
+    column, other = [block], [across(block)]
+
+    def came(piece, *holds):
+        column.append(after(piece, other[-1], *holds))
+        other.append(across(column[-1]))
+
+    up, down = line(block, 1, 1), line(block, 1, -1)
+    up_one, down_one = up, down
+    came(jnp.where(z % 2 == 0, down, up))
+    up, down = line(after(up, *first_holds), 2, 1), line(after(down, *first_holds), 2, -1)
+    came(jnp.where(z < 2, down, up))
+    last_holds = (other[1], *last_holds)
+    up, down = line(after(up, *last_holds), 3, 1), line(after(down, *last_holds), 3, -1)
+    last = jnp.where(z < 2, jnp.where(z == 0, down, down_one), jnp.where(z == 3, up, up_one))
+    came(last, *(crossing(last) if crossing else ()))
+    return [jnp.concatenate(pair, axis=0) for pair in zip(column, other, strict=True)], column[-1]
 
 
 def nothing(*others):
@@ -134,6 +181,13 @@
 
 def after(value, *others):
     return value + nothing(*others).astype(value.dtype) if others else value
+
+
+def after_in_place(value, *others):
+    value = lax.optimization_barrier(value)
+    start = (0,) * value.ndim
+    first = lax.slice(value, start, (1,) * (value.ndim - 1) + (128,))
+    return lax.dynamic_update_slice(value, after(first, *others), start)
 
 
 def pairs_of():
@@ -177,7 +231,7 @@
             out_specs=pl.BlockSpec(block, lambda i, order: (i, 0, 0)),
         ),
         out_shape=jax.ShapeDtypeStruct(blocks.shape, blocks.dtype),
-        compiler_params=pltpu.CompilerParams(vmem_limit_bytes=32 * 1024 * 1024),
+        compiler_params=pltpu.CompilerParams(vmem_limit_bytes=56 * 1024 * 1024),
         cost_estimate=pl.CostEstimate(flops=0, bytes_accessed=4 * blocks.size, transcendentals=0),
     )(order.astype(jnp.int32), blocks)
 
@@ -197,7 +251,7 @@
             out_specs=pl.BlockSpec((rows, columns), lambda i, order: (0, i)),
         ),
         out_shape=jax.ShapeDtypeStruct((rows, count * columns), received[0].dtype),
-        compiler_params=pltpu.CompilerParams(vmem_limit_bytes=32 * 1024 * 1024),
+        compiler_params=pltpu.CompilerParams(vmem_limit_bytes=56 * 1024 * 1024),
         cost_estimate=pl.CostEstimate(
             flops=0, bytes_accessed=4 * count * rows * columns, transcendentals=0
         ),
@@ -207,12 +261,15 @@
 def scatter_rows(partial, order):
     sums, came = {}, []
     for n, k in enumerate(order):
-        term = partial(k, came[n - 2 : n - 1] if n >= 2 else [])
+        earlier = came[n - 2 : n - 1] if n >= 2 else []
+        if n == DEPTH - 1:
+            earlier = earlier + [sums[order[0]]] if order[0] else earlier
+        term = partial(k, earlier)
         rows = term.shape[0] // 2
         came.append(across(term[rows:]))
         total = term[:rows].astype(jnp.float32) + came[-1].astype(jnp.float32)
-        sums[k] = turn(total.astype(jnp.bfloat16), k).astype(jnp.float32) if k else total
-    return sum(sums[k] for k in range(DEPTH)), came
+        sums[k] = turn(total.astype(jnp.bfloat16), k) if k else total
+    return sum(sums[k].astype(jnp.float32) for k in range(DEPTH)), came
 
 
 def sum_everywhere(value):
@@ -269,22 +326,15 @@
     return after(total, *holds).astype(jnp.bfloat16)
 
 
-def reduce_by_hand(rows, *holds):
-    dp = lax.axis_index("dp")
-    y, core = dp // 2, dp % 2
+def reduce_over_cores(rows):
+    core = lax.axis_index("dp") % 2
     parts = rows.reshape(2, 2, -1, *rows.shape[1:])
-    parts = add_low(take(parts, core, 1), other_core(take(parts, 1 - core, 1)))
-    return add_low(take(parts, y, 0), other_y(take(parts, 1 - y, 0)), *holds)
-
-
-def reduce_along_seq(rows, holds, last_holds):
-    z, x = lax.axis_index("seq") // 2, lax.axis_index("seq") % 2
-    parts = rows.reshape(DEPTH, 2, -1, *rows.shape[1:])
-    parts = add_low(take(parts, x, 1), across(take(parts, 1 - x, 1)), *holds)
-    total = after(take(parts, z, 0).astype(jnp.float32), *last_holds)
-    for k in range(1, DEPTH):
-        total = total + turn(take(parts, z ^ k, 0), k).astype(jnp.float32)
-    return total
+    return add_low(take(parts, core, 1), other_core(take(parts, 1 - core, 1)))
+
+
+def reduce_over_y(parts):
+    y = lax.axis_index("dp") // 2
+    return add_low(take(parts, y, 0), other_y(take(parts, 1 - y, 0)))
 
 
 def body(
@@ -341,6 +391,9 @@
         gains = gains.transpose(2, 1, 0, 3).reshape(2, width)
         documents = small[:, gain_parts.size : gain_parts.size + rows]
         documents = jnp.concatenate([take(documents, s, 0) for s in sources]).astype(f32)
+    with jax.named_scope("expand"):
+        expand_low = expand_weight.astype(bf16).reshape(owned, 2 * n_dp, n_seq, slab)
+        expand_low = by_place(expand_low, n_seq)
     with jax.named_scope("shrink"):
         shrink = share(shrink_weight.astype(bf16))
     gain_one, gain_two = gains[0], gains[1]
@@ -367,7 +420,14 @@
 
     with jax.named_scope("tokens"):
         block = jnp.concatenate([inputs_low, outer_weight.astype(bf16)], axis=0)
-        pieces = gather_rows(block, [inner_blocks, inner_first])
+        expand_sent = []
+
+        def send_expand(last):
+            expand_sent.append(after_in_place(expand_low, last))
+            return expand_sent
+
+        pieces, last = gather_rows(block, [inner_blocks, expand_low], [inner_first])
+        expand_sent = [after_in_place(expand_low, last)]
         pieces = [piece.reshape(2, rows + owned, width) for piece in pieces]
         token_pieces = [piece[:, :rows].reshape(2 * rows, width) for piece in pieces]
     with jax.named_scope("outer"):
@@ -375,11 +435,12 @@
         outer[0] = after(outer[0], shrink)
         outer = share(in_place(outer).reshape(n_seq * owned, width))
     with jax.named_scope("expand"):
-        expand_low = after(expand_weight, *token_pieces[1:]).astype(bf16)
-        expand_low = expand_low.reshape(owned, 2 * n_dp, n_seq, slab)
-        expand_blocks = exchange(by_place(expand_low, n_seq))
+        expand_blocks = exchange(expand_sent[0])
     with jax.named_scope("attend"):
-        attend_pieces = [(first_norm(piece)[0] * gain_one).astype(bf16) for piece in token_pieces]
+        attend_gain = after(gain_one, expand_sent[0])
+        attend_pieces = [
+            (first_norm(piece)[0] * attend_gain).astype(bf16) for piece in token_pieces
+        ]
         projected = jnp.concatenate([multiply(piece, inner) for piece in attend_pieces], axis=0)
         visible = (documents[:, None] == documents[None, :]) & (places[None, :] <= places[:, None])
         visible = visible.astype(f32)
@@ -396,7 +457,7 @@
     with jax.named_scope("rows"):
         attended_rows = side_by_side(exchange_small(list(attended)))
     with jax.named_scope("expand"):
-        expand_blocks = after(expand_blocks, attended_rows, outer)
+        expand_blocks = after_in_place(expand_blocks, attended_rows, outer)
         expand = share(expand_blocks.reshape(n_seq * owned, -1))
     inputs = inputs_low.astype(f32)
     residual = inputs + multiply(attended_rows, outer)
@@ -404,11 +465,11 @@
     normed_second = residual * inverse_second
 
     with jax.named_scope("mlp_input"):
-        mlp_pieces = gather_rows((normed_second * gain_two).astype(bf16))
+        mlp_pieces, _ = gather_rows((normed_second * gain_two).astype(bf16))
     with jax.named_scope("gate_up"):
         gate_ups = [multiply(piece, expand) for piece in mlp_pieces]
     with jax.named_scope("cotangent"):
-        upstream_pieces = gather_rows(after(upstream, *mlp_pieces[1:]))
+        upstream_pieces, _ = gather_rows(after(upstream, *mlp_pieces[1:]))
     activations, gate_up_grads = [None] * DEPTH, [None] * DEPTH
 
     def feed_back(k, earlier):
@@ -424,32 +485,25 @@
 
     with jax.named_scope("d_mlp_input"):
         d_mlp_input, came = scatter_rows(feed_back, [0, 2, 1, 3])
+    partial_gain_two = jnp.sum(d_mlp_input * normed_second, axis=0)
+    d_residual = upstream.astype(f32) + norm_back(
+        d_mlp_input * gain_two, normed_second, inverse_second
+    )
+
+    with jax.named_scope("heads"):
+        d_residual_low = d_residual.astype(bf16)
+        d_attended = contract_last(d_residual_low, outer).astype(bf16)
+        d_attended = by_place(d_attended.reshape(rows, 1, n_seq, own_width), n_seq)
     with jax.named_scope("grad_expand"):
         grad_expand = contract_rows(
             jnp.concatenate(mlp_pieces, axis=0), jnp.concatenate(gate_up_grads, axis=0)
         )
-        grad_expand = after(grad_expand, *came[3:4]).astype(bf16)
-    with jax.named_scope("grad_shrink"):
-        grad_shrink = contract_rows(
-            jnp.concatenate(activations, axis=0), jnp.concatenate(upstream_pieces, axis=0)
-        )
-        grad_shrink = after(grad_shrink, *came[3:4]).astype(bf16)
-    d_mlp_input = after(d_mlp_input, grad_expand, grad_shrink)
+        grad_expand = after(grad_expand, d_attended).astype(bf16)
+    with jax.named_scope("heads"):
+        d_attended = pick(exchange(d_attended), jnp.stack(sources)).reshape(length, own_width)
+        d_attended = after(d_attended, grad_expand)
     with jax.named_scope("grad_expand"):
         grad_expand = reduce_over(grad_expand)
-    with jax.named_scope("grad_shrink"):
-        grad_shrink = reduce_over(grad_shrink).astype(f32)
-    partial_gain_two = jnp.sum(d_mlp_input * normed_second, axis=0)
-    d_residual = upstream.astype(f32) + norm_back(
-        d_mlp_input * gain_two, normed_second, inverse_second
-    )
-
-    with jax.named_scope("heads"):
-        d_residual_low = d_residual.astype(bf16)
-        d_attended = contract_last(d_residual_low, outer).astype(bf16)
-        d_attended = by_place(d_attended.reshape(rows, 1, n_seq, own_width), n_seq)
-        d_attended = exchange_small([take(d_attended, s, 0) for s in sources])
-        d_attended = jnp.concatenate(d_attended)
     with jax.named_scope("attend_back"):
         d_query, d_key, d_value = [], [], []
         for h in range(own_heads):
@@ -463,47 +517,61 @@
             [part.astype(bf16) for part in d_query + d_key + d_value], axis=1
         )
     with jax.named_scope("feed"):
-        feed = multiply(jnp.concatenate(activations, axis=0), shrink)
-        feed = after(feed, d_attended).astype(bf16).reshape(DEPTH, 2, rows, width)
-        feed = add_low(feed[:, 0], across(feed[:, 1]), d_projected)
+        feed_terms = multiply(jnp.concatenate(activations, axis=0), shrink)
+        feed_terms = after(feed_terms, d_residual_low).astype(bf16)
+        feed_terms = feed_terms.reshape(DEPTH, 2, rows, width)
+        feed = add_low(feed_terms[:, 0], across(feed_terms[:, 1]), d_projected)
         output = residual + feed[0].astype(f32)
         for k in range(1, DEPTH):
             output = output + turn(feed[k], k).astype(f32)
+    with jax.named_scope("grad_shrink"):
+        grad_shrink = contract_rows(
+            jnp.concatenate(activations, axis=0), jnp.concatenate(upstream_pieces, axis=0)
+        )
+        grad_shrink = reduce_over(after(grad_shrink, d_projected).astype(bf16))
+    with jax.named_scope("own_expand"):
+        own_expand = exchange(grad_expand.reshape(n_seq, owned, -1))
+    with jax.named_scope("grad_inner"):
+        grad_inner = contract_rows(jnp.concatenate(attend_pieces, axis=0), d_projected)
+        grad_inner_core = reduce_over_cores(grad_inner.astype(bf16))
+        grad_inner = reduce_over_y(grad_inner_core)
+    held = {FAR_FIRST[1]: [grad_inner_core], FAR_FIRST[2]: [feed], FAR_FIRST[3]: [own_expand]}
     gain_terms = [None] * DEPTH
 
     def attend_back(k, earlier):
         term = contract_last(d_projected[2 * rows * k : 2 * rows * (k + 1)], inner)
-        if k == FAR_FIRST[0]:
-            term = after(term, feed)
+        term = after(term, *held.get(k, ()))
         gain_terms[k] = jnp.sum(term * first_norm(token_pieces[k])[0], axis=0)
         return term.astype(bf16)
 
     with jax.named_scope("d_attend_input"):
         d_attend_input, came_last = scatter_rows(attend_back, FAR_FIRST)
+    d_attend_input = after(d_attend_input, output)
     partial_gain_one = sum(gain_terms)
     normed_first, inverse_first = first_norm(inputs_low)
     input_gradient = d_residual + norm_back(d_attend_input * gain_one, normed_first, inverse_first)
 
-    with jax.named_scope("own_expand"):
-        own_expand = exchange(grad_expand.reshape(n_seq, owned, -1))
+    with jax.named_scope("own_inner"):
+        own_inner = exchange(grad_inner.reshape(n_seq, owned, -1))
     with jax.named_scope("grad_outer"):
-        grad_outer = contract_rows(attended_rows, d_residual_low).astype(bf16)
-        grad_outer = reduce_by_hand(grad_outer, came_last[-1])
-        grad_outer = reduce_along_seq(grad_outer, [d_attend_input], [own_expand])
-    grad_inner = contract_rows(jnp.concatenate(attend_pieces, axis=0), d_projected)
-    with jax.named_scope("grad_inner"):
-        grad_inner = reduce_by_hand(grad_inner.astype(bf16), came_last[-1])
+        residual_grads, _ = gather_rows(d_residual_low)
+        grad_outer = contract_rows(
+            attended.reshape(length, own_width), jnp.concatenate(residual_grads, axis=0)
+        )
+        grad_outer = reduce_over_y(reduce_over_cores(grad_outer.astype(bf16)))
+        grad_outer = move(
+            grad_outer, lambda dp, z, x: (z, 2 * x + dp // 2, dp % 2)
+        )
 
     local_squares = sum(
         jnp.sum(jnp.square(grad.astype(f32)))
         for grad in (grad_inner, grad_outer, grad_expand, grad_shrink)
     )
     with jax.named_scope("sums"):
-        sums = sum_everywhere(
-            jnp.concatenate(
-                [partial_gain_one, partial_gain_two, jnp.full((128,), local_squares)]
-            ).reshape(-1, 128)
-        ).reshape(-1)
+        sums = jnp.concatenate(
+            [partial_gain_one, partial_gain_two, jnp.full((128,), local_squares)]
+        )
+        sums = sum_everywhere(after(sums, d_attend_input).reshape(-1, 128)).reshape(-1)
     gains_whole = sums[: 2 * width].reshape(2, width)
     grad_gains = lax.dynamic_slice_in_dim(
         gains_whole, device * norm_gains.shape[1], norm_gains.shape[1], 1
@@ -511,30 +579,12 @@
     global_norm = jnp.sqrt(sums[2 * width] + jnp.sum(gains_whole * gains_whole))
     factor = CLIP / jnp.maximum(global_norm, CLIP)
 
-    with jax.named_scope("own_inner"):
-        grad_inner = exchange(grad_inner.reshape(n_seq, owned, -1))
-    grad_inner = grad_inner.reshape(n_seq, owned, 3, own_width)
-    grad_inner = grad_inner.transpose(1, 2, 0, 3).reshape(inner_weight.shape)
-    grad_expand = own_expand.reshape(n_seq, owned, 2 * n_dp, slab)
-    grad_expand = grad_expand.transpose(1, 2, 0, 3).reshape(expand_weight.shape)
-
-    gradients = (grad_inner, grad_outer, grad_expand, grad_shrink, grad_gains)
-    masters = (inner_weight, outer_weight, expand_weight, shrink_weight, norm_gains)
-    firsts = (first_inner, first_outer, first_expand, first_shrink, first_gains)
-    seconds = (second_inner, second_outer, second_expand, second_shrink, second_gains)
-    decays = (DECAY, DECAY, DECAY, DECAY, 0.0)
-    rates = (RATE, RATE, RATE, RATE, GAIN_RATE)
     results = [
-        adamw(
-            masters[index],
-            gradients[index].astype(f32),
-            firsts[index],
-            seconds[index],
-            factor,
-            decays[index],
-            rates[index],
-        )
-        for index in range(5)
+        adamw_matrix(inner_weight, own_inner, first_inner, second_inner, factor, own_width),
+        adamw_matrix(outer_weight, grad_outer, first_outer, second_outer, factor),
+        adamw_matrix(expand_weight, own_expand, first_expand, second_expand, factor, slab),
+        adamw_matrix(shrink_weight, grad_shrink, first_shrink, second_shrink, factor),
+        adamw(norm_gains, grad_gains, first_gains, second_gains, factor, 0.0, GAIN_RATE),
     ]
     return (
         output[None],

time: 843 us -> 799 us (0.948)
  waiting for transfers between devices: 319 us -> 237 us
  Pallas kernels: 5.37 us -> 49.9 us
  other arithmetic: 107 us -> 87.7 us
    ppermute x82, waiting for transfers between devices: 302 us -> 231 us  [move(): return lax.ppermute(value, BOTH, pairs)]
    pallas_call x0 -> x4, Pallas kernels: none -> 27 us  [adamw_matrix(): pl.pallas_call(adamw_blocks, grid=grid, in_specs=[pl.BlockSpec(memory_spa...]
    sub x5 -> x1, other arithmetic: 18.5 us -> 0.67 us  [adamw(): return (first, second, weight - rate * (update + decay * weight))]
    all_to_all x4 -> x5, starting transfers between devices: 21.7 us -> 37 us  [exchange(): return lax.all_to_all(blocks, 'seq', 0, 0, tiled=True)]
    pallas_call x2 -> x3, Pallas kernels: 4.61 us -> 17.5 us  [pick(): pl.pallas_call(copy_block, grid_spec=pltpu.PrefetchScalarGridSpec(num_sca...]
    slice x22 -> x33, local copies, waits for them, and re-layouts: 16.9 us -> 27.6 us  [nothing(): lax.slice(other, (0,) * other.ndim, (1,) * other.ndim)]
    all_to_all x4 -> x5, waiting for transfers between devices: 16.6 us -> 6.22 us  [exchange(): return lax.all_to_all(blocks, 'seq', 0, 0, tiled=True)]
    unnamed x16 -> x20, other arithmetic: 5.9 us -> 15.5 us
  transfers between devices with their start and end apart: 91 -> 92, of which waited for: 38 -> 37; matrix products, arithmetic and copies ran while one was open for 27% -> 29% of each run, Pallas kernels for 0% -> 5%
where the time goes in v3:
time: 799 us; the launch traced here: 790 us
  waiting for transfers between devices  237 us (30%)
  starting transfers between devices  174 us (22%)
  matrix products  109 us (14%)
  other arithmetic  87.7 us (11%)
  local copies, waits for them, and re-layouts  87.5 us (11%)
  Pallas kernels  49.9 us (6%)
  between operations  44.5 us (6%)
    ppermute x82, waiting for transfers between devices, move(): return lax.ppermute(value, BOTH, pairs)  231 us
    ppermute x82, starting transfers between devices, move(): return lax.ppermute(value, BOTH, pairs)  137 us
    dot_general x17, matrix products, contract_last(): lax.dot_general(left, right, (((1,), (1,)), ((), ())), preferred_element_...  43.4 us
    all_to_all x5, starting transfers between devices, exchange(): return lax.all_to_all(blocks, 'seq', 0, 0, tiled=True)  37 us
    dot_general x14, matrix products, multiply(): return jnp.dot(left, right, preferred_element_type=jnp.float32)  35.6 us
    unnamed x266, local copies, waits for them, and re-layouts  30.1 us
    dot_general x8, matrix products, contract_rows(): lax.dot_general(left, right, (((0,), (0,)), ((), ())), preferred_element_...  29.8 us
    slice x33, local copies, waits for them, and re-layouts, nothing(): lax.slice(other, (0,) * other.ndim, (1,) * other.ndim)  27.6 us
  transfers between devices with their start and end apart: 92, of which 37 were waited for; matrix products, arithmetic and copies ran while one was open for 29% of the time, Pallas kernels for 5%

profile of v3, /device:TPU:0, one launch (start us, length us, event | category | flops | bytes accessed | tf_op | source)
XLA Modules:
  0.0 789.9 jit_solution(2411009996227488556)
XLA Ops:
  17.0 6.0 all-to-all-start
  27.4 5.5 collective-permute-start.6
  41.0 12.4 %collective-permute-done.3 = bf16[192,2048]{1,0:T(8,128)(2,1)} collective-permute-done((bf16[192,2048]{1,0:T(8,128)(2,1)}, bf16[192,2048]{1,0:T(8,128)(2,1)}, u32[]{:S(2)}, u32[]{:S(2)}) %collective-permute-start.3) | collective-permute-done | bytes 786464 | tf_op jit(solution)/shard_map/tokens/ppermute | solution.py:133
  68.6 11.9 %collective-permute-done.7 = bf16[192,2048]{1,0:T(8,128)(2,1)} collective-permute-done((bf16[192,2048]{1,0:T(8,128)(2,1)}, bf16[192,2048]{1,0:T(8,128)(2,1)}, u32[]{:S(2)}, u32[]{:S(2)}) %collective-permute-start.7) | collective-permute-done | bytes 786464 | tf_op jit(solution)/shard_map/tokens/ppermute | solution.py:133
  85.2 9.7 %collective-permute-done.5 = bf16[192,2048]{1,0:T(8,128)(2,1)} collective-permute-done((bf16[192,2048]{1,0:T(8,128)(2,1)}, bf16[192,2048]{1,0:T(8,128)(2,1)}, u32[]{:S(2)}, u32[]{:S(2)}) %collective-permute-start.5) | collective-permute-done | bytes 786464 | tf_op jit(solution)/shard_map/tokens/ppermute | solution.py:133
  101.5 14.5 %collective-permute-done.12 = bf16[192,2048]{1,0:T(8,128)(2,1)} collective-permute-done((bf16[192,2048]{1,0:T(8,128)(2,1)}, bf16[192,2048]{1,0:T(8,128)(2,1)}, u32[]{:S(2)}, u32[]{:S(2)}) %collective-permute-start.12) | collective-permute-done | bytes 786464 | tf_op jit(solution)/shard_map/tokens/ppermute | solution.py:133
  129.6 7.7 collective-permute-done.14
  144.8 6.4 outer.1
  167.9 4.4 all-to-all-start.1
  178.0 5.7 inner.1
  213.5 15.3 %collective-permute-done.18 = bf16[128,256]{1,0:T(8,128)(2,1)S(1)} collective-permute-done((bf16[128,256]{1,0:T(8,128)(2,1)S(1)}, bf16[128,256]{1,0:T(8,128)(2,1)S(1)}, u32[]{:S(2)}, u32[]{:S(2)}) %collective-permute-start.18) | collective-permute-done | bytes 65568 | tf_op jit(solution)/shard_map/rows/ppermute | solution.py:133
  232.3 5.4 rows.1
  243.7 5.0 multiply_reduce_fusion.13
  250.4 5.5 collective-permute-start.24
  255.9 6.2 collective-permute-done.22
  270.8 8.8 %collective-permute-done.25 = bf16[128,2048]{1,0:T(8,128)(2,1)S(1)} collective-permute-done((bf16[128,2048]{1,0:T(8,128)(2,1)S(1)}, bf16[128,2048]{1,0:T(8,128)(2,1)S(1)}, u32[]{:S(2)}, u32[]{:S(2)}) %collective-permute-start.25) | collective-permute-done | bytes 524320 | tf_op jit(solution)/shard_map/mlp_input/ppermute | solution.py:133
  288.8 6.9 collective-permute-done.30
  304.3 4.6 collective-permute-start.36
  319.0 6.5 collective-permute-done.38
  333.1 10.8 %collective-permute-done.39 = bf16[128,2048]{1,0:T(8,128)(2,1)S(1)} collective-permute-done((bf16[128,2048]{1,0:T(8,128)(2,1)S(1)}, bf16[128,2048]{1,0:T(8,128)(2,1)S(1)}, u32[]{:S(2)}, u32[]{:S(2)}) %collective-permute-start.39) | collective-permute-done | bytes 524320 | tf_op jit(solution)/shard_map/cotangent/ppermute | solution.py:133
  349.7 6.2 fusion.40
  375.4 5.1 fusion.59
  388.7 4.3 multiply_convert_fusion.11
  397.9 5.5 collective-permute-start.43
  405.7 5.3 collective-permute-start.48
  412.9 17.1 %collective-permute-done.43 = bf16[128,2048]{1,0:T(8,128)(2,1)S(1)} collective-permute-done((bf16[128,2048]{1,0:T(8,128)(2,1)S(1)}, bf16[128,2048]{1,0:T(8,128)(2,1)S(1)}, u32[]{:S(2)}, u32[]{:S(2)}) %collective-permute-start.43) | collective-permute-done | bytes 524320 | tf_op jit(solution)/shard_map/d_mlp_input/ppermute | solution.py:133
  441.5 15.2 %add_convert_fusion = bf16[2048,2048]{1,0:T(8,128)(2,1)} fusion(f32[]{:T(128)} %bitcast.79, bf16[1024,2048]{1,0:T(8,128)(2,1)} %constant_dynamic-update-slice_fusion.8, bf16[256,1024]{1,0:T(8,128)(2,1)} %copy-done.112, bf16[256,1024]{1,0:T(8,128)(2,1)} %copy-done.111, bf16[256,1024]{1,0:T(8,128)(2,1)} %copy-done.108, bf16[256,1024]{1,0:T(8,128)(2,1)} %copy-done.107, ...), kind=kOutput, calls=%fused_computation | convolution fusion | flops 8631877632 | bytes 16777220 | tf_op jit(solution)/shard_map/grad_expand/dot_general | solution.py:53
  458.9 9.7 %all-to-all-start.2 = ((bf16[8,128,256]{2,1,0:T(8,128)(2,1)}), bf16[8,128,256]{2,1,0:T(8,128)(2,1)}, u32[]{:S(2)}, u32[]{:S(2)}) async-start(bf16[8,128,256]{2,1,0:T(8,128)(2,1)} %bitcast.77), calls=%async_computation.2 | async-start | bytes 1048576 | tf_op jit(solution)/shard_map/heads/all_to_all | solution.py:203
  472.4 5.4 collective-permute-start.64
  478.4 7.3 add_convert_fusion.2
  498.4 5.4 heads.1
  527.0 6.3 add_convert_fusion.1
  533.3 16.0 %collective-permute-done.65 = bf16[128,2048]{1,0:T(8,128)(2,1)} collective-permute-done((bf16[128,2048]{1,0:T(8,128)(2,1)}, bf16[128,2048]{1,0:T(8,128)(2,1)}, u32[]{:S(2)}, u32[]{:S(2)}) %collective-permute-start.65) | collective-permute-done | bytes 524320 | tf_op jit(solution)/shard_map/grad_outer/ppermute | solution.py:133
  559.0 6.1 all-to-all-start.3
  571.6 12.8 %collective-permute-done.68 = bf16[128,2048]{1,0:T(8,128)(2,1)} collective-permute-done((bf16[128,2048]{1,0:T(8,128)(2,1)}, bf16[128,2048]{1,0:T(8,128)(2,1)}, u32[]{:S(2)}, u32[]{:S(2)}) %collective-permute-start.68) | collective-permute-done | bytes 524320 | tf_op jit(solution)/shard_map/grad_outer/ppermute | solution.py:133
  594.4 5.3 collective-permute-done.71
  610.3 6.2 all-to-all-done.3.grad
  618.4 4.4 multiply_reduce_fusion.5
  631.6 5.4 collective-permute-done.73
  645.4 17.0 %collective-permute-done.51 = bf16[128,2048]{1,0:T(8,128)(2,1)} collective-permute-done((bf16[128,2048]{1,0:T(8,128)(2,1)}, bf16[128,2048]{1,0:T(8,128)(2,1)}, u32[]{:S(2)}, u32[]{:S(2)}) %collective-permute-start.51) | collective-permute-done | bytes 524320 | tf_op jit(solution)/shard_map/feed/ppermute | solution.py:133
  672.6 12.6 %collective-permute-start.61 = (bf16[512,768]{1,0:T(8,128)(2,1)S(1)}, bf16[512,768]{1,0:T(8,128)(2,1)S(1)}, u32[]{:S(2)}, u32[]{:S(2)}) collective-permute-start(bf16[512,768]{1,0:T(8,128)(2,1)S(1)} %dynamic-slice_bitcast_fusion.1), channel_id=1, source_target_pairs={{0,16},{1,17},{2,18},{3,19},{4,20},{5,21},{6,22},{7,23},{8,24},{9,... | collective-permute-start | bytes 2359304 | tf_op jit(solution)/shard_map/grad_inner/ppermute | solution.py:133
  687.2 7.2 collective-permute-start.60
  714.6 10.8 %all-to-all-start.4 = ((bf16[8,64,768]{2,1,0:T(8,128)(2,1)}), bf16[8,64,768]{2,1,0:T(8,128)(2,1)}, u32[]{:S(2)}, u32[]{:S(2)}) async-start(bf16[8,64,768]{2,1,0:T(8,128)(2,1)} %bitcast.327), calls=%async_computation.6 | async-start | bytes 1572864 | tf_op jit(solution)/shard_map/own_inner/all_to_all | solution.py:203
  730.0 10.2 %collective-permute-done.78 = f32[33,128]{1,0:T(8,128)S(1)} collective-permute-done((f32[33,128]{1,0:T(8,128)S(1)}, f32[33,128]{1,0:T(8,128)S(1)}, u32[]{:S(2)}, u32[]{:S(2)}) %collective-permute-start.78) | collective-permute-done | bytes 16928 | tf_op jit(solution)/shard_map/sums/ppermute | solution.py:133
  740.2 7.8 collective-permute-done.79
  757.2 6.2 shard_map.325
  763.4 12.2 %shard_map.324 = (f32[64,16384]{1,0:T(8,128)}, f32[64,16384]{1,0:T(8,128)}, f32[64,16384]{1,0:T(8,128)}) custom-call(f32[1]{0:T(128)} %bitcast.119.factor, f32[64,16384]{1,0:T(8,128)} %weight.6, bf16[8,64,2048]{2,1,0:T(8,128)(2,1)} %all-to-all-done.3.grad, f32[64,16384]{1,0:T(8,128)} %first.6, f32[64,16384]{1,0:T(8,128)} %second.6), custom_call_target="tpu_custom_call" | custom-call | flops 20971520 | bytes 27262976 | tf_op jit(solution)/shard_map/pallas_call | solution.py:107
  776.3 5.8 shard_map.322
  (640 shorter events, 347.5 us)
Async XLA Ops:
  7.2 130.2 %all-gather.4.cloned.1.call-start = ((), (), s32[]{:S(2)}) async-start(), calls=%async_computation.7 | async-start | bytes 5242880 | tf_op jit(solution)/shard_map/shrink/all_gather | solution.py:294
  17.0 38.1 %all-to-all-start = ((bf16[8,80,768]{2,1,0:T(8,128)(2,1)}), bf16[8,80,768]{2,1,0:T(8,128)(2,1)}, u32[]{:S(2)}, u32[]{:S(2)}) async-start(bf16[8,80,768]{2,1,0:T(8,128)(2,1)} %pad_maximum_fusion.9), calls=%async_computation | async-start | bytes 1966080 | tf_op jit(solution)/shard_map/inner/all_to_all | solution.py:203
  23.0 215.9 %all-gather.6.cloned.1.call-start = ((), (), s32[]{:S(2)}) async-start(), calls=%async_computation.8 | async-start | bytes 10485760 | tf_op jit(solution)/shard_map/outer/all_gather | solution.py:294
  24.1 29.2 %collective-permute-start.3 = (bf16[192,2048]{1,0:T(8,128)(2,1)}, bf16[192,2048]{1,0:T(8,128)(2,1)}, u32[]{:S(2)}, u32[]{:S(2)}) collective-permute-start(bf16[192,2048]{1,0:T(8,128)(2,1)} %pad_maximum_fusion.10), channel_id=1, source_target_pairs={{0,1},{1,0},{2,3},{3,2},{4,5},{5,4},{6,7},{7,6},{8,9},{9,8},{10,11... | collective-permute-start | bytes 2359304 | tf_op jit(solution)/shard_map/tokens/ppermute | solution.py:133
  26.1 32.5 %collective-permute-start.4 = (bf16[192,2048]{1,0:T(8,128)(2,1)}, bf16[192,2048]{1,0:T(8,128)(2,1)S(1)}, u32[]{:S(2)}, u32[]{:S(2)}) collective-permute-start(bf16[192,2048]{1,0:T(8,128)(2,1)} %pad_maximum_fusion.10), channel_id=1, source_target_pairs={{2,0},{3,1},{4,2},{5,3},{6,4},{7,5},{10,8},{11,9},{12,10},{13,11},... | collective-permute-start | bytes 2359304 | tf_op jit(solution)/shard_map/tokens/ppermute | solution.py:133
  27.4 31.2 %collective-permute-start.6 = (bf16[192,2048]{1,0:T(8,128)(2,1)}, bf16[192,2048]{1,0:T(8,128)(2,1)}, u32[]{:S(2)}, u32[]{:S(2)}) collective-permute-start(bf16[192,2048]{1,0:T(8,128)(2,1)} %pad_maximum_fusion.10), channel_id=1, source_target_pairs={{0,2},{1,3},{2,4},{3,5},{4,6},{5,7},{8,10},{9,11},{10,12},{11,13},... | collective-permute-start | bytes 2359304 | tf_op jit(solution)/shard_map/tokens/ppermute | solution.py:133
  65.8 19.5 %collective-permute-start.10 = (bf16[192,2048]{1,0:T(8,128)(2,1)}, bf16[192,2048]{1,0:T(8,128)(2,1)}, u32[]{:S(2)}, u32[]{:S(2)}) collective-permute-start(bf16[192,2048]{1,0:T(8,128)(2,1)} %get-tuple-element.122), channel_id=1, source_target_pairs={{2,4},{3,5},{4,6},{5,7},{10,12},{11,13},{12,14},{13,15},{18,20},{1... | collective-permute-start | bytes 2359304 | tf_op jit(solution)/shard_map/tokens/ppermute | solution.py:133
  67.3 27.6 %collective-permute-start.5 = (bf16[192,2048]{1,0:T(8,128)(2,1)}, bf16[192,2048]{1,0:T(8,128)(2,1)}, u32[]{:S(2)}, u32[]{:S(2)}) collective-permute-start(bf16[192,2048]{1,0:T(8,128)(2,1)} %get-tuple-element.120), channel_id=1, source_target_pairs={{2,0},{3,1},{4,2},{5,3},{10,8},{11,9},{12,10},{13,11},{18,16},{19,... | collective-permute-start | bytes 2359304 | tf_op jit(solution)/shard_map/tokens/ppermute | solution.py:133
  99.3 19.8 %collective-permute-start.9 = (bf16[192,2048]{1,0:T(8,128)(2,1)}, bf16[192,2048]{1,0:T(8,128)(2,1)S(1)}, u32[]{:S(2)}, u32[]{:S(2)}) collective-permute-start(bf16[192,2048]{1,0:T(8,128)(2,1)} %get-tuple-element.119), channel_id=1, source_target_pairs={{2,0},{3,1},{10,8},{11,9},{18,16},{19,17},{26,24},{27,25}} | collective-permute-start | bytes 2359304 | tf_op jit(solution)/shard_map/tokens/ppermute | solution.py:133
  167.9 71.0 %all-to-all-start.1 = ((bf16[8,64,2048]{2,1,0:T(8,128)(2,1)}), bf16[8,64,2048]{2,1,0:T(8,128)(2,1)}, u32[]{:S(2)}, u32[]{:S(2)}) async-start(bf16[8,64,2048]{2,1,0:T(8,128)(2,1)} %dynamic_update_slice.23), calls=%async_computation.1 | async-start | bytes 4194304 | tf_op jit(solution)/shard_map/expand/all_to_all | solution.py:203
  172.3 177.4 %all-gather.8.cloned.1.call-start = ((), (), s32[]{:S(2)}) async-start(), calls=%async_computation.9 | async-start | bytes 10485760 | tf_op jit(solution)/shard_map/expand/all_gather | solution.py:294
  203.1 25.7 %collective-permute-start.18 = (bf16[128,256]{1,0:T(8,128)(2,1)S(1)}, bf16[128,256]{1,0:T(8,128)(2,1)S(1)}, u32[]{:S(2)}, u32[]{:S(2)}) collective-permute-start(bf16[128,256]{1,0:T(8,128)(2,1)S(1)} %get-tuple-element.141), channel_id=1, source_target_pairs={{0,4},{1,5},{2,6},{3,7},{4,0},{5,1},{6,2},{7,3},{8,12},{9,13},{10,... | collective-permute-start | bytes 196616 | tf_op jit(solution)/shard_map/rows/ppermute | solution.py:133
  205.9 25.6 %collective-permute-start.19 = (bf16[128,256]{1,0:T(8,128)(2,1)S(1)}, bf16[128,256]{1,0:T(8,128)(2,1)S(1)}, u32[]{:S(2)}, u32[]{:S(2)}) collective-permute-start(bf16[128,256]{1,0:T(8,128)(2,1)S(1)} %get-tuple-element.142), channel_id=1, source_target_pairs={{0,5},{1,4},{2,7},{3,6},{4,1},{5,0},{6,3},{7,2},{8,13},{9,12},{10,... | collective-permute-start | bytes 196616 | tf_op jit(solution)/shard_map/rows/ppermute | solution.py:133
  208.0 23.5 %collective-permute-start.20 = (bf16[128,256]{1,0:T(8,128)(2,1)S(1)}, bf16[128,256]{1,0:T(8,128)(2,1)S(1)}, u32[]{:S(2)}, u32[]{:S(2)}) collective-permute-start(bf16[128,256]{1,0:T(8,128)(2,1)S(1)} %get-tuple-element.143), channel_id=1, source_target_pairs={{0,6},{1,7},{2,4},{3,5},{4,2},{5,3},{6,0},{7,1},{8,14},{9,15},{10,... | collective-permute-start | bytes 196616 | tf_op jit(solution)/shard_map/rows/ppermute | solution.py:133
  210.7 20.8 %collective-permute-start.21 = (bf16[128,256]{1,0:T(8,128)(2,1)S(1)}, bf16[128,256]{1,0:T(8,128)(2,1)S(1)}, u32[]{:S(2)}, u32[]{:S(2)}) collective-permute-start(bf16[128,256]{1,0:T(8,128)(2,1)S(1)} %get-tuple-element.137), channel_id=1, source_target_pairs={{0,7},{1,6},{2,5},{3,4},{4,3},{5,2},{6,1},{7,0},{8,15},{9,14},{10,... | collective-permute-start | bytes 196616 | tf_op jit(solution)/shard_map/rows/ppermute | solution.py:133
  243.4 315.6 %reduce-scatter.3.cloned.1.call-start = ((), (), s32[]{:S(2)}) async-start(), calls=%async_computation.10 | async-start | bytes 10485760 | tf_op jit(solution)/shard_map/grad_expand/reduce_scatter | solution.py:317
  332.4 43.0 %collective-permute-start.33 = (bf16[128,2048]{1,0:T(8,128)(2,1)}, bf16[128,2048]{1,0:T(8,128)(2,1)}, u32[]{:S(2)}, u32[]{:S(2)}) collective-permute-start(bf16[128,2048]{1,0:T(8,128)(2,1)} %get-tuple-element.70), channel_id=1, source_target_pairs={{0,1},{1,0},{2,3},{3,2},{4,5},{5,4},{6,7},{7,6},{8,9},{9,8},{10,11... | collective-permute-start | bytes 1572872 | tf_op jit(solution)/shard_map/mlp_input/ppermute | solution.py:133
  348.4 40.4 %collective-permute-start.46 = (bf16[128,2048]{1,0:T(8,128)(2,1)}, bf16[128,2048]{1,0:T(8,128)(2,1)}, u32[]{:S(2)}, u32[]{:S(2)}) collective-permute-start(bf16[128,2048]{1,0:T(8,128)(2,1)} %get-tuple-element.48), channel_id=1, source_target_pairs={{0,1},{1,0},{2,3},{3,2},{4,5},{5,4},{6,7},{7,6},{8,9},{9,8},{10,11... | collective-permute-start | bytes 1572872 | tf_op jit(solution)/shard_map/cotangent/ppermute | solution.py:133
  397.9 32.1 %collective-permute-start.43 = (bf16[128,2048]{1,0:T(8,128)(2,1)S(1)}, bf16[128,2048]{1,0:T(8,128)(2,1)S(1)}, u32[]{:S(2)}, u32[]{:S(2)}) collective-permute-start(bf16[128,2048]{1,0:T(8,128)(2,1)S(1)} %add_convert_fusion.7), channel_id=1, source_target_pairs={{0,4},{1,5},{2,6},{3,7},{4,0},{5,1},{6,2},{7,3},{8,12},{9,13},{10,... | collective-permute-start | bytes 1572872 | tf_op jit(solution)/shard_map/d_mlp_input/ppermute | solution.py:133
  403.5 26.5 %collective-permute-start.42 = (bf16[128,2048]{1,0:T(8,128)(2,1)S(1)}, bf16[128,2048]{1,0:T(8,128)(2,1)S(1)}, u32[]{:S(2)}, u32[]{:S(2)}) collective-permute-start(bf16[128,2048]{1,0:T(8,128)(2,1)S(1)} %add_convert_fusion.8), channel_id=1, source_target_pairs={{0,2},{1,3},{2,0},{3,1},{4,6},{5,7},{6,4},{7,5},{8,10},{9,11},{10,... | collective-permute-start | bytes 1572872 | tf_op jit(solution)/shard_map/d_mlp_input/ppermute | solution.py:133
  405.7 24.3 %collective-permute-start.48 = (bf16[128,2048]{1,0:T(8,128)(2,1)S(1)}, bf16[128,2048]{1,0:T(8,128)(2,1)S(1)}, u32[]{:S(2)}, u32[]{:S(2)}) collective-permute-start(bf16[128,2048]{1,0:T(8,128)(2,1)S(1)} %add_convert_fusion.6), channel_id=1, source_target_pairs={{0,6},{1,7},{2,4},{3,5},{4,2},{5,3},{6,0},{7,1},{8,14},{9,15},{10,... | collective-permute-start | bytes 1572872 | tf_op jit(solution)/shard_map/d_mlp_input/ppermute | solution.py:133
  458.9 39.6 %all-to-all-start.2 = ((bf16[8,128,256]{2,1,0:T(8,128)(2,1)}), bf16[8,128,256]{2,1,0:T(8,128)(2,1)}, u32[]{:S(2)}, u32[]{:S(2)}) async-start(bf16[8,128,256]{2,1,0:T(8,128)(2,1)} %bitcast.77), calls=%async_computation.2 | async-start | bytes 1048576 | tf_op jit(solution)/shard_map/heads/all_to_all | solution.py:203
  468.5 197.6 %reduce-scatter.5.cloned.1.call-start = ((), (), s32[]{:S(2)}) async-start(), calls=%async_computation.11 | async-start | bytes 5242880 | tf_op jit(solution)/shard_map/grad_shrink/reduce_scatter | solution.py:317
  469.1 20.2 %collective-permute-start.62 = (bf16[128,2048]{1,0:T(8,128)(2,1)S(1)}, bf16[128,2048]{1,0:T(8,128)(2,1)S(1)}, u32[]{:S(2)}, u32[]{:S(2)}) collective-permute-start(bf16[128,2048]{1,0:T(8,128)(2,1)S(1)} %copy-done.37), channel_id=1, source_target_pairs={{0,1},{1,0},{2,3},{3,2},{4,5},{5,4},{6,7},{7,6},{8,9},{9,8},{10,11... | collective-permute-start | bytes 1572872 | tf_op jit(solution)/shard_map/grad_outer/ppermute | solution.py:133
  471.1 20.3 %collective-permute-start.63 = (bf16[128,2048]{1,0:T(8,128)(2,1)S(1)}, bf16[128,2048]{1,0:T(8,128)(2,1)}, u32[]{:S(2)}, u32[]{:S(2)}) collective-permute-start(bf16[128,2048]{1,0:T(8,128)(2,1)S(1)} %copy-done.37), channel_id=1, source_target_pairs={{2,0},{3,1},{4,2},{5,3},{6,4},{7,5},{10,8},{11,9},{12,10},{13,11},... | collective-permute-start | bytes 1572872 | tf_op jit(solution)/shard_map/grad_outer/ppermute | solution.py:133
  489.1 101.4 %collective-permute-start.49 = (bf16[4,128,2048]{2,1,0:T(8,128)(2,1)}, bf16[4,128,2048]{2,1,0:T(8,128)(2,1)}, u32[]{:S(2)}, u32[]{:S(2)}) collective-permute-start(bf16[4,128,2048]{2,1,0:T(8,128)(2,1)} %slice_bitcast_fusion), channel_id=1, source_target_pairs={{0,1},{1,0},{2,3},{3,2},{4,5},{5,4},{6,7},{7,6},{8,9},{9,8},{10,11... | collective-permute-start | bytes 6291464 | tf_op jit(solution)/shard_map/feed/ppermute | solution.py:133
  493.6 55.8 %collective-permute-start.65 = (bf16[128,2048]{1,0:T(8,128)(2,1)}, bf16[128,2048]{1,0:T(8,128)(2,1)}, u32[]{:S(2)}, u32[]{:S(2)}) collective-permute-start(bf16[128,2048]{1,0:T(8,128)(2,1)} %get-tuple-element.60), channel_id=1, source_target_pairs={{0,1},{1,0},{2,3},{3,2},{4,5},{5,4},{6,7},{7,6},{8,9},{9,8},{10,11... | collective-permute-start | bytes 1572872 | tf_op jit(solution)/shard_map/grad_outer/ppermute | solution.py:133
  495.5 57.6 %collective-permute-start.66 = (bf16[128,2048]{1,0:T(8,128)(2,1)}, bf16[128,2048]{1,0:T(8,128)(2,1)}, u32[]{:S(2)}, u32[]{:S(2)}) collective-permute-start(bf16[128,2048]{1,0:T(8,128)(2,1)} %collective-permute-done.63), channel_id=1, source_target_pairs={{2,0},{3,1},{4,2},{5,3},{10,8},{11,9},{12,10},{13,11},{18,16},{19,... | collective-permute-start | bytes 1572872 | tf_op jit(solution)/shard_map/grad_outer/ppermute | solution.py:133
  496.8 56.3 %collective-permute-start.67 = (bf16[128,2048]{1,0:T(8,128)(2,1)}, bf16[128,2048]{1,0:T(8,128)(2,1)}, u32[]{:S(2)}, u32[]{:S(2)}) collective-permute-start(bf16[128,2048]{1,0:T(8,128)(2,1)} %collective-permute-done.64), channel_id=1, source_target_pairs={{2,4},{3,5},{4,6},{5,7},{10,12},{11,13},{12,14},{13,15},{18,20},{1... | collective-permute-start | bytes 1572872 | tf_op jit(solution)/shard_map/grad_outer/ppermute | solution.py:133
  526.8 38.9 %collective-permute-start.56 = (bf16[128,2048]{1,0:T(8,128)(2,1)}, bf16[128,2048]{1,0:T(8,128)(2,1)}, u32[]{:S(2)}, u32[]{:S(2)}) collective-permute-start(bf16[128,2048]{1,0:T(8,128)(2,1)} %slice.582), channel_id=1, source_target_pairs={{0,1},{1,0},{2,3},{3,2},{4,5},{5,4},{6,7},{7,6},{8,9},{9,8},{10,11... | collective-permute-start | bytes 1572872 | tf_op jit(solution)/shard_map/d_attend_input/ppermute | solution.py:133
  556.2 28.2 %collective-permute-start.68 = (bf16[128,2048]{1,0:T(8,128)(2,1)}, bf16[128,2048]{1,0:T(8,128)(2,1)}, u32[]{:S(2)}, u32[]{:S(2)}) collective-permute-start(bf16[128,2048]{1,0:T(8,128)(2,1)} %get-tuple-element.58), channel_id=1, source_target_pairs={{0,1},{1,0},{2,3},{3,2},{4,5},{5,4},{6,7},{7,6},{8,9},{9,8},{10,11... | collective-permute-start | bytes 1572872 | tf_op jit(solution)/shard_map/grad_outer/ppermute | solution.py:133
  556.3 31.9 %collective-permute-start.69 = (bf16[128,2048]{1,0:T(8,128)(2,1)}, bf16[128,2048]{1,0:T(8,128)(2,1)}, u32[]{:S(2)}, u32[]{:S(2)}) collective-permute-start(bf16[128,2048]{1,0:T(8,128)(2,1)} %get-tuple-element.123), channel_id=1, source_target_pairs={{2,0},{3,1},{10,8},{11,9},{18,16},{19,17},{26,24},{27,25}} | collective-permute-start | bytes 1572872 | tf_op jit(solution)/shard_map/grad_outer/ppermute | solution.py:133
  557.6 30.6 %collective-permute-start.70 = (bf16[128,2048]{1,0:T(8,128)(2,1)}, bf16[128,2048]{1,0:T(8,128)(2,1)}, u32[]{:S(2)}, u32[]{:S(2)}) collective-permute-start(bf16[128,2048]{1,0:T(8,128)(2,1)} %get-tuple-element.124), channel_id=1, source_target_pairs={{4,6},{5,7},{12,14},{13,15},{20,22},{21,23},{28,30},{29,31}} | collective-permute-start | bytes 1572872 | tf_op jit(solution)/shard_map/grad_outer/ppermute | solution.py:133
  559.0 57.5 %all-to-all-start.3 = ((bf16[8,64,2048]{2,1,0:T(8,128)(2,1)}), bf16[8,64,2048]{2,1,0:T(8,128)(2,1)}, u32[]{:S(2)}, u32[]{:S(2)}) async-start(bf16[8,64,2048]{2,1,0:T(8,128)(2,1)} %bitcast.303), calls=%async_computation.4 | async-start | bytes 4194304 | tf_op jit(solution)/shard_map/own_expand/all_to_all | solution.py:203
  568.1 135.0 %collective-permute-start.57 = (bf16[128,2048]{1,0:T(8,128)(2,1)}, bf16[128,2048]{1,0:T(8,128)(2,1)}, u32[]{:S(2)}, u32[]{:S(2)}) collective-permute-start(bf16[128,2048]{1,0:T(8,128)(2,1)} %add_convert_fusion.4), channel_id=1, source_target_pairs={{0,4},{1,5},{2,6},{3,7},{4,0},{5,1},{6,2},{7,3},{8,12},{9,13},{10,... | collective-permute-start | bytes 1572872 | tf_op jit(solution)/shard_map/d_attend_input/ppermute | solution.py:133
  601.9 24.9 %collective-permute-start.72 = (bf16[2,64,2048]{2,1,0:T(8,128)(2,1)}, bf16[2,64,2048]{2,1,0:T(8,128)(2,1)}, u32[]{:S(2)}, u32[]{:S(2)}) collective-permute-start(bf16[2,64,2048]{2,1,0:T(8,128)(2,1)} %dynamic-slice_bitcast_fusion.2), channel_id=1, source_target_pairs={{0,8},{1,9},{2,10},{3,11},{4,12},{5,13},{6,14},{7,15},{8,0},{9,1},... | collective-permute-start | bytes 1572872 | tf_op jit(solution)/shard_map/grad_outer/ppermute | solution.py:133
  606.2 23.0 %collective-permute-start.54 = (bf16[128,2048]{1,0:T(8,128)(2,1)}, bf16[128,2048]{1,0:T(8,128)(2,1)}, u32[]{:S(2)}, u32[]{:S(2)}) collective-permute-start(bf16[128,2048]{1,0:T(8,128)(2,1)} %slice.579), channel_id=1, source_target_pairs={{0,1},{1,0},{2,3},{3,2},{4,5},{5,4},{6,7},{7,6},{8,9},{9,8},{10,11... | collective-permute-start | bytes 1572872 | tf_op jit(solution)/shard_map/d_attend_input/ppermute | solution.py:133
  607.5 37.0 %collective-permute-start.50 = (bf16[128,2048]{1,0:T(8,128)(2,1)}, bf16[128,2048]{1,0:T(8,128)(2,1)}, u32[]{:S(2)}, u32[]{:S(2)}) collective-permute-start(bf16[128,2048]{1,0:T(8,128)(2,1)} %get-tuple-element.107), channel_id=1, source_target_pairs={{0,2},{1,3},{2,0},{3,1},{4,6},{5,7},{6,4},{7,5},{8,10},{9,11},{10,... | collective-permute-start | bytes 1572872 | tf_op jit(solution)/shard_map/feed/ppermute | solution.py:133
  608.7 53.8 %collective-permute-start.51 = (bf16[128,2048]{1,0:T(8,128)(2,1)}, bf16[128,2048]{1,0:T(8,128)(2,1)}, u32[]{:S(2)}, u32[]{:S(2)}) collective-permute-start(bf16[128,2048]{1,0:T(8,128)(2,1)} %get-tuple-element.109), channel_id=1, source_target_pairs={{0,4},{1,5},{2,6},{3,7},{4,0},{5,1},{6,2},{7,3},{8,12},{9,13},{10,... | collective-permute-start | bytes 1572872 | tf_op jit(solution)/shard_map/feed/ppermute | solution.py:133
  637.0 25.5 %collective-permute-start.52 = (bf16[128,2048]{1,0:T(8,128)(2,1)S(1)}, bf16[128,2048]{1,0:T(8,128)(2,1)S(1)}, u32[]{:S(2)}, u32[]{:S(2)}) collective-permute-start(bf16[128,2048]{1,0:T(8,128)(2,1)S(1)} %copy-done.77), channel_id=1, source_target_pairs={{0,6},{1,7},{2,4},{3,5},{4,2},{5,3},{6,0},{7,1},{8,14},{9,15},{10,... | collective-permute-start | bytes 1572872 | tf_op jit(solution)/shard_map/feed/ppermute | solution.py:133
  638.7 64.4 %collective-permute-start.55 = (bf16[128,2048]{1,0:T(8,128)(2,1)}, bf16[128,2048]{1,0:T(8,128)(2,1)}, u32[]{:S(2)}, u32[]{:S(2)}) collective-permute-start(bf16[128,2048]{1,0:T(8,128)(2,1)} %add_convert_fusion.5), channel_id=1, source_target_pairs={{0,2},{1,3},{2,0},{3,1},{4,6},{5,7},{6,4},{7,5},{8,10},{9,11},{10,... | collective-permute-start | bytes 1572872 | tf_op jit(solution)/shard_map/d_attend_input/ppermute | solution.py:133
  644.5 20.9 %collective-permute-start.74 = (bf16[64,2048]{1,0:T(8,128)(2,1)S(1)}, bf16[64,2048]{1,0:T(8,128)(2,1)S(1)}, u32[]{:S(2)}, u32[]{:S(2)}) collective-permute-start(bf16[64,2048]{1,0:T(8,128)(2,1)S(1)} %fusion.108), channel_id=1, source_target_pairs={{0,0},{1,4},{2,8},{3,12},{4,16},{5,20},{6,24},{7,28},{8,1},{9,5},{... | collective-permute-start | bytes 786440 | tf_op jit(solution)/shard_map/grad_outer/ppermute | solution.py:133
  662.4 22.9 %collective-permute-start.59 = (bf16[128,2048]{1,0:T(8,128)(2,1)}, bf16[128,2048]{1,0:T(8,128)(2,1)}, u32[]{:S(2)}, u32[]{:S(2)}) collective-permute-start(bf16[128,2048]{1,0:T(8,128)(2,1)} %slice.586), channel_id=1, source_target_pairs={{0,1},{1,0},{2,3},{3,2},{4,5},{5,4},{6,7},{7,6},{8,9},{9,8},{10,11... | collective-permute-start | bytes 1572872 | tf_op jit(solution)/shard_map/d_attend_input/ppermute | solution.py:133
  670.5 32.6 %collective-permute-start.53 = (bf16[128,2048]{1,0:T(8,128)(2,1)}, bf16[128,2048]{1,0:T(8,128)(2,1)}, u32[]{:S(2)}, u32[]{:S(2)}) collective-permute-start(bf16[128,2048]{1,0:T(8,128)(2,1)} %slice.575), channel_id=1, source_target_pairs={{0,1},{1,0},{2,3},{3,2},{4,5},{5,4},{6,7},{7,6},{8,9},{9,8},{10,11... | collective-permute-start | bytes 1572872 | tf_op jit(solution)/shard_map/d_attend_input/ppermute | solution.py:133
  672.6 25.9 %collective-permute-start.61 = (bf16[512,768]{1,0:T(8,128)(2,1)S(1)}, bf16[512,768]{1,0:T(8,128)(2,1)S(1)}, u32[]{:S(2)}, u32[]{:S(2)}) collective-permute-start(bf16[512,768]{1,0:T(8,128)(2,1)S(1)} %dynamic-slice_bitcast_fusion.1), channel_id=1, source_target_pairs={{0,16},{1,17},{2,18},{3,19},{4,20},{5,21},{6,22},{7,23},{8,24},{9,... | collective-permute-start | bytes 2359304 | tf_op jit(solution)/shard_map/grad_inner/ppermute | solution.py:133
  687.2 19.5 %collective-permute-start.60 = (bf16[128,2048]{1,0:T(8,128)(2,1)}, bf16[128,2048]{1,0:T(8,128)(2,1)}, u32[]{:S(2)}, u32[]{:S(2)}) collective-permute-start(bf16[128,2048]{1,0:T(8,128)(2,1)} %add_convert_fusion.3), channel_id=1, source_target_pairs={{0,6},{1,7},{2,4},{3,5},{4,2},{5,3},{6,0},{7,1},{8,14},{9,15},{10,... | collective-permute-start | bytes 1572872 | tf_op jit(solution)/shard_map/d_attend_input/ppermute | solution.py:133
  714.6 61.7 %all-to-all-start.4 = ((bf16[8,64,768]{2,1,0:T(8,128)(2,1)}), bf16[8,64,768]{2,1,0:T(8,128)(2,1)}, u32[]{:S(2)}, u32[]{:S(2)}) async-start(bf16[8,64,768]{2,1,0:T(8,128)(2,1)} %bitcast.327), calls=%async_computation.6 | async-start | bytes 1572864 | tf_op jit(solution)/shard_map/own_inner/all_to_all | solution.py:203
  727.5 20.4 %collective-permute-start.79 = (f32[33,128]{1,0:T(8,128)S(1)}, f32[33,128]{1,0:T(8,128)S(1)}, u32[]{:S(2)}, u32[]{:S(2)}) collective-permute-start(f32[33,128]{1,0:T(8,128)S(1)} %add_add_fusion.2), channel_id=1, source_target_pairs={{0,4},{1,5},{2,6},{3,7},{4,0},{5,1},{6,2},{7,3},{8,12},{9,13},{10,... | collective-permute-start | bytes 50696 | tf_op jit(solution)/shard_map/sums/ppermute | solution.py:133
  (163 other events, 1700.4 us)
Sparse Core Ops, SparseCore 0:
  14.1 35.9 all-gather.3
  151.4 55.2 all-gather.5
  243.5 57.4 all-gather.7
  456.9 75.8 reduce-scatter.2
  535.9 44.5 reduce-scatter.4

commit v4 on v3

--- a/solution.py
+++ b/solution.py
@@ -469,7 +469,7 @@
     with jax.named_scope("gate_up"):
         gate_ups = [multiply(piece, expand) for piece in mlp_pieces]
     with jax.named_scope("cotangent"):
-        upstream_pieces, _ = gather_rows(after(upstream, *mlp_pieces[1:]))
+        upstream_pieces, _ = gather_rows(after(upstream, *mlp_pieces[1:]), (), gate_ups[:1])
     activations, gate_up_grads = [None] * DEPTH, [None] * DEPTH
 
     def feed_back(k, earlier):
@@ -551,8 +551,6 @@
     normed_first, inverse_first = first_norm(inputs_low)
     input_gradient = d_residual + norm_back(d_attend_input * gain_one, normed_first, inverse_first)
 
-    with jax.named_scope("own_inner"):
-        own_inner = exchange(grad_inner.reshape(n_seq, owned, -1))
     with jax.named_scope("grad_outer"):
         residual_grads, _ = gather_rows(d_residual_low)
         grad_outer = contract_rows(
@@ -579,6 +577,9 @@
     global_norm = jnp.sqrt(sums[2 * width] + jnp.sum(gains_whole * gains_whole))
     factor = CLIP / jnp.maximum(global_norm, CLIP)
 
+    with jax.named_scope("own_inner"):
+        own_inner = after_in_place(grad_inner, factor)
+        own_inner = exchange(own_inner.reshape(n_seq, owned, -1))
     results = [
         adamw_matrix(inner_weight, own_inner, first_inner, second_inner, factor, own_width),
         adamw_matrix(outer_weight, grad_outer, first_outer, second_outer, factor),

time: 799 us -> 784 us (0.981)
  waiting for transfers between devices: 237 us -> 203 us
    ppermute x82, waiting for transfers between devices: 231 us -> 203 us  [move(): return lax.ppermute(value, BOTH, pairs)]
    ppermute x82, starting transfers between devices: 137 us -> 150 us  [move(): return lax.ppermute(value, BOTH, pairs)]
    slice x33 -> x34, local copies, waits for them, and re-layouts: 27.6 us -> 28.2 us  [nothing(): lax.slice(other, (0,) * other.ndim, (1,) * other.ndim)]
    unnamed x266 -> x260, local copies, waits for them, and re-layouts: 30.1 us -> 29.7 us
  transfers between devices with their start and end apart: 92 -> 92, of which waited for: 37 -> 38; matrix products, arithmetic and copies ran while one was open for 29% -> 31% of each run, Pallas kernels for 5% -> 5%
where the time goes in v4:
time: 784 us; the launch traced here: 775 us
  waiting for transfers between devices  203 us (26%)
  starting transfers between devices  181 us (23%)
  matrix products  112 us (14%)
  other arithmetic  94.2 us (12%)
  local copies, waits for them, and re-layouts  88.9 us (11%)
  Pallas kernels  50 us (6%)
  between operations  46.1 us (6%)
    ppermute x82, waiting for transfers between devices, move(): return lax.ppermute(value, BOTH, pairs)  203 us
    ppermute x82, starting transfers between devices, move(): return lax.ppermute(value, BOTH, pairs)  150 us
    dot_general x17, matrix products, contract_last(): lax.dot_general(left, right, (((1,), (1,)), ((), ())), preferred_element_...  44.1 us
    dot_general x14, matrix products, multiply(): return jnp.dot(left, right, preferred_element_type=jnp.float32)  35.2 us
    dot_general x8, matrix products, contract_rows(): lax.dot_general(left, right, (((0,), (0,)), ((), ())), preferred_element_...  32.3 us
    unnamed x260, local copies, waits for them, and re-layouts  29.7 us
    all_to_all x5, starting transfers between devices, exchange(): return lax.all_to_all(blocks, 'seq', 0, 0, tiled=True)  29.5 us
    slice x34, local copies, waits for them, and re-layouts, nothing(): lax.slice(other, (0,) * other.ndim, (1,) * other.ndim)  28.2 us
  transfers between devices with their start and end apart: 92, of which 38 were waited for; matrix products, arithmetic and copies ran while one was open for 31% of the time, Pallas kernels for 5%

profile of v4, /device:TPU:0, one launch (start us, length us, event | category | flops | bytes accessed | tf_op | source)
XLA Modules:
  0.0 774.5 jit_solution(4336321322593333165)
XLA Ops:
  17.0 6.0 all-to-all-start
  27.4 5.5 collective-permute-start.6
  41.0 12.4 %collective-permute-done.3 = bf16[192,2048]{1,0:T(8,128)(2,1)} collective-permute-done((bf16[192,2048]{1,0:T(8,128)(2,1)}, bf16[192,2048]{1,0:T(8,128)(2,1)}, u32[]{:S(2)}, u32[]{:S(2)}) %collective-permute-start.3) | collective-permute-done | bytes 786464 | tf_op jit(solution)/shard_map/tokens/ppermute | solution.py:133
  68.6 11.9 %collective-permute-done.7 = bf16[192,2048]{1,0:T(8,128)(2,1)} collective-permute-done((bf16[192,2048]{1,0:T(8,128)(2,1)}, bf16[192,2048]{1,0:T(8,128)(2,1)}, u32[]{:S(2)}, u32[]{:S(2)}) %collective-permute-start.7) | collective-permute-done | bytes 786464 | tf_op jit(solution)/shard_map/tokens/ppermute | solution.py:133
  85.2 9.7 %collective-permute-done.5 = bf16[192,2048]{1,0:T(8,128)(2,1)} collective-permute-done((bf16[192,2048]{1,0:T(8,128)(2,1)}, bf16[192,2048]{1,0:T(8,128)(2,1)}, u32[]{:S(2)}, u32[]{:S(2)}) %collective-permute-start.5) | collective-permute-done | bytes 786464 | tf_op jit(solution)/shard_map/tokens/ppermute | solution.py:133
  101.4 14.7 %collective-permute-done.12 = bf16[192,2048]{1,0:T(8,128)(2,1)} collective-permute-done((bf16[192,2048]{1,0:T(8,128)(2,1)}, bf16[192,2048]{1,0:T(8,128)(2,1)}, u32[]{:S(2)}, u32[]{:S(2)}) %collective-permute-start.12) | collective-permute-done | bytes 786464 | tf_op jit(solution)/shard_map/tokens/ppermute | solution.py:133
  129.6 7.7 collective-permute-done.14
  144.8 6.4 outer.1
  167.9 4.4 all-to-all-start.1
  178.0 5.6 inner.1
  213.5 15.3 %collective-permute-done.18 = bf16[128,256]{1,0:T(8,128)(2,1)S(1)} collective-permute-done((bf16[128,256]{1,0:T(8,128)(2,1)S(1)}, bf16[128,256]{1,0:T(8,128)(2,1)S(1)}, u32[]{:S(2)}, u32[]{:S(2)}) %collective-permute-start.18) | collective-permute-done | bytes 65568 | tf_op jit(solution)/shard_map/rows/ppermute | solution.py:133
  232.3 5.4 rows.1
  243.9 5.0 multiply_reduce_fusion.13
  250.6 5.5 collective-permute-start.24
  256.1 6.2 collective-permute-done.22
  271.0 8.8 %collective-permute-done.25 = bf16[128,2048]{1,0:T(8,128)(2,1)S(1)} collective-permute-done((bf16[128,2048]{1,0:T(8,128)(2,1)S(1)}, bf16[128,2048]{1,0:T(8,128)(2,1)S(1)}, u32[]{:S(2)}, u32[]{:S(2)}) %collective-permute-start.25) | collective-permute-done | bytes 524320 | tf_op jit(solution)/shard_map/mlp_input/ppermute | solution.py:133
  289.0 6.9 collective-permute-done.30
  305.3 5.4 collective-permute-start.36
  323.8 9.6 %collective-permute-done.38 = bf16[128,2048]{1,0:T(8,128)(2,1)S(1)} collective-permute-done((bf16[128,2048]{1,0:T(8,128)(2,1)S(1)}, bf16[128,2048]{1,0:T(8,128)(2,1)S(1)}, u32[]{:S(2)}, u32[]{:S(2)}) %collective-permute-start.38) | collective-permute-done | bytes 524320 | tf_op jit(solution)/shard_map/cotangent/ppermute | solution.py:133
  335.5 6.2 fusion.40
  361.7 5.1 fusion.59
  388.2 9.5 %collective-permute-done.46 = bf16[128,2048]{1,0:T(8,128)(2,1)S(1)} collective-permute-done((bf16[128,2048]{1,0:T(8,128)(2,1)S(1)}, bf16[128,2048]{1,0:T(8,128)(2,1)S(1)}, u32[]{:S(2)}, u32[]{:S(2)}) %collective-permute-start.46) | collective-permute-done | bytes 524320 | tf_op jit(solution)/shard_map/cotangent/ppermute | solution.py:133
  397.7 4.8 multiply_convert_fusion.11
  410.0 4.0 collective-permute-start.43
  415.2 6.2 collective-permute-start.48
  423.2 10.5 %collective-permute-done.48 = bf16[128,2048]{1,0:T(8,128)(2,1)S(1)} collective-permute-done((bf16[128,2048]{1,0:T(8,128)(2,1)S(1)}, bf16[128,2048]{1,0:T(8,128)(2,1)S(1)}, u32[]{:S(2)}, u32[]{:S(2)}) %collective-permute-start.48) | collective-permute-done | bytes 524320 | tf_op jit(solution)/shard_map/d_mlp_input/ppermute | solution.py:133
  445.1 15.6 %add_convert_fusion = bf16[2048,2048]{1,0:T(8,128)(2,1)} fusion(f32[]{:T(128)} %bitcast.80, bf16[1024,2048]{1,0:T(8,128)(2,1)} %constant_dynamic-update-slice_fusion.8, bf16[256,1024]{1,0:T(8,128)(2,1)} %copy-done.109, bf16[256,1024]{1,0:T(8,128)(2,1)} %copy-done.108, bf16[256,1024]{1,0:T(8,128)(2,1)} %copy-done.105, bf16[256,1024]{1,0:T(8,128)(2,1)} %copy-done.104, ...), kind=kOutput, calls=%fused_computation | convolution fusion | flops 8631877632 | bytes 16777220 | tf_op jit(solution)/shard_map/grad_expand/dot_general | solution.py:53
  462.8 9.8 %all-to-all-start.2 = ((bf16[8,128,256]{2,1,0:T(8,128)(2,1)}), bf16[8,128,256]{2,1,0:T(8,128)(2,1)}, u32[]{:S(2)}, u32[]{:S(2)}) async-start(bf16[8,128,256]{2,1,0:T(8,128)(2,1)} %bitcast.78), calls=%async_computation.2 | async-start | bytes 1048576 | tf_op jit(solution)/shard_map/heads/all_to_all | solution.py:203
  476.5 5.4 collective-permute-start.64
  482.5 7.3 add_convert_fusion.2
  502.4 5.6 heads.1
  531.1 8.4 %add_convert_fusion.1 = bf16[1024,2048]{1,0:T(8,128)(2,1)} fusion(f32[]{:T(128)} %bitcast.83, bf16[1024,2048]{1,0:T(8,128)(2,1)} %constant_dynamic-update-slice_fusion.25, bf16[256,1024]{1,0:T(8,128)(2,1)S(1)} %copy-done.113, bf16[256,1024]{1,0:T(8,128)(2,1)S(1)} %copy-done.111, bf16[256,1024]{1,0:T(8,128)(2,1)S(1)} %copy-done.112, ...), kind=kOutput, calls=%fused_computation.1 | convolution fusion | flops 4307550208 | bytes 10485764 | tf_op jit(solution)/shard_map/grad_shrink/dot_general | solution.py:53
  539.5 13.6 %collective-permute-done.65 = bf16[128,2048]{1,0:T(8,128)(2,1)} collective-permute-done((bf16[128,2048]{1,0:T(8,128)(2,1)}, bf16[128,2048]{1,0:T(8,128)(2,1)}, u32[]{:S(2)}, u32[]{:S(2)}) %collective-permute-start.65) | collective-permute-done | bytes 524320 | tf_op jit(solution)/shard_map/grad_outer/ppermute | solution.py:133
  565.3 5.0 all-to-all-start.3
  579.2 8.9 %collective-permute-done.69 = bf16[128,2048]{1,0:T(8,128)(2,1)} collective-permute-done((bf16[128,2048]{1,0:T(8,128)(2,1)}, bf16[128,2048]{1,0:T(8,128)(2,1)}, u32[]{:S(2)}, u32[]{:S(2)}) %collective-permute-start.69) | collective-permute-done | bytes 524320 | tf_op jit(solution)/shard_map/grad_outer/ppermute | solution.py:133
  594.4 5.4 collective-permute-done.71
  612.4 4.4 multiply_reduce_fusion.5
  625.2 5.7 collective-permute-done.73
  639.3 10.4 %collective-permute-done.51 = bf16[128,2048]{1,0:T(8,128)(2,1)} collective-permute-done((bf16[128,2048]{1,0:T(8,128)(2,1)}, bf16[128,2048]{1,0:T(8,128)(2,1)}, u32[]{:S(2)}, u32[]{:S(2)}) %collective-permute-start.51) | collective-permute-done | bytes 524320 | tf_op jit(solution)/shard_map/feed/ppermute | solution.py:133
  658.9 8.0 %collective-permute-start.53 = (bf16[128,2048]{1,0:T(8,128)(2,1)}, bf16[128,2048]{1,0:T(8,128)(2,1)}, u32[]{:S(2)}, u32[]{:S(2)}) collective-permute-start(bf16[128,2048]{1,0:T(8,128)(2,1)} %slice.585), channel_id=1, source_target_pairs={{0,1},{1,0},{2,3},{3,2},{4,5},{5,4},{6,7},{7,6},{8,9},{9,8},{10,11... | collective-permute-start | bytes 1572872 | tf_op jit(solution)/shard_map/d_attend_input/ppermute | solution.py:133
  666.9 9.6 %collective-permute-start.61 = (bf16[512,768]{1,0:T(8,128)(2,1)S(1)}, bf16[512,768]{1,0:T(8,128)(2,1)S(1)}, u32[]{:S(2)}, u32[]{:S(2)}) collective-permute-start(bf16[512,768]{1,0:T(8,128)(2,1)S(1)} %dynamic-slice_bitcast_fusion.1), channel_id=1, source_target_pairs={{0,16},{1,17},{2,18},{3,19},{4,20},{5,21},{6,22},{7,23},{8,24},{9,... | collective-permute-start | bytes 2359304 | tf_op jit(solution)/shard_map/grad_inner/ppermute | solution.py:133
  678.6 7.7 collective-permute-start.60
  694.7 4.6 collective-permute-done.60
  709.8 7.5 collective-permute-start.78
  731.7 4.3 all-to-all-start.4
  741.7 6.2 shard_map.325
  747.9 12.2 %shard_map.324 = (f32[64,16384]{1,0:T(8,128)}, f32[64,16384]{1,0:T(8,128)}, f32[64,16384]{1,0:T(8,128)}) custom-call(f32[1]{0:T(128)} %bitcast.120.factor, f32[64,16384]{1,0:T(8,128)} %weight.6, bf16[8,64,2048]{2,1,0:T(8,128)(2,1)} %all-to-all-done.3.grad, f32[64,16384]{1,0:T(8,128)} %first.6, f32[64,16384]{1,0:T(8,128)} %second.6), custom_call_target="tpu_custom_call" | custom-call | flops 20971520 | bytes 27262976 | tf_op jit(solution)/shard_map/pallas_call | solution.py:107
  760.8 5.8 shard_map.322
  (637 shorter events, 358.4 us)
Async XLA Ops:
  7.2 130.2 %all-gather.4.cloned.1.call-start = ((), (), s32[]{:S(2)}) async-start(), calls=%async_computation.7 | async-start | bytes 5242880 | tf_op jit(solution)/shard_map/shrink/all_gather | solution.py:294
  17.0 38.2 %all-to-all-start = ((bf16[8,80,768]{2,1,0:T(8,128)(2,1)}), bf16[8,80,768]{2,1,0:T(8,128)(2,1)}, u32[]{:S(2)}, u32[]{:S(2)}) async-start(bf16[8,80,768]{2,1,0:T(8,128)(2,1)} %pad_maximum_fusion.9), calls=%async_computation | async-start | bytes 1966080 | tf_op jit(solution)/shard_map/inner/all_to_all | solution.py:203
  23.0 215.9 %all-gather.6.cloned.1.call-start = ((), (), s32[]{:S(2)}) async-start(), calls=%async_computation.8 | async-start | bytes 10485760 | tf_op jit(solution)/shard_map/outer/all_gather | solution.py:294
  24.1 29.2 %collective-permute-start.3 = (bf16[192,2048]{1,0:T(8,128)(2,1)}, bf16[192,2048]{1,0:T(8,128)(2,1)}, u32[]{:S(2)}, u32[]{:S(2)}) collective-permute-start(bf16[192,2048]{1,0:T(8,128)(2,1)} %pad_maximum_fusion.10), channel_id=1, source_target_pairs={{0,1},{1,0},{2,3},{3,2},{4,5},{5,4},{6,7},{7,6},{8,9},{9,8},{10,11... | collective-permute-start | bytes 2359304 | tf_op jit(solution)/shard_map/tokens/ppermute | solution.py:133
  26.1 32.5 %collective-permute-start.4 = (bf16[192,2048]{1,0:T(8,128)(2,1)}, bf16[192,2048]{1,0:T(8,128)(2,1)S(1)}, u32[]{:S(2)}, u32[]{:S(2)}) collective-permute-start(bf16[192,2048]{1,0:T(8,128)(2,1)} %pad_maximum_fusion.10), channel_id=1, source_target_pairs={{2,0},{3,1},{4,2},{5,3},{6,4},{7,5},{10,8},{11,9},{12,10},{13,11},... | collective-permute-start | bytes 2359304 | tf_op jit(solution)/shard_map/tokens/ppermute | solution.py:133
  27.4 31.2 %collective-permute-start.6 = (bf16[192,2048]{1,0:T(8,128)(2,1)}, bf16[192,2048]{1,0:T(8,128)(2,1)}, u32[]{:S(2)}, u32[]{:S(2)}) collective-permute-start(bf16[192,2048]{1,0:T(8,128)(2,1)} %pad_maximum_fusion.10), channel_id=1, source_target_pairs={{0,2},{1,3},{2,4},{3,5},{4,6},{5,7},{8,10},{9,11},{10,12},{11,13},... | collective-permute-start | bytes 2359304 | tf_op jit(solution)/shard_map/tokens/ppermute | solution.py:133
  65.8 19.5 %collective-permute-start.10 = (bf16[192,2048]{1,0:T(8,128)(2,1)}, bf16[192,2048]{1,0:T(8,128)(2,1)}, u32[]{:S(2)}, u32[]{:S(2)}) collective-permute-start(bf16[192,2048]{1,0:T(8,128)(2,1)} %get-tuple-element.122), channel_id=1, source_target_pairs={{2,4},{3,5},{4,6},{5,7},{10,12},{11,13},{12,14},{13,15},{18,20},{1... | collective-permute-start | bytes 2359304 | tf_op jit(solution)/shard_map/tokens/ppermute | solution.py:133
  67.3 27.6 %collective-permute-start.5 = (bf16[192,2048]{1,0:T(8,128)(2,1)}, bf16[192,2048]{1,0:T(8,128)(2,1)}, u32[]{:S(2)}, u32[]{:S(2)}) collective-permute-start(bf16[192,2048]{1,0:T(8,128)(2,1)} %get-tuple-element.120), channel_id=1, source_target_pairs={{2,0},{3,1},{4,2},{5,3},{10,8},{11,9},{12,10},{13,11},{18,16},{19,... | collective-permute-start | bytes 2359304 | tf_op jit(solution)/shard_map/tokens/ppermute | solution.py:133
  98.6 19.4 %collective-permute-start.11 = (bf16[192,2048]{1,0:T(8,128)(2,1)}, bf16[192,2048]{1,0:T(8,128)(2,1)S(1)}, u32[]{:S(2)}, u32[]{:S(2)}) collective-permute-start(bf16[192,2048]{1,0:T(8,128)(2,1)} %get-tuple-element.118), channel_id=1, source_target_pairs={{4,6},{5,7},{12,14},{13,15},{20,22},{21,23},{28,30},{29,31}} | collective-permute-start | bytes 2359304 | tf_op jit(solution)/shard_map/tokens/ppermute | solution.py:133
  99.3 19.8 %collective-permute-start.9 = (bf16[192,2048]{1,0:T(8,128)(2,1)}, bf16[192,2048]{1,0:T(8,128)(2,1)S(1)}, u32[]{:S(2)}, u32[]{:S(2)}) collective-permute-start(bf16[192,2048]{1,0:T(8,128)(2,1)} %get-tuple-element.119), channel_id=1, source_target_pairs={{2,0},{3,1},{10,8},{11,9},{18,16},{19,17},{26,24},{27,25}} | collective-permute-start | bytes 2359304 | tf_op jit(solution)/shard_map/tokens/ppermute | solution.py:133
  167.9 71.0 %all-to-all-start.1 = ((bf16[8,64,2048]{2,1,0:T(8,128)(2,1)}), bf16[8,64,2048]{2,1,0:T(8,128)(2,1)}, u32[]{:S(2)}, u32[]{:S(2)}) async-start(bf16[8,64,2048]{2,1,0:T(8,128)(2,1)} %dynamic_update_slice.26), calls=%async_computation.1 | async-start | bytes 4194304 | tf_op jit(solution)/shard_map/expand/all_to_all | solution.py:203
  172.3 163.2 %all-gather.8.cloned.1.call-start = ((), (), s32[]{:S(2)}) async-start(), calls=%async_computation.9 | async-start | bytes 10485760 | tf_op jit(solution)/shard_map/expand/all_gather | solution.py:294
  203.1 25.6 %collective-permute-start.18 = (bf16[128,256]{1,0:T(8,128)(2,1)S(1)}, bf16[128,256]{1,0:T(8,128)(2,1)S(1)}, u32[]{:S(2)}, u32[]{:S(2)}) collective-permute-start(bf16[128,256]{1,0:T(8,128)(2,1)S(1)} %get-tuple-element.141), channel_id=1, source_target_pairs={{0,4},{1,5},{2,6},{3,7},{4,0},{5,1},{6,2},{7,3},{8,12},{9,13},{10,... | collective-permute-start | bytes 196616 | tf_op jit(solution)/shard_map/rows/ppermute | solution.py:133
  205.9 25.6 %collective-permute-start.19 = (bf16[128,256]{1,0:T(8,128)(2,1)S(1)}, bf16[128,256]{1,0:T(8,128)(2,1)S(1)}, u32[]{:S(2)}, u32[]{:S(2)}) collective-permute-start(bf16[128,256]{1,0:T(8,128)(2,1)S(1)} %get-tuple-element.142), channel_id=1, source_target_pairs={{0,5},{1,4},{2,7},{3,6},{4,1},{5,0},{6,3},{7,2},{8,13},{9,12},{10,... | collective-permute-start | bytes 196616 | tf_op jit(solution)/shard_map/rows/ppermute | solution.py:133
  208.0 23.5 %collective-permute-start.20 = (bf16[128,256]{1,0:T(8,128)(2,1)S(1)}, bf16[128,256]{1,0:T(8,128)(2,1)S(1)}, u32[]{:S(2)}, u32[]{:S(2)}) collective-permute-start(bf16[128,256]{1,0:T(8,128)(2,1)S(1)} %get-tuple-element.143), channel_id=1, source_target_pairs={{0,6},{1,7},{2,4},{3,5},{4,2},{5,3},{6,0},{7,1},{8,14},{9,15},{10,... | collective-permute-start | bytes 196616 | tf_op jit(solution)/shard_map/rows/ppermute | solution.py:133
  210.8 20.7 %collective-permute-start.21 = (bf16[128,256]{1,0:T(8,128)(2,1)S(1)}, bf16[128,256]{1,0:T(8,128)(2,1)S(1)}, u32[]{:S(2)}, u32[]{:S(2)}) collective-permute-start(bf16[128,256]{1,0:T(8,128)(2,1)S(1)} %get-tuple-element.137), channel_id=1, source_target_pairs={{0,7},{1,6},{2,5},{3,4},{4,3},{5,2},{6,1},{7,0},{8,15},{9,14},{10,... | collective-permute-start | bytes 196616 | tf_op jit(solution)/shard_map/rows/ppermute | solution.py:133
  243.4 321.9 %reduce-scatter.3.cloned.1.call-start = ((), (), s32[]{:S(2)}) async-start(), calls=%async_computation.10 | async-start | bytes 10485760 | tf_op jit(solution)/shard_map/grad_expand/reduce_scatter | solution.py:317
  319.8 42.0 %collective-permute-start.33 = (bf16[128,2048]{1,0:T(8,128)(2,1)}, bf16[128,2048]{1,0:T(8,128)(2,1)}, u32[]{:S(2)}, u32[]{:S(2)}) collective-permute-start(bf16[128,2048]{1,0:T(8,128)(2,1)} %get-tuple-element.70), channel_id=1, source_target_pairs={{0,1},{1,0},{2,3},{3,2},{4,5},{5,4},{6,7},{7,6},{8,9},{9,8},{10,11... | collective-permute-start | bytes 1572872 | tf_op jit(solution)/shard_map/mlp_input/ppermute | solution.py:133
  321.1 29.5 %collective-permute-start.35 = (bf16[128,2048]{1,0:T(8,128)(2,1)}, bf16[128,2048]{1,0:T(8,128)(2,1)}, u32[]{:S(2)}, u32[]{:S(2)}) collective-permute-start(bf16[128,2048]{1,0:T(8,128)(2,1)} %collective-permute-done.34), channel_id=1, source_target_pairs={{2,0},{3,1},{4,2},{5,3},{10,8},{11,9},{12,10},{13,11},{18,16},{19,... | collective-permute-start | bytes 1572872 | tf_op jit(solution)/shard_map/cotangent/ppermute | solution.py:133
  322.4 28.2 %collective-permute-start.37 = (bf16[128,2048]{1,0:T(8,128)(2,1)}, bf16[128,2048]{1,0:T(8,128)(2,1)}, u32[]{:S(2)}, u32[]{:S(2)}) collective-permute-start(bf16[128,2048]{1,0:T(8,128)(2,1)} %collective-permute-done.36), channel_id=1, source_target_pairs={{2,4},{3,5},{4,6},{5,7},{10,12},{11,13},{12,14},{13,15},{18,20},{1... | collective-permute-start | bytes 1572872 | tf_op jit(solution)/shard_map/cotangent/ppermute | solution.py:133
  348.3 23.5 %collective-permute-start.32 = (bf16[128,2048]{1,0:T(8,128)(2,1)S(1)}, bf16[128,2048]{1,0:T(8,128)(2,1)S(1)}, u32[]{:S(2)}, u32[]{:S(2)}) collective-permute-start(bf16[128,2048]{1,0:T(8,128)(2,1)S(1)} %slice.543), channel_id=1, source_target_pairs={{0,1},{1,0},{2,3},{3,2},{4,5},{5,4},{6,7},{7,6},{8,9},{9,8},{10,11... | collective-permute-start | bytes 1572872 | tf_op jit(solution)/shard_map/d_mlp_input/ppermute | solution.py:133
  354.5 21.7 %collective-permute-start.44 = (bf16[128,2048]{1,0:T(8,128)(2,1)S(1)}, bf16[128,2048]{1,0:T(8,128)(2,1)S(1)}, u32[]{:S(2)}, u32[]{:S(2)}) collective-permute-start(bf16[128,2048]{1,0:T(8,128)(2,1)S(1)} %get-tuple-element.133), channel_id=1, source_target_pairs={{2,0},{3,1},{10,8},{11,9},{18,16},{19,17},{26,24},{27,25}} | collective-permute-start | bytes 1572872 | tf_op jit(solution)/shard_map/cotangent/ppermute | solution.py:133
  355.8 20.4 %collective-permute-start.45 = (bf16[128,2048]{1,0:T(8,128)(2,1)S(1)}, bf16[128,2048]{1,0:T(8,128)(2,1)S(1)}, u32[]{:S(2)}, u32[]{:S(2)}) collective-permute-start(bf16[128,2048]{1,0:T(8,128)(2,1)S(1)} %get-tuple-element.134), channel_id=1, source_target_pairs={{4,6},{5,7},{12,14},{13,15},{20,22},{21,23},{28,30},{29,31}} | collective-permute-start | bytes 1572872 | tf_op jit(solution)/shard_map/cotangent/ppermute | solution.py:133
  378.4 19.3 %collective-permute-start.46 = (bf16[128,2048]{1,0:T(8,128)(2,1)S(1)}, bf16[128,2048]{1,0:T(8,128)(2,1)S(1)}, u32[]{:S(2)}, u32[]{:S(2)}) collective-permute-start(bf16[128,2048]{1,0:T(8,128)(2,1)S(1)} %get-tuple-element.48), channel_id=1, source_target_pairs={{0,1},{1,0},{2,3},{3,2},{4,5},{5,4},{6,7},{7,6},{8,9},{9,8},{10,11... | collective-permute-start | bytes 1572872 | tf_op jit(solution)/shard_map/cotangent/ppermute | solution.py:133
  384.9 21.8 %collective-permute-start.41 = (bf16[128,2048]{1,0:T(8,128)(2,1)S(1)}, bf16[128,2048]{1,0:T(8,128)(2,1)S(1)}, u32[]{:S(2)}, u32[]{:S(2)}) collective-permute-start(bf16[128,2048]{1,0:T(8,128)(2,1)S(1)} %slice.556), channel_id=1, source_target_pairs={{0,1},{1,0},{2,3},{3,2},{4,5},{5,4},{6,7},{7,6},{8,9},{9,8},{10,11... | collective-permute-start | bytes 1572872 | tf_op jit(solution)/shard_map/d_mlp_input/ppermute | solution.py:133
  462.8 39.5 %all-to-all-start.2 = ((bf16[8,128,256]{2,1,0:T(8,128)(2,1)}), bf16[8,128,256]{2,1,0:T(8,128)(2,1)}, u32[]{:S(2)}, u32[]{:S(2)}) async-start(bf16[8,128,256]{2,1,0:T(8,128)(2,1)} %bitcast.78), calls=%async_computation.2 | async-start | bytes 1048576 | tf_op jit(solution)/shard_map/heads/all_to_all | solution.py:203
  472.6 181.9 %reduce-scatter.5.cloned.1.call-start = ((), (), s32[]{:S(2)}) async-start(), calls=%async_computation.11 | async-start | bytes 5242880 | tf_op jit(solution)/shard_map/grad_shrink/reduce_scatter | solution.py:317
  473.2 20.3 %collective-permute-start.62 = (bf16[128,2048]{1,0:T(8,128)(2,1)S(1)}, bf16[128,2048]{1,0:T(8,128)(2,1)S(1)}, u32[]{:S(2)}, u32[]{:S(2)}) collective-permute-start(bf16[128,2048]{1,0:T(8,128)(2,1)S(1)} %copy-done.37), channel_id=1, source_target_pairs={{0,1},{1,0},{2,3},{3,2},{4,5},{5,4},{6,7},{7,6},{8,9},{9,8},{10,11... | collective-permute-start | bytes 1572872 | tf_op jit(solution)/shard_map/grad_outer/ppermute | solution.py:133
  475.2 20.3 %collective-permute-start.63 = (bf16[128,2048]{1,0:T(8,128)(2,1)S(1)}, bf16[128,2048]{1,0:T(8,128)(2,1)}, u32[]{:S(2)}, u32[]{:S(2)}) collective-permute-start(bf16[128,2048]{1,0:T(8,128)(2,1)S(1)} %copy-done.37), channel_id=1, source_target_pairs={{2,0},{3,1},{4,2},{5,3},{6,4},{7,5},{10,8},{11,9},{12,10},{13,11},... | collective-permute-start | bytes 1572872 | tf_op jit(solution)/shard_map/grad_outer/ppermute | solution.py:133
  476.5 19.0 %collective-permute-start.64 = (bf16[128,2048]{1,0:T(8,128)(2,1)S(1)}, bf16[128,2048]{1,0:T(8,128)(2,1)}, u32[]{:S(2)}, u32[]{:S(2)}) collective-permute-start(bf16[128,2048]{1,0:T(8,128)(2,1)S(1)} %copy-done.37), channel_id=1, source_target_pairs={{0,2},{1,3},{2,4},{3,5},{4,6},{5,7},{8,10},{9,11},{10,12},{11,13},... | collective-permute-start | bytes 1572872 | tf_op jit(solution)/shard_map/grad_outer/ppermute | solution.py:133
  493.3 97.2 %collective-permute-start.49 = (bf16[4,128,2048]{2,1,0:T(8,128)(2,1)}, bf16[4,128,2048]{2,1,0:T(8,128)(2,1)}, u32[]{:S(2)}, u32[]{:S(2)}) collective-permute-start(bf16[4,128,2048]{2,1,0:T(8,128)(2,1)} %slice_bitcast_fusion), channel_id=1, source_target_pairs={{0,1},{1,0},{2,3},{3,2},{4,5},{5,4},{6,7},{7,6},{8,9},{9,8},{10,11... | collective-permute-start | bytes 6291464 | tf_op jit(solution)/shard_map/feed/ppermute | solution.py:133
  497.7 55.4 %collective-permute-start.65 = (bf16[128,2048]{1,0:T(8,128)(2,1)}, bf16[128,2048]{1,0:T(8,128)(2,1)}, u32[]{:S(2)}, u32[]{:S(2)}) collective-permute-start(bf16[128,2048]{1,0:T(8,128)(2,1)} %get-tuple-element.60), channel_id=1, source_target_pairs={{0,1},{1,0},{2,3},{3,2},{4,5},{5,4},{6,7},{7,6},{8,9},{9,8},{10,11... | collective-permute-start | bytes 1572872 | tf_op jit(solution)/shard_map/grad_outer/ppermute | solution.py:133
  499.6 57.2 %collective-permute-start.66 = (bf16[128,2048]{1,0:T(8,128)(2,1)}, bf16[128,2048]{1,0:T(8,128)(2,1)}, u32[]{:S(2)}, u32[]{:S(2)}) collective-permute-start(bf16[128,2048]{1,0:T(8,128)(2,1)} %collective-permute-done.63), channel_id=1, source_target_pairs={{2,0},{3,1},{4,2},{5,3},{10,8},{11,9},{12,10},{13,11},{18,16},{19,... | collective-permute-start | bytes 1572872 | tf_op jit(solution)/shard_map/grad_outer/ppermute | solution.py:133
  500.9 56.0 %collective-permute-start.67 = (bf16[128,2048]{1,0:T(8,128)(2,1)}, bf16[128,2048]{1,0:T(8,128)(2,1)}, u32[]{:S(2)}, u32[]{:S(2)}) collective-permute-start(bf16[128,2048]{1,0:T(8,128)(2,1)} %collective-permute-done.64), channel_id=1, source_target_pairs={{2,4},{3,5},{4,6},{5,7},{10,12},{11,13},{12,14},{13,15},{18,20},{1... | collective-permute-start | bytes 1572872 | tf_op jit(solution)/shard_map/grad_outer/ppermute | solution.py:133
  530.9 39.4 %collective-permute-start.56 = (bf16[128,2048]{1,0:T(8,128)(2,1)}, bf16[128,2048]{1,0:T(8,128)(2,1)}, u32[]{:S(2)}, u32[]{:S(2)}) collective-permute-start(bf16[128,2048]{1,0:T(8,128)(2,1)} %slice.592), channel_id=1, source_target_pairs={{0,1},{1,0},{2,3},{3,2},{4,5},{5,4},{6,7},{7,6},{8,9},{9,8},{10,11... | collective-permute-start | bytes 1572872 | tf_op jit(solution)/shard_map/d_attend_input/ppermute | solution.py:133
  562.5 25.6 %collective-permute-start.69 = (bf16[128,2048]{1,0:T(8,128)(2,1)}, bf16[128,2048]{1,0:T(8,128)(2,1)}, u32[]{:S(2)}, u32[]{:S(2)}) collective-permute-start(bf16[128,2048]{1,0:T(8,128)(2,1)} %get-tuple-element.123), channel_id=1, source_target_pairs={{2,0},{3,1},{10,8},{11,9},{18,16},{19,17},{26,24},{27,25}} | collective-permute-start | bytes 1572872 | tf_op jit(solution)/shard_map/grad_outer/ppermute | solution.py:133
  563.8 24.3 %collective-permute-start.70 = (bf16[128,2048]{1,0:T(8,128)(2,1)}, bf16[128,2048]{1,0:T(8,128)(2,1)}, u32[]{:S(2)}, u32[]{:S(2)}) collective-permute-start(bf16[128,2048]{1,0:T(8,128)(2,1)} %get-tuple-element.124), channel_id=1, source_target_pairs={{4,6},{5,7},{12,14},{13,15},{20,22},{21,23},{28,30},{29,31}} | collective-permute-start | bytes 1572872 | tf_op jit(solution)/shard_map/grad_outer/ppermute | solution.py:133
  565.3 45.2 %all-to-all-start.3 = ((bf16[8,64,2048]{2,1,0:T(8,128)(2,1)}), bf16[8,64,2048]{2,1,0:T(8,128)(2,1)}, u32[]{:S(2)}, u32[]{:S(2)}) async-start(bf16[8,64,2048]{2,1,0:T(8,128)(2,1)} %bitcast.304), calls=%async_computation.4 | async-start | bytes 4194304 | tf_op jit(solution)/shard_map/own_expand/all_to_all | solution.py:203
  572.6 122.1 %collective-permute-start.57 = (bf16[128,2048]{1,0:T(8,128)(2,1)}, bf16[128,2048]{1,0:T(8,128)(2,1)}, u32[]{:S(2)}, u32[]{:S(2)}) collective-permute-start(bf16[128,2048]{1,0:T(8,128)(2,1)} %add_convert_fusion.4), channel_id=1, source_target_pairs={{0,4},{1,5},{2,6},{3,7},{4,0},{5,1},{6,2},{7,3},{8,12},{9,13},{10,... | collective-permute-start | bytes 1572872 | tf_op jit(solution)/shard_map/d_attend_input/ppermute | solution.py:133
  607.5 30.7 %collective-permute-start.50 = (bf16[128,2048]{1,0:T(8,128)(2,1)}, bf16[128,2048]{1,0:T(8,128)(2,1)}, u32[]{:S(2)}, u32[]{:S(2)}) collective-permute-start(bf16[128,2048]{1,0:T(8,128)(2,1)} %get-tuple-element.107), channel_id=1, source_target_pairs={{0,2},{1,3},{2,0},{3,1},{4,6},{5,7},{6,4},{7,5},{8,10},{9,11},{10,... | collective-permute-start | bytes 1572872 | tf_op jit(solution)/shard_map/feed/ppermute | solution.py:133
  607.6 42.1 %collective-permute-start.51 = (bf16[128,2048]{1,0:T(8,128)(2,1)}, bf16[128,2048]{1,0:T(8,128)(2,1)}, u32[]{:S(2)}, u32[]{:S(2)}) collective-permute-start(bf16[128,2048]{1,0:T(8,128)(2,1)} %get-tuple-element.109), channel_id=1, source_target_pairs={{0,4},{1,5},{2,6},{3,7},{4,0},{5,1},{6,2},{7,3},{8,12},{9,13},{10,... | collective-permute-start | bytes 1572872 | tf_op jit(solution)/shard_map/feed/ppermute | solution.py:133
  630.9 19.9 %collective-permute-start.52 = (bf16[128,2048]{1,0:T(8,128)(2,1)S(1)}, bf16[128,2048]{1,0:T(8,128)(2,1)S(1)}, u32[]{:S(2)}, u32[]{:S(2)}) collective-permute-start(bf16[128,2048]{1,0:T(8,128)(2,1)S(1)} %copy-done.76), channel_id=1, source_target_pairs={{0,6},{1,7},{2,4},{3,5},{4,2},{5,3},{6,0},{7,1},{8,14},{9,15},{10,... | collective-permute-start | bytes 1572872 | tf_op jit(solution)/shard_map/feed/ppermute | solution.py:133
  632.5 62.2 %collective-permute-start.55 = (bf16[128,2048]{1,0:T(8,128)(2,1)}, bf16[128,2048]{1,0:T(8,128)(2,1)}, u32[]{:S(2)}, u32[]{:S(2)}) collective-permute-start(bf16[128,2048]{1,0:T(8,128)(2,1)} %add_convert_fusion.5), channel_id=1, source_target_pairs={{0,2},{1,3},{2,0},{3,1},{4,6},{5,7},{6,4},{7,5},{8,10},{9,11},{10,... | collective-permute-start | bytes 1572872 | tf_op jit(solution)/shard_map/d_attend_input/ppermute | solution.py:133
  649.7 26.9 %collective-permute-start.59 = (bf16[128,2048]{1,0:T(8,128)(2,1)}, bf16[128,2048]{1,0:T(8,128)(2,1)}, u32[]{:S(2)}, u32[]{:S(2)}) collective-permute-start(bf16[128,2048]{1,0:T(8,128)(2,1)} %slice.596), channel_id=1, source_target_pairs={{0,1},{1,0},{2,3},{3,2},{4,5},{5,4},{6,7},{7,6},{8,9},{9,8},{10,11... | collective-permute-start | bytes 1572872 | tf_op jit(solution)/shard_map/d_attend_input/ppermute | solution.py:133
  658.9 35.7 %collective-permute-start.53 = (bf16[128,2048]{1,0:T(8,128)(2,1)}, bf16[128,2048]{1,0:T(8,128)(2,1)}, u32[]{:S(2)}, u32[]{:S(2)}) collective-permute-start(bf16[128,2048]{1,0:T(8,128)(2,1)} %slice.585), channel_id=1, source_target_pairs={{0,1},{1,0},{2,3},{3,2},{4,5},{5,4},{6,7},{7,6},{8,9},{9,8},{10,11... | collective-permute-start | bytes 1572872 | tf_op jit(solution)/shard_map/d_attend_input/ppermute | solution.py:133
  666.9 23.1 %collective-permute-start.61 = (bf16[512,768]{1,0:T(8,128)(2,1)S(1)}, bf16[512,768]{1,0:T(8,128)(2,1)S(1)}, u32[]{:S(2)}, u32[]{:S(2)}) collective-permute-start(bf16[512,768]{1,0:T(8,128)(2,1)S(1)} %dynamic-slice_bitcast_fusion.1), channel_id=1, source_target_pairs={{0,16},{1,17},{2,18},{3,19},{4,20},{5,21},{6,22},{7,23},{8,24},{9,... | collective-permute-start | bytes 2359304 | tf_op jit(solution)/shard_map/grad_inner/ppermute | solution.py:133
  678.6 20.7 %collective-permute-start.60 = (bf16[128,2048]{1,0:T(8,128)(2,1)}, bf16[128,2048]{1,0:T(8,128)(2,1)}, u32[]{:S(2)}, u32[]{:S(2)}) collective-permute-start(bf16[128,2048]{1,0:T(8,128)(2,1)} %add_convert_fusion.3), channel_id=1, source_target_pairs={{0,6},{1,7},{2,4},{3,5},{4,2},{5,3},{6,0},{7,1},{8,14},{9,15},{10,... | collective-permute-start | bytes 1572872 | tf_op jit(solution)/shard_map/d_attend_input/ppermute | solution.py:133
  731.7 29.1 %all-to-all-start.4 = ((bf16[8,64,768]{2,1,0:T(8,128)(2,1)}), bf16[8,64,768]{2,1,0:T(8,128)(2,1)}, u32[]{:S(2)}, u32[]{:S(2)}) async-start(bf16[8,64,768]{2,1,0:T(8,128)(2,1)} %bitcast.328), calls=%async_computation.6 | async-start | bytes 1572864 | tf_op jit(solution)/shard_map/own_inner/all_to_all | solution.py:203
  (160 other events, 1616.0 us)
Sparse Core Ops, SparseCore 0:
  14.1 35.9 all-gather.3
  151.4 55.2 all-gather.5
  243.5 57.4 all-gather.7
  460.9 75.9 reduce-scatter.2
  539.6 46.9 reduce-scatter.4
